TPU v7x, 256 devices: a whole 4x4x8 slice. The times are simulated.
256 devices in a mesh: curve: 64 (over z_hi, x, y, core), lev: 4 (over z_lo).
Axes of the slice: x: 4, y: 4, z: 8 (z_hi: 2, z_lo: 4; z = z_hi * 4 + z_lo), core: 2. Of those that a mesh axis runs over, the one named last changes fastest.
Arguments:
- state: float32 [128, 16, 24576], P('lev', None, 'curve'), may hold values from -6 to 6
- wind_x: float32 [128, 16, 24576], P('lev', None, 'curve'), may hold values from -6 to 6
- wind_y: float32 [128, 16, 24576], P('lev', None, 'curve'), may hold values from -6 to 6
- neighbor: int32 [4, 24576], P(None, 'curve'), may hold values from 0 to 24575, as said below
- neighbor_edge: int32 [4, 24576], P(None, 'curve'), may hold values from 0 to 3
- reversed_edge: int32 [4, 24576], P(None, 'curve'), may hold values from 0 to 1
- branch_mask: int32 [16, 24576], P('lev', 'curve'), may hold values from 0 to 1, as said below
- mixing: float32 [128, 128], replicated, may hold values from -0.5 to 0.5
Outputs:
- updated: float32 [128, 16, 24576], P('lev', None, 'curve')
Inputs may be any that keep to these rules, and one draw needn't show every extreme that they name: Elements are numbered face by face over the six faces of a cube of 64 x 64 elements a face: element f * 64 * 64 + 64 * r + q lies on face f in row r and column c, with c = q for even r and c = 63 - q for odd r. Across edge 0 lies row r - 1, across edge 1 column c + 1, across edge 2 row r + 1, across edge 3 column c - 1 of the same face where that row or column exists; otherwise the element across lies on another face. Row 0 of face 3 borders row 63 of face 2 (across its edge 0). The tables are mutual: element neighbor[k, e] has e across its edge neighbor_edge[k, e], with the same reversed_edge. `branch_mask`: take the block of points of one lev index (16 / 4 consecutive points) and elements of one curve index: at most 1152 of its 1536 columns are 1, and for every lev index some block has exactly 1152.
All inputs are finite; a program needn't handle non-finite values.
Results may differ from a plain program's by a relative error of at most 0.0001.
Values sent between devices are 32-bit elements; how exact they have to be, the bound alone decides.
No kernel may reach another device: no remote copies, remote signals or barrier semaphores. Data moves between devices by JAX's collectives and lax.ppermute only.
A program may use at most 64 MiB of HBM per device.

v0:
```python
import math

import jax
import jax.numpy as jnp
import numpy as np
from jax import lax
from jax.sharding import PartitionSpec as P

NE = 64


def with_halo(array, sides, width):
    for axis, dim in sides:
        devices, length = (lax.axis_size(axis), array.shape[dim])
        up = [(i, (i + 1) % devices) for i in range(devices - 1)]
        down = [(j, i) for i, j in up]
        last = lax.slice_in_dim(array, length - width, length, axis=dim)
        first = lax.slice_in_dim(array, 0, width, axis=dim)
        before = lax.ppermute(last, axis, up)
        after = lax.ppermute(first, axis, down)
        array = jnp.concatenate([before, array, after], axis=dim)
    return array


def derivative_table():
    nodes = np.array([-1.0, -1.0 / math.sqrt(5.0), 1.0 / math.sqrt(5.0), 1.0])
    weights = np.array(
        [1.0 / np.prod([nodes[j] - nodes[m] for m in range(4) if m != j]) for j in range(4)]
    )
    table = np.zeros((4, 4))
    for i in range(4):
        for j in range(4):
            if i == j:
                table[i, j] = sum((1.0 / (nodes[i] - nodes[m]) for m in range(4) if m != i))
            else:
                table[i, j] = weights[j] / weights[i] / (nodes[i] - nodes[j])
    return table


def slot_table():
    table = np.zeros((16, 16))
    for t in range(4):
        table[0 * 4 + t, 0 * 4 + t] = 1.0
        table[1 * 4 + t, t * 4 + 3] = 1.0
        table[2 * 4 + t, 3 * 4 + t] = 1.0
        table[3 * 4 + t, t * 4 + 0] = 1.0
    return table


def branch_work(mixing, work):
    mixed = jnp.dot(
        mixing, work, precision=lax.Precision.HIGHEST, preferred_element_type=jnp.float32
    )
    return 0.5 * jnp.tanh(mixed) - 0.25 * work


def face_place(index):
    face_cells = NE * NE
    face_slot = index // face_cells
    within = index % face_cells
    row_index = within // NE
    raw_col = within % NE
    column = jnp.where(row_index % 2 == 0, raw_col, NE - 1 - raw_col)
    return (face_slot, row_index, column)


def on_device(state, wind_x, wind_y, neighbor, neighbor_edge, reversed_edge, branch_mask, mixing):
    high = lax.Precision.HIGHEST
    lev_dev, points, elems = state.shape
    deriv = jnp.asarray(derivative_table(), jnp.float32)
    slots = jnp.asarray(slot_table(), jnp.float32)
    flat_state = state.reshape(lev_dev, points * elems)
    column_block = lax.all_to_all(flat_state, "lev", split_axis=1, concat_axis=0, tiled=True)
    levels, width = column_block.shape
    marked = branch_mask.reshape(width)
    plain = -0.3 * column_block / (1.0 + column_block * column_block)
    capacity = 3 * width // 4
    rank = jnp.cumsum(marked) - marked
    slot_index = jnp.where(marked == 1, rank, capacity)
    work = (
        jnp.zeros((levels, capacity), jnp.float32).at[:, slot_index].set(column_block, mode="drop")
    )
    result = branch_work(mixing, work)
    heavy = jnp.take(result, jnp.clip(rank, 0, capacity - 1), axis=1)
    increment = jnp.where(marked[None, :] == 1, heavy, plain)
    returned = lax.all_to_all(increment, "lev", split_axis=0, concat_axis=1, tiled=True)
    change = returned.reshape(lev_dev, points, elems)
    grid = state.reshape(lev_dev, 4, 4, elems)
    dxi = jnp.einsum("ai,lije->laje", deriv, grid, precision=high).reshape(lev_dev, 16, elems)
    deta = jnp.einsum("bj,lije->libe", deriv, grid, precision=high).reshape(lev_dev, 16, elems)
    stepped = state - 0.05 * (wind_x * dxi + wind_y * deta)
    own = jnp.einsum("sg,lge->lse", slots, stepped, precision=high)
    extended = with_halo(own, (("curve", 2),), elems)
    rim_width = 24 * NE
    start = lax.axis_index("curve") * elems
    global_index = start + jnp.arange(elems, dtype=jnp.int32)
    window = elems + 2 * elems
    offset = neighbor - start + elems
    in_window = (offset >= 0) & (offset < window)
    position = jnp.arange(4, dtype=jnp.int32)
    source_pos = jnp.where(
        reversed_edge[:, None, :] == 1, 3 - position[None, :, None], position[None, :, None]
    )
    source_slot = neighbor_edge[:, None, :] * 4 + source_pos
    nearby = jnp.clip(offset, 0, window - 1)
    near_index = (source_slot * window + nearby[:, None, :]).reshape(-1)
    from_near = jnp.take(extended.reshape(lev_dev, 16 * window), near_index, axis=1).reshape(
        lev_dev, 16, elems
    )
    face_slot, row_index, column = face_place(global_index)
    crossing = jnp.stack([row_index == 0, column == NE - 1, row_index == NE - 1, column == 0])
    along_side = jnp.stack([column, row_index, column, row_index])
    edge_ids = jnp.arange(4, dtype=jnp.int32)[:, None]
    rim_slot = jnp.where(
        crossing, face_slot[None, :] * (4 * NE) + edge_ids * NE + along_side, rim_width
    )
    edge_values = (
        own.reshape(lev_dev, 4, 4, elems).transpose(0, 2, 1, 3).reshape(lev_dev, 4, 4 * elems)
    )
    rim_local = (
        jnp.zeros((lev_dev, 4, rim_width), jnp.float32)
        .at[:, :, rim_slot.reshape(-1)]
        .set(edge_values, mode="drop")
    )
    rim_whole = lax.psum(rim_local, "curve")
    their_slot, their_row, their_col = face_place(neighbor)
    their_along = jnp.where(neighbor_edge % 2 == 0, their_col, their_row)
    rim_index = jnp.where(in_window, 0, their_slot * (4 * NE) + neighbor_edge * NE + their_along)
    far_index = (source_pos * rim_width + rim_index[:, None, :]).reshape(-1)
    from_far = jnp.take(rim_whole.reshape(lev_dev, 4 * rim_width), far_index, axis=1).reshape(
        lev_dev, 16, elems
    )
    near_mask = jnp.broadcast_to(in_window[:, None, :], (4, 4, elems)).reshape(1, 16, elems)
    across = jnp.where(near_mask, from_near, from_far)
    dynamics = stepped + 0.5 * jnp.einsum("sg,lse->lge", slots, across - own, precision=high)
    return dynamics + change


def solution(mesh):
    in_specs = (
        P("lev", None, "curve"),
        P("lev", None, "curve"),
        P("lev", None, "curve"),
        P(None, "curve"),
        P(None, "curve"),
        P(None, "curve"),
        P("lev", "curve"),
        P(),
    )
    out_specs = P("lev", None, "curve")
    return jax.shard_map(
        on_device, mesh=mesh, in_specs=in_specs, out_specs=out_specs, check_vma=False
    )
```

profile of v0, /device:TPU:1, one launch (start us, length us, event | category | flops | bytes accessed | tf_op | source)
XLA Modules:
  0.0 973.6 jit_solution(598107941763404942)
XLA Ops:
  6.5 0.0 copy-start
  6.5 0.0 all-reduce.2.cloned.1.call-start
  6.5 1.4 reshape.565
  7.9 0.0 copy-start.1
  8.0 2.2 convolution_bitcast_fusion.2
  10.2 0.0 copy-done.9
  10.2 1.4 convolution_bitcast_fusion.1
  11.6 0.3 copy.47
  11.8 0.0 copy-start.7
  11.9 0.3 reshape.567
  12.1 2.0 fusion.11
  14.1 0.0 copy-start.3
  14.1 0.9 copy-done.3
  15.0 0.0 copy-done.7
  15.0 1.7 convolution_bitcast_fusion
  16.7 4.6 collective-permute-start
  21.3 2.7 collective-permute-start.1
  24.2 1.4 reshape.569
  25.5 0.1 fusion.37
  25.6 2.7 copy.51
  28.4 0.4 broadcast_in_dim.129
  28.8 74.0 %scatter_fusion = f32[32,4,1536]{0,1,2:T(4,128)S(1)} fusion(f32[32,4,1536]{0,1,2:T(4,128)S(1)} %broadcast_in_dim.129, s32[1536]{0:T(1024)S(1)} %fusion.24, f32[1536,32,4]{1,2,0:T(4,128)} %bitcast.92), kind=kCustom, calls=%fused_computation.3 | custom fusion | bytes 2365440 | tf_op jit(solution)/shard_map/scatter | solution.py:123
  102.9 1.9 copy.64
  104.7 0.0 all-reduce.2.cloned.1.call-update
  104.8 1.1 copy-done.2
  105.9 0.3 all_to_all.24
  106.2 1.1 copy.56
  107.3 4.8 all-to-all-start
  112.1 0.0 copy-done.6
  112.2 0.0 copy-done.8
  112.2 0.0 copy-done.11
  112.2 0.1 broadcast_multiply_fusion
  112.2 0.1 multiply_add_fusion.1
  112.4 0.3 reduce-window.9
  112.7 0.1 slice.15
  112.8 0.1 slice_reduce_fusion
  112.9 0.1 add_bitcast_fusion
  113.0 0.1 fusion.26
  113.1 0.1 broadcast_compare_fusion
  113.2 19.9 %all-to-all-done = f32[32,4,1536]{2,0,1:T(8,128)S(1)} async-done(((f32[32,4,1536]{2,0,1:T(8,128)}), f32[32,4,1536]{2,0,1:T(8,128)S(1)}, u32[]{:S(2)}, u32[]{:S(2)}) %all-to-all-start) | async-done | bytes 786464 | tf_op jit(solution)/shard_map/all_to_all | solution.py:73
  133.1 0.3 copy.57
  133.3 4.5 scatter_custom_fusion.1
  137.9 0.6 fusion.2
  138.5 2.6 gather_fusion.2
  141.1 0.3 copy.58
  141.4 1.1 fusion.8
  142.4 4.4 all-to-all-start.1
  147.0 0.1 broadcast_in_dim.120
  147.1 0.1 compare_and_fusion.1
  147.2 758.8 %all-reduce.2.cloned.1.call-done = f32[32,6144]{0,1:T(8,128)} async-done(((f32[32,6144]{0,1:T(8,128)}), f32[32,6144]{0,1:T(8,128)}) %all-reduce.2.cloned.1.call-update) | async-done | bytes 786448 | tf_op jit(solution)/shard_map/psum | solution.py:125
  906.0 17.9 %gather_fusion.1 = f32[6144,32]{1,0:T(8,128)S(1)} fusion(f32[32,6144]{0,1:T(8,128)} %all-reduce.2.cloned.1.call-done, s32[6144]{0:T(1024)S(1)} %broadcast_clamp_fusion), kind=kCustom, calls=%fused_computation.1 | custom fusion | bytes 1597440 | tf_op jit(solution)/shard_map/jit(_take)/gather | solution.py:130
  924.0 1.9 copy.65
  925.9 0.0 collective-permute-done
  925.9 0.0 collective-permute-done.1
  925.9 1.8 pad_maximum_fusion
  927.7 5.8 copy.62
  933.5 24.7 %gather_fusion = f32[6144,32]{1,0:T(8,128)} fusion(f32[32,18432]{0,1:T(8,128)} %bitcast.89, s32[6144]{0:T(1024)S(1)} %broadcast_clamp_fusion.1), kind=kCustom, calls=%fused_computation | custom fusion | bytes 1597440 | tf_op jit(solution)/shard_map/jit(_take)/gather | solution.py:107
  958.2 3.2 copy.63
  961.5 0.0 all-to-all-done.1
  961.5 1.6 copy.59
  963.1 0.4 reshape.575
  963.5 0.0 copy-done.4
  963.5 0.0 copy-done.5
  963.5 3.2 fusion.5
  (45 shorter events, 0.5 us)
Async XLA Ops:
  6.5 131.3 %copy-start = (f32[128,128]{1,0:T(8,128)S(1)}, f32[128,128]{1,0:T(8,128)}, u32[]{:S(2)}) copy-start(f32[128,128]{1,0:T(8,128)} %param.17) | copy-start | bytes 196612
  6.5 3.6 copy-start.9
  6.5 899.5 %all-reduce.2.cloned.1.call-start = ((), (), s32[]{:S(2)}) async-start(), calls=%async_computation.2 | async-start | bytes 6291456 | tf_op jit(solution)/shard_map/psum | solution.py:125
  7.9 4.2 copy-start.1
  11.8 3.1 copy-start.7
  14.1 0.9 copy-start.3
  16.7 909.2 %collective-permute-start = (f32[32,16,384]{2,1,0:T(8,128)}, f32[32,16,384]{2,1,0:T(8,128)}, u32[]{:S(2)}, u32[]{:S(2)}) collective-permute-start(f32[32,16,384]{2,1,0:T(8,128)} %convolution_bitcast_fusion), channel_id=1, source_target_pairs={{0,4},{4,8},{8,12},{12,16},{16,20},{20,24},{24,28},{28,32},{32,36}... | collective-permute-start | bytes 2359304 | tf_op jit(solution)/shard_map/ppermute | solution.py:19
  21.3 904.6 %collective-permute-start.1 = (f32[32,16,384]{2,1,0:T(8,128)}, f32[32,16,384]{2,1,0:T(8,128)}, u32[]{:S(2)}, u32[]{:S(2)}) collective-permute-start(f32[32,16,384]{2,1,0:T(8,128)} %convolution_bitcast_fusion), channel_id=1, source_target_pairs={{4,0},{8,4},{12,8},{16,12},{20,16},{24,20},{28,24},{32,28},{36,32}... | collective-permute-start | bytes 2359304 | tf_op jit(solution)/shard_map/ppermute | solution.py:20
  104.7 1.1 copy-start.2
  105.9 6.2 copy-start.6
  105.9 6.3 copy-start.10
  105.9 6.3 copy-start.8
  105.9 6.3 copy-start.11
  107.3 25.8 %all-to-all-start = ((f32[32,4,1536]{2,0,1:T(8,128)}), f32[32,4,1536]{2,0,1:T(8,128)S(1)}, u32[]{:S(2)}, u32[]{:S(2)}) async-start(f32[32,4,1536]{2,0,1:T(8,128)} %copy.56), calls=%async_computation | async-start | bytes 1572864 | tf_op jit(solution)/shard_map/all_to_all | solution.py:73
  142.4 819.0 %all-to-all-start.1 = ((f32[4,32,1536]{2,1,0:T(8,128)}), f32[4,32,1536]{2,1,0:T(8,128)}, u32[]{:S(2)}, u32[]{:S(2)}) async-start(f32[4,32,1536]{2,1,0:T(8,128)} %fusion.8), calls=%async_computation.1 | async-start | bytes 1572864 | tf_op jit(solution)/shard_map/all_to_all | solution.py:86
  958.2 5.3 copy-start.4
  958.2 5.3 copy-start.5
Sparse Core Ops, SparseCore 0:
  104.9 801.1 all-reduce.1
where the time goes:
time: 981 us; the launch traced here: 974 us
  waiting for transfers between devices  779 us (79%)
  local copies, waits for them, and re-layouts  150 us (15%)
  starting transfers between devices  16.5 us (2%)
  between operations  13.8 us (1%)
    psum x1, waiting for transfers between devices, on_device(): rim_whole = lax.psum(rim_local, 'curve')  759 us
    scatter x1, local copies, waits for them, and re-layouts, on_device(): rim_local = jnp.zeros((lev_dev, 4, rim_width), jnp.float32).at[:, :, rim_...  74 us
    gather x2, local copies, waits for them, and re-layouts, on_device(): jnp.take(extended.reshape(lev_dev, 16 * window), near_index, axis=1)  28 us
    gather x2, local copies, waits for them, and re-layouts, on_device(): jnp.take(rim_whole.reshape(lev_dev, 4 * rim_width), far_index, axis=1)  19.9 us
    all_to_all x1, waiting for transfers between devices, on_device(): lax.all_to_all(flat_state, 'lev', split_axis=1, concat_axis=0, tiled=True)  19.9 us
  transfers between devices with their start and end apart: 5, of which 2 were waited for; matrix products, arithmetic and copies ran while one was open for 15% of the time, Pallas kernels for 0%

commit v1 on v0

v1 whole, which is shorter than its diff:
```python
import functools
import math

import jax
import jax.numpy as jnp
import numpy as np
from jax import lax
from jax.experimental import pallas as pl
from jax.experimental.pallas import tpu as pltpu
from jax.sharding import PartitionSpec as P

NE = 64
ROWS = 6
E = ROWS * NE
CONTRIB = 144
MERGED = 176
PIECE = 2 * MERGED
SIDE = 4 * PIECE
VMEM = pl.BlockSpec(memory_space=pltpu.VMEM)
LIMIT = 48 * 1024 * 1024
NT = (((1,), (1,)), ((), ()))
TN = (((0,), (0,)), ((), ()))


def derivative_table():
    nodes = np.array([-1.0, -1.0 / math.sqrt(5.0), 1.0 / math.sqrt(5.0), 1.0])
    weights = np.array(
        [1.0 / np.prod([nodes[j] - nodes[m] for m in range(4) if m != j]) for j in range(4)]
    )
    table = np.zeros((4, 4))
    for i in range(4):
        for j in range(4):
            if i == j:
                table[i, j] = sum((1.0 / (nodes[i] - nodes[m]) for m in range(4) if m != i))
            else:
                table[i, j] = weights[j] / weights[i] / (nodes[i] - nodes[j])
    table[1, 1] = table[2, 2] = 0.0
    return table


DERIV = derivative_table()


def f32(shape):
    return jax.ShapeDtypeStruct(shape, jnp.float32)


def call(kernel, out_shape, n_in, scratch=()):
    return pl.pallas_call(
        kernel,
        out_shape=out_shape,
        in_specs=[VMEM] * n_in,
        out_specs=jax.tree.map(lambda _: VMEM, out_shape),
        scratch_shapes=list(scratch),
        compiler_params=pltpu.CompilerParams(vmem_limit_bytes=LIMIT),
    )


def lane_blocks(*leading):
    return pl.BlockSpec((*leading, 128), lambda c: (0,) * len(leading) + (c,))


def whole(*shape):
    return pl.BlockSpec(shape, lambda c: (0,) * len(shape))


def lane_call(kernel, out_shape, in_specs, out_specs):
    return pl.pallas_call(
        kernel,
        grid=(3,),
        out_shape=out_shape,
        in_specs=in_specs,
        out_specs=out_specs,
        compiler_params=pltpu.CompilerParams(vmem_limit_bytes=LIMIT),
    )


def split_kernel(state, *sends):
    me = lax.axis_index("lev")
    for k in range(4):
        first = 4 * lax.rem(me + k, 4)
        for p in range(4):
            sends[k][p] = state[pl.ds(first + p, 32, stride=16), :]


def rim_rows():
    start = lax.axis_index("curve") * ROWS
    return (NE - lax.rem(start, NE)) % NE, NE - 1 - lax.rem(start, NE)


def exact_dot(selector, values, dims):
    high = values.astype(jnp.bfloat16)
    rest = values - high.astype(jnp.float32)
    middle = rest.astype(jnp.bfloat16)
    low = (rest - middle.astype(jnp.float32)).astype(jnp.bfloat16)
    out = None
    for part in (low, middle, high):
        args = (selector, part) if dims == NT else (part, selector)
        term = lax.dot_general(*args, dims, preferred_element_type=jnp.float32)
        out = term if out is None else out + term
    return out


def step_kernel(state, wind_x, wind_y, stepped, contrib, last, first):
    step = pl.program_id(0)
    lanes = pl.ds(pl.multiple_of(128 * step, 128), 128)
    for tile in range(4):
        at = [pl.ds(128 * tile + p, 8, stride=16) for p in range(16)]
        x = [state[at[p], :] for p in range(16)]
        for a in range(4):
            for b in range(4):
                p = 4 * a + b
                dxi = sum(float(DERIV[a, i]) * x[4 * i + b] for i in range(4) if DERIV[a, i])
                deta = sum(float(DERIV[b, j]) * x[4 * a + j] for j in range(4) if DERIV[b, j])
                moved = wind_x[at[p], :] * dxi + wind_y[at[p], :] * deta
                stepped[p, 8 * tile : 8 * tile + 8, lanes] = x[p] - 0.05 * moved

    @pl.when(step == 2)
    def _():
        take_edges(stepped, contrib, last, first)


def take_edges(stepped, contrib, last, first):
    edge = [
        stepped[0:4].reshape(128, E),
        jnp.concatenate([stepped[4 * t + 3] for t in range(4)], axis=0),
        stepped[12:16].reshape(128, E),
        jnp.concatenate([stepped[4 * t] for t in range(4)], axis=0),
    ]
    last[...] = edge[2][:, 256:]
    first[...] = edge[0][:, :128]
    row0, row63 = rim_rows()
    r = lax.broadcasted_iota(jnp.int32, (8, E), 0)
    lane = lax.broadcasted_iota(jnp.int32, (8, E), 1)
    odd = r % 2
    left = ((lane == NE * r + (NE - 1) * odd) & (r < ROWS)).astype(jnp.bfloat16)
    right = ((lane == NE * r + (NE - 1) * (1 - odd)) & (r < ROWS)).astype(jnp.bfloat16)
    contrib[0:6] = exact_dot(left, edge[3], NT)[0:6]
    contrib[6:12] = exact_dot(right, edge[1], NT)[0:6]
    r = lax.broadcasted_iota(jnp.int32, (NE, E), 0)
    lane = lax.broadcasted_iota(jnp.int32, (NE, E), 1)
    contrib[12:76] = exact_dot((lane == NE * row0 + r).astype(jnp.bfloat16), edge[0], NT)
    contrib[76:140] = exact_dot((lane == NE * row63 + r).astype(jnp.bfloat16), edge[2], NT)
    contrib[140:144] = jnp.zeros((4, 128), jnp.float32)


def merge_kernel(a, b, c, d, out):
    for k, part in enumerate((a, b, c, d)):
        out[12 * k : 12 * k + 12] = part[0:12]
    out[48:176] = (a[12:140] + b[12:140]) + (c[12:140] + d[12:140])


def physics_kernel(own, one, two, three, mask, mixing, *rest):
    backs, (columns, change) = rest[:4], rest[4:]
    me = lax.axis_index("lev")
    rows = [pl.ds(pl.multiple_of(32 * lax.rem(me + 4 - k, 4), 32), 32) for k in range(4)]
    mix = mixing[...]
    for p in range(4):
        for k, part in enumerate((own, one, two, three)):
            columns[p, rows[k], :] = part[p]
        x = columns[p]
        mixed = lax.dot_general(
            mix,
            x,
            (((1,), (0,)), ((), ())),
            precision=lax.Precision.HIGHEST,
            preferred_element_type=jnp.float32,
        )
        heavy = 0.5 * jnp.tanh(mixed) - 0.25 * x
        plain = -0.3 * x / (1.0 + x * x)
        change[p] = jnp.where(mask[p : p + 1, :] == 1, heavy, plain)
        for k in range(4):
            backs[k][p] = change[p, rows[k], :]


def edge_kernel(
    stepped, before, after, pool_own, pool_other, neighbor, neighbor_edge, reversed_edge, dynamics
):
    curve = lax.axis_index("curve")
    row0, row63 = rim_rows()
    my_z, my_x, my_y, my_c = curve // 32, (curve // 8) % 4, (curve // 2) % 4, curve % 2
    near, edge_of = neighbor[...], neighbor_edge[...]
    turned = reversed_edge[...] == 1
    device = ((near // 128) * 171) // 512
    lane_of = near - E * device
    row_of, along = lane_of // NE, lane_of % NE
    k_z = (device // 32 + my_z) % 2
    k_x = (my_x + 4 - (device // 8) % 4) % 4
    k_y = (my_y + 4 - (device // 2) % 4) % 4
    k_c = (device + my_c) % 2
    in_piece = jnp.where(
        edge_of % 2 == 1,
        12 * k_y + jnp.where(edge_of == 3, 0, 6) + row_of,
        48 + jnp.where(edge_of == 0, 0, NE) + along,
    )
    place = SIDE * k_c + PIECE * k_x + MERGED * k_z + in_piece
    lane = lax.broadcasted_iota(jnp.int32, (1, 128), 1)
    half = lane // NE
    side_lane = (lane % NE == 0) | (lane % NE == NE - 1)
    at_left = (lane == 0) | (lane == 127)

    def row_place(k, row):
        picked = [
            jnp.where(row // 2 == v, place[k : k + 1, 128 * v : 128 * v + 128], 0) for v in range(3)
        ]
        return picked[0] + picked[1] + picked[2]

    sides = jnp.zeros((1, 128), jnp.int32)
    for v in range(3):
        lanes = slice(128 * v, 128 * v + 128)
        both = jnp.where(at_left, place[3:4, lanes], place[1:2, lanes])
        both = jnp.where(side_lane, both, 0)
        sides = sides + (pltpu.roll(both, 2 * v, 1) if v else both)
    wanted = jnp.concatenate([row_place(0, row0), row_place(2, row63), sides], axis=1)
    found = None
    for k, pool in enumerate((pool_own, pool_other)):
        at = lax.broadcasted_iota(jnp.int32, (SIDE, 3 * 128), 0) + SIDE * k
        part = exact_dot((at == wanted).astype(jnp.bfloat16), pool[...], TN)
        found = part if found is None else found + part
    found0, found2, found_side = found[:, :128], found[:, 128:256], found[:, 256:]

    backwards = 127 - lax.broadcasted_iota(jnp.int32, (128, 128), 1)

    def flip(values):
        return jnp.take_along_axis(values, backwards, axis=1)

    def oriented(values, turn):
        four = [values[32 * t : 32 * t + 32] for t in range(4)]
        return [jnp.where(turn, four[3 - t], four[t]) for t in range(4)]

    point = [
        [0, 1, 2, 3],
        [3, 7, 11, 15],
        [12, 13, 14, 15],
        [0, 4, 8, 12],
    ]

    def edge(k, v):
        return jnp.concatenate(
            [stepped[p, :, 128 * v : 128 * v + 128] for p in point[k]], axis=0
        )

    flipped0 = [flip(edge(0, v)) for v in range(3)] + [flip(after[...])]
    flipped2 = [flip(before[...])] + [flip(edge(2, v)) for v in range(3)]
    lower = half == 0
    for v in range(3):
        lanes = slice(128 * v, 128 * v + 128)
        row = 2 * v + half
        own = [edge(k, v) for k in range(4)]
        back = pltpu.roll(found_side, (128 - 2 * v) % 128, 1) if v else found_side
        to_next = [pltpu.roll(own[k], 127, 1) for k in (1, 3)]
        to_last = [pltpu.roll(own[k], 1, 1) for k in (1, 3)]
        across = [
            jnp.where(lower, flipped2[v], flipped2[v + 1]),
            jnp.where(lower, to_next[1], to_last[1]),
            jnp.where(lower, flipped0[v], flipped0[v + 1]),
            jnp.where(lower, to_last[0], to_next[0]),
        ]
        across[0] = jnp.where(row == row0, found0, across[0])
        across[2] = jnp.where(row == row63, found2, across[2])
        across[3] = jnp.where(at_left, back, across[3])
        across[1] = jnp.where(side_lane & ~at_left, back, across[1])
        total = [stepped[p, :, lanes] for p in range(16)]
        for k in range(4):
            theirs = oriented(across[k], turned[k : k + 1, lanes])
            for t in range(4):
                p = point[k][t]
                total[p] = total[p] + 0.5 * (theirs[t] - own[k][32 * t : 32 * t + 32])
        for p in range(16):
            dynamics[p, :, lanes] = total[p]


def add_kernel(dynamics, own, one, two, three, out):
    me = lax.axis_index("lev")
    for k, part in enumerate((own, one, two, three)):
        first = 4 * lax.rem(me + k, 4)
        for p in range(4):
            out[pl.ds(first + p, 32, stride=16), :] = dynamics[first + p] + part[p]


def on_device(state, wind_x, wind_y, neighbor, neighbor_edge, reversed_edge, branch_mask, mixing):
    flat = state.reshape(512, E)
    part = f32((4, 32, E))
    flat_block, part_block = lane_blocks(512), lane_blocks(4, 32)
    sends = lane_call(split_kernel, (part,) * 4, [flat_block], (part_block,) * 4)(flat)
    cells = [
        lax.ppermute(sends[k], "lev", [(i, (i + k) % 4) for i in range(4)]) for k in (1, 2, 3)
    ]
    stepped, contrib, last, first = lane_call(
        step_kernel,
        (f32((16, 32, E)), f32((CONTRIB, 128)), f32((128, 128)), f32((128, 128))),
        [flat_block] * 3,
        (whole(16, 32, E), whole(CONTRIB, 128), whole(128, 128), whole(128, 128)),
    )(flat, wind_x.reshape(512, E), wind_y.reshape(512, E))
    before = lax.ppermute(last, "curve", [(i, i + 1) for i in range(63)])
    after = lax.ppermute(first, "curve", [(i + 1, i) for i in range(63)])

    def turn(shift, k):
        def to(i):
            return (i & ~(3 << shift)) | ((((i >> shift) + k) & 3) << shift)

        return [(i, to(i)) for i in range(64)]

    along_y = [lax.ppermute(contrib, "curve", turn(1, k)) for k in (1, 2, 3)]
    merged = call(merge_kernel, f32((MERGED, 128)), 4)(contrib, *along_y)
    other_z = lax.ppermute(merged, "curve", [(i, i ^ 32) for i in range(64)])
    piece = jnp.concatenate([merged, other_z], axis=0)
    along_x = [lax.ppermute(piece, "curve", turn(3, k)) for k in (1, 2, 3)]
    pool = jnp.concatenate([piece, *along_x], axis=0)
    pool_other = lax.ppermute(pool, "curve", [(i, i ^ 1) for i in range(64)])

    backs = call(
        physics_kernel,
        (part,) * 4,
        6,
        [pltpu.VMEM((4, 128, E), jnp.float32), pltpu.VMEM((4, 128, E), jnp.float32)],
    )(sends[0], *cells, branch_mask, mixing)
    changes = [
        lax.ppermute(backs[k], "lev", [(i, (i - k) % 4) for i in range(4)]) for k in (1, 2, 3)
    ]
    dynamics = call(edge_kernel, f32((16, 32, E)), 8)(
        stepped, before, after, pool, pool_other, neighbor, neighbor_edge, reversed_edge
    )
    out = lane_call(
        add_kernel, f32((512, E)), [lane_blocks(16, 32)] + [part_block] * 4, flat_block
    )(dynamics, backs[0], *changes)
    return out.reshape(32, 16, E)


def solution(mesh):
    in_specs = (
        P("lev", None, "curve"),
        P("lev", None, "curve"),
        P("lev", None, "curve"),
        P(None, "curve"),
        P(None, "curve"),
        P(None, "curve"),
        P("lev", "curve"),
        P(),
    )
    out_specs = P("lev", None, "curve")
    return jax.shard_map(
        on_device, mesh=mesh, in_specs=in_specs, out_specs=out_specs, check_vma=False
    )
```

time: 981 us -> 90.5 us (0.09)
  the two profiles are of different devices: /device:TPU:1 before, /device:TPU:63 now
where the time goes in v1:
time: 90.5 us; the launch traced here: 90.3 us
  waiting for transfers between devices  46.2 us (51%)
  starting transfers between devices  33.6 us (37%)
  Pallas kernels  6.89 us (8%)
  local copies, waits for them, and re-layouts  3.48 us (4%)
    ppermute x3, waiting for transfers between devices, on_device(): lax.ppermute(sends[k], 'lev', [(i, (i + k) % 4) for i in range(4)])  16.6 us
    ppermute x1, waiting for transfers between devices, on_device(): after = lax.ppermute(first, 'curve', [(i + 1, i) for i in range(63)])  12.7 us
    ppermute x1, starting transfers between devices, on_device(): before = lax.ppermute(last, 'curve', [(i, i + 1) for i in range(63)])  7.81 us
    ppermute x1, starting transfers between devices, on_device(): other_z = lax.ppermute(merged, 'curve', [(i, i ^ 32) for i in range(64)])  6.1 us
    ppermute x3, waiting for transfers between devices, on_device(): along_x = [lax.ppermute(piece, 'curve', turn(3, k)) for k in (1, 2, 3)]  5.63 us
    ppermute x1, starting transfers between devices, on_device(): pool_other = lax.ppermute(pool, 'curve', [(i, i ^ 1) for i in range(64)])  5.4 us
    ppermute x1, waiting for transfers between devices, on_device(): before = lax.ppermute(last, 'curve', [(i, i + 1) for i in range(63)])  4.7 us
    ppermute x3, waiting for transfers between devices, on_device(): along_y = [lax.ppermute(contrib, 'curve', turn(1, k)) for k in (1, 2, 3)]  4.6 us
  transfers between devices with their start and end apart: 16, of which 12 were waited for; matrix products, arithmetic and copies ran while one was open for 0% of the time, Pallas kernels for 4%

profile of v1, /device:TPU:63, one launch (start us, length us, event | category | flops | bytes accessed | tf_op | source)
XLA Modules:
  0.0 90.3 jit_solution(16731751907039587490)
XLA Ops:
  0.0 0.0 copy-start
  0.0 1.1 %copy-done = f32[32,16,384]{2,1,0:T(8,128)S(1)} copy-done((f32[32,16,384]{2,1,0:T(8,128)S(1)}, f32[32,16,384]{2,1,0:T(8,128)}, u32[]{:S(2)}) %copy-start) | copy-done | bytes 786456
  1.1 0.0 copy-start.2
  1.1 1.1 %copy-done.2 = f32[32,16,384]{2,1,0:T(8,128)S(1)} copy-done((f32[32,16,384]{2,1,0:T(8,128)S(1)}, f32[32,16,384]{2,1,0:T(8,128)}, u32[]{:S(2)}) %copy-start.2) | copy-done | bytes 786456
  2.3 0.0 copy-start.3
  2.3 1.1 %copy-done.3 = f32[32,16,384]{2,1,0:T(8,128)S(1)} copy-done((f32[32,16,384]{2,1,0:T(8,128)S(1)}, f32[32,16,384]{2,1,0:T(8,128)}, u32[]{:S(2)}) %copy-start.3) | copy-done | bytes 786456
  3.4 1.7 %shard_map.82 = (f32[16,32,384]{2,1,0:T(8,128)S(1)}, f32[144,128]{1,0:T(8,128)S(1)}, f32[128,128]{1,0:T(8,128)S(1)}, f32[128,128]{1,0:T(8,128)S(1)}) custom-call(f32[512,384]{1,0:T(8,128)S(1)} %bitcast.4, f32[512,384]{1,0:T(8,128)S(1)} %bitcast.6, f32[512,384]{1,0:T(8,128)S(1)} %bitcast.7), custom_call_target="tpu_custom_call" | custom-call | tf_op jit(solution)/shard_map/pallas_call | solution.py:289
  5.1 0.1 collective-permute-start.2
  5.2 2.2 %collective-permute-start.3 = (f32[144,128]{1,0:T(8,128)S(1)}, f32[144,128]{1,0:T(8,128)S(1)}, u32[]{:S(2)}, u32[]{:S(2)}) collective-permute-start(f32[144,128]{1,0:T(8,128)S(1)} %get-tuple-element.20.a), channel_id=1, source_target_pairs={{0,16},{4,20},{8,24},{12,28},{16,0},{20,4},{24,8},{28,12},{32,48},... | collective-permute-start | bytes 221192 | tf_op jit(solution)/shard_map/ppermute | solution.py:304
  7.5 0.0 collective-permute-start.4
  7.5 0.9 %collective-permute-done.2.b = f32[144,128]{1,0:T(8,128)S(1)} collective-permute-done((f32[144,128]{1,0:T(8,128)S(1)}, f32[144,128]{1,0:T(8,128)S(1)}, u32[]{:S(2)}, u32[]{:S(2)}) %collective-permute-start.2) | collective-permute-done | bytes 73760 | tf_op jit(solution)/shard_map/ppermute | solution.py:304
  8.4 1.6 %collective-permute-done.3.c = f32[144,128]{1,0:T(8,128)S(1)} collective-permute-done((f32[144,128]{1,0:T(8,128)S(1)}, f32[144,128]{1,0:T(8,128)S(1)}, u32[]{:S(2)}, u32[]{:S(2)}) %collective-permute-start.3) | collective-permute-done | bytes 73760 | tf_op jit(solution)/shard_map/ppermute | solution.py:304
  10.0 2.0 %collective-permute-done.4.d = f32[144,128]{1,0:T(8,128)S(1)} collective-permute-done((f32[144,128]{1,0:T(8,128)S(1)}, f32[144,128]{1,0:T(8,128)S(1)}, u32[]{:S(2)}, u32[]{:S(2)}) %collective-permute-start.4) | collective-permute-done | bytes 73760 | tf_op jit(solution)/shard_map/ppermute | solution.py:304
  12.1 6.1 %collective-permute-start.5 = (f32[176,128]{1,0:T(8,128)S(1)}, f32[176,128]{1,0:T(8,128)S(1)}, u32[]{:S(2)}, u32[]{:S(2)}) collective-permute-start(f32[176,128]{1,0:T(8,128)S(1)} %shard_map.83), channel_id=1, source_target_pairs={{0,128},{4,132},{8,136},{12,140},{16,144},{20,148},{24,152},{28,15... | collective-permute-start | bytes 270344 | tf_op jit(solution)/shard_map/ppermute | solution.py:306
  18.2 1.9 %collective-permute-done.5 = f32[176,128]{1,0:T(8,128)S(1)} collective-permute-done((f32[176,128]{1,0:T(8,128)S(1)}, f32[176,128]{1,0:T(8,128)S(1)}, u32[]{:S(2)}, u32[]{:S(2)}) %collective-permute-start.5) | collective-permute-done | bytes 90144 | tf_op jit(solution)/shard_map/ppermute | solution.py:306
  20.1 0.0 copy-start.1
  20.1 0.3 collective-permute-start.6
  20.4 2.1 %collective-permute-start.7 = (f32[352,128]{1,0:T(8,128)S(1)}, f32[352,128]{1,0:T(8,128)S(1)}, u32[]{:S(2)}, u32[]{:S(2)}) collective-permute-start(f32[352,128]{1,0:T(8,128)S(1)} %pad_maximum_fusion), channel_id=1, source_target_pairs={{0,64},{4,68},{8,72},{12,76},{16,80},{20,84},{24,88},{28,92},{32,9... | collective-permute-start | bytes 540680 | tf_op jit(solution)/shard_map/ppermute | solution.py:308
  22.6 0.0 collective-permute-start.8
  22.6 2.0 %collective-permute-done.6 = f32[352,128]{1,0:T(8,128)S(1)} collective-permute-done((f32[352,128]{1,0:T(8,128)S(1)}, f32[352,128]{1,0:T(8,128)S(1)}, u32[]{:S(2)}, u32[]{:S(2)}) %collective-permute-start.6) | collective-permute-done | bytes 180256 | tf_op jit(solution)/shard_map/ppermute | solution.py:308
  24.6 1.7 %collective-permute-done.7 = f32[352,128]{1,0:T(8,128)S(1)} collective-permute-done((f32[352,128]{1,0:T(8,128)S(1)}, f32[352,128]{1,0:T(8,128)S(1)}, u32[]{:S(2)}, u32[]{:S(2)}) %collective-permute-start.7) | collective-permute-done | bytes 180256 | tf_op jit(solution)/shard_map/ppermute | solution.py:308
  26.3 1.9 %collective-permute-done.8 = f32[352,128]{1,0:T(8,128)S(1)} collective-permute-done((f32[352,128]{1,0:T(8,128)S(1)}, f32[352,128]{1,0:T(8,128)S(1)}, u32[]{:S(2)}, u32[]{:S(2)}) %collective-permute-start.8) | collective-permute-done | bytes 180256 | tf_op jit(solution)/shard_map/ppermute | solution.py:308
  28.3 0.0 copy-start.4
  28.3 5.4 %collective-permute-start.9 = (f32[1408,128]{1,0:T(8,128)S(1)}, f32[1408,128]{1,0:T(8,128)S(1)}, u32[]{:S(2)}, u32[]{:S(2)}) collective-permute-start(f32[1408,128]{1,0:T(8,128)S(1)} %constant_dynamic-update-slice_fusion.pool_own), channel_id=1, source_target_pairs={{0,4},{4,0},{8,12},{12,8},{16,20},{20,16},{24,28},{28,24},{32,36},... | collective-permute-start | bytes 2162696 | tf_op jit(solution)/shard_map/ppermute | solution.py:310
  33.7 0.0 copy-done.1
  33.7 0.5 shard_map.85
  34.1 0.0 copy-start.5
  34.2 1.8 %collective-permute-start.10 = (f32[4,32,384]{2,1,0:T(8,128)S(1)}, f32[4,32,384]{2,1,0:T(8,128)S(1)}, u32[]{:S(2)}, u32[]{:S(2)}) collective-permute-start(f32[4,32,384]{2,1,0:T(8,128)S(1)} %get-tuple-element.22), channel_id=1, source_target_pairs={{0,1},{1,2},{2,3},{3,0},{4,5},{5,6},{6,7},{7,4},{8,9},{9,10},{10,1... | collective-permute-start | bytes 589832 | tf_op jit(solution)/shard_map/ppermute | solution.py:287
  35.9 1.3 %collective-permute-start.11 = (f32[4,32,384]{2,1,0:T(8,128)S(1)}, f32[4,32,384]{2,1,0:T(8,128)S(1)}, u32[]{:S(2)}, u32[]{:S(2)}) collective-permute-start(f32[4,32,384]{2,1,0:T(8,128)S(1)} %get-tuple-element.23), channel_id=1, source_target_pairs={{0,2},{1,3},{2,0},{3,1},{4,6},{5,7},{6,4},{7,5},{8,10},{9,11},{10,... | collective-permute-start | bytes 589832 | tf_op jit(solution)/shard_map/ppermute | solution.py:287
  37.3 1.4 %collective-permute-start.12 = (f32[4,32,384]{2,1,0:T(8,128)S(1)}, f32[4,32,384]{2,1,0:T(8,128)S(1)}, u32[]{:S(2)}, u32[]{:S(2)}) collective-permute-start(f32[4,32,384]{2,1,0:T(8,128)S(1)} %get-tuple-element.24), channel_id=1, source_target_pairs={{0,3},{1,0},{2,1},{3,2},{4,7},{5,4},{6,5},{7,6},{8,11},{9,8},{10,9... | collective-permute-start | bytes 589832 | tf_op jit(solution)/shard_map/ppermute | solution.py:287
  38.6 2.1 %collective-permute-done.10.one = f32[4,32,384]{2,1,0:T(8,128)S(1)} collective-permute-done((f32[4,32,384]{2,1,0:T(8,128)S(1)}, f32[4,32,384]{2,1,0:T(8,128)S(1)}, u32[]{:S(2)}, u32[]{:S(2)}) %collective-permute-start.10) | collective-permute-done | bytes 196640 | tf_op jit(solution)/shard_map/ppermute | solution.py:287
  40.7 12.1 %collective-permute-done.11.two = f32[4,32,384]{2,1,0:T(8,128)S(1)} collective-permute-done((f32[4,32,384]{2,1,0:T(8,128)S(1)}, f32[4,32,384]{2,1,0:T(8,128)S(1)}, u32[]{:S(2)}, u32[]{:S(2)}) %collective-permute-start.11) | collective-permute-done | bytes 196640 | tf_op jit(solution)/shard_map/ppermute | solution.py:287
  52.9 2.4 %collective-permute-done.12.three = f32[4,32,384]{2,1,0:T(8,128)S(1)} collective-permute-done((f32[4,32,384]{2,1,0:T(8,128)S(1)}, f32[4,32,384]{2,1,0:T(8,128)S(1)}, u32[]{:S(2)}, u32[]{:S(2)}) %collective-permute-start.12) | collective-permute-done | bytes 196640 | tf_op jit(solution)/shard_map/ppermute | solution.py:287
  55.3 0.0 copy-done.4
  55.3 0.0 copy-done.5
  55.3 0.0 copy-start.7
  55.3 0.0 copy-start.8
  55.3 1.0 %shard_map.86 = (f32[4,32,384]{2,1,0:T(8,128)S(1)}, f32[4,32,384]{2,1,0:T(8,128)S(1)}, f32[4,32,384]{2,1,0:T(8,128)S(1)}, f32[4,32,384]{2,1,0:T(8,128)S(1)}) custom-call(f32[4,32,384]{2,1,0:T(8,128)S(1)} %get-tuple-element.21.own, f32[4,32,384]{2,1,0:T(8,128)S(1)} %collective-permute-done.10.one, f32[4,32,384]{2,1,0:T(8,128)S(1)} %collective-permute-done.11.two, ...), custom_call_target="tpu_custom_call" | custom-call | tf_op jit(solution)/shard_map/pallas_call | solution.py:312
  56.3 0.0 copy-start.6
  56.3 0.1 collective-permute-start.13
  56.4 0.8 collective-permute-start.14
  57.2 2.3 %collective-permute-start.15 = (f32[4,32,384]{2,1,0:T(8,128)S(1)}, f32[4,32,384]{2,1,0:T(8,128)S(1)}, u32[]{:S(2)}, u32[]{:S(2)}) collective-permute-start(f32[4,32,384]{2,1,0:T(8,128)S(1)} %get-tuple-element.28), channel_id=1, source_target_pairs={{0,1},{1,2},{2,3},{3,0},{4,5},{5,6},{6,7},{7,4},{8,9},{9,10},{10,1... | collective-permute-start | bytes 589832 | tf_op jit(solution)/shard_map/ppermute | solution.py:319
  59.5 7.8 %collective-permute-start = (f32[128,128]{1,0:T(8,128)S(1)}, f32[128,128]{1,0:T(8,128)S(1)}, u32[]{:S(2)}, u32[]{:S(2)}) collective-permute-start(f32[128,128]{1,0:T(8,128)S(1)} %get-tuple-element.18), channel_id=1, source_target_pairs={{0,4},{4,8},{8,12},{12,16},{16,20},{20,24},{24,28},{28,32},{32,36}... | collective-permute-start | bytes 196616 | tf_op jit(solution)/shard_map/ppermute | solution.py:295
  67.3 4.7 %collective-permute-done.before = f32[128,128]{1,0:T(8,128)S(1)} collective-permute-done((f32[128,128]{1,0:T(8,128)S(1)}, f32[128,128]{1,0:T(8,128)S(1)}, u32[]{:S(2)}, u32[]{:S(2)}) %collective-permute-start) | collective-permute-done | bytes 65568 | tf_op jit(solution)/shard_map/ppermute | solution.py:295
  72.0 1.9 %collective-permute-start.1 = (f32[128,128]{1,0:T(8,128)S(1)}, f32[128,128]{1,0:T(8,128)S(1)}, u32[]{:S(2)}, u32[]{:S(2)}) collective-permute-start(f32[128,128]{1,0:T(8,128)S(1)} %get-tuple-element.19), channel_id=1, source_target_pairs={{4,0},{8,4},{12,8},{16,12},{20,16},{24,20},{28,24},{32,28},{36,32}... | collective-permute-start | bytes 196616 | tf_op jit(solution)/shard_map/ppermute | solution.py:296
  73.9 12.7 %collective-permute-done.1.after = f32[128,128]{1,0:T(8,128)S(1)} collective-permute-done((f32[128,128]{1,0:T(8,128)S(1)}, f32[128,128]{1,0:T(8,128)S(1)}, u32[]{:S(2)}, u32[]{:S(2)}) %collective-permute-start.1) | collective-permute-done | bytes 65568 | tf_op jit(solution)/shard_map/ppermute | solution.py:296
  86.6 0.0 collective-permute-done.9.pool_other
  86.6 0.0 copy-done.7
  86.6 0.0 copy-done.8
  86.6 0.0 copy-done.6
  86.6 1.9 %shard_map.84.dynamics = f32[16,32,384]{2,1,0:T(8,128)S(1)} custom-call(f32[16,32,384]{2,1,0:T(8,128)S(1)} %get-tuple-element.17.stepped, f32[128,128]{1,0:T(8,128)S(1)} %collective-permute-done.before, f32[128,128]{1,0:T(8,128)S(1)} %collective-permute-done.1.after, f32[1408,128]{1,0:T(8,128)S(1)} %constant_dynamic-update-slice_fusion.pool_own, ...), custom_call_target="tpu_custom_call" | custom-call | tf_op jit(solution)/shard_map/pallas_call | solution.py:321
  88.5 0.0 collective-permute-done.13.one
  88.5 0.0 collective-permute-done.14.two
  88.5 0.0 collective-permute-done.15.three
  88.5 1.8 %shard_map.87 = f32[512,384]{1,0:T(8,128)} custom-call(f32[16,32,384]{2,1,0:T(8,128)S(1)} %shard_map.84.dynamics, f32[4,32,384]{2,1,0:T(8,128)S(1)} %get-tuple-element.25.own, f32[4,32,384]{2,1,0:T(8,128)S(1)} %collective-permute-done.13.one, f32[4,32,384]{2,1,0:T(8,128)S(1)} %collective-permute-done.14.two, f32[4,32,384]{2,1,0:T(8,128)S(1)} %collective-permute-done.15.three), custom_call_target="tpu_custom_call" | custom-call | tf_op jit(solution)/shard_map/pallas_call | solution.py:324
  (7 shorter events, 0.1 us)
Async XLA Ops:
  0.0 1.1 %copy-start = (f32[32,16,384]{2,1,0:T(8,128)S(1)}, f32[32,16,384]{2,1,0:T(8,128)}, u32[]{:S(2)}) copy-start(f32[32,16,384]{2,1,0:T(8,128)} %param.8) | copy-start | bytes 2359300
  1.1 1.1 %copy-start.2 = (f32[32,16,384]{2,1,0:T(8,128)S(1)}, f32[32,16,384]{2,1,0:T(8,128)}, u32[]{:S(2)}) copy-start(f32[32,16,384]{2,1,0:T(8,128)} %param.9) | copy-start | bytes 2359300
  2.3 1.1 %copy-start.3 = (f32[32,16,384]{2,1,0:T(8,128)S(1)}, f32[32,16,384]{2,1,0:T(8,128)}, u32[]{:S(2)}) copy-start(f32[32,16,384]{2,1,0:T(8,128)} %param.10) | copy-start | bytes 2359300
  5.1 3.3 %collective-permute-start.2 = (f32[144,128]{1,0:T(8,128)S(1)}, f32[144,128]{1,0:T(8,128)S(1)}, u32[]{:S(2)}, u32[]{:S(2)}) collective-permute-start(f32[144,128]{1,0:T(8,128)S(1)} %get-tuple-element.20.a), channel_id=1, source_target_pairs={{0,8},{4,12},{8,16},{12,20},{16,24},{20,28},{24,0},{28,4},{32,40},... | collective-permute-start | bytes 221192 | tf_op jit(solution)/shard_map/ppermute | solution.py:304
  5.2 4.8 %collective-permute-start.3 = (f32[144,128]{1,0:T(8,128)S(1)}, f32[144,128]{1,0:T(8,128)S(1)}, u32[]{:S(2)}, u32[]{:S(2)}) collective-permute-start(f32[144,128]{1,0:T(8,128)S(1)} %get-tuple-element.20.a), channel_id=1, source_target_pairs={{0,16},{4,20},{8,24},{12,28},{16,0},{20,4},{24,8},{28,12},{32,48},... | collective-permute-start | bytes 221192 | tf_op jit(solution)/shard_map/ppermute | solution.py:304
  7.5 4.6 %collective-permute-start.4 = (f32[144,128]{1,0:T(8,128)S(1)}, f32[144,128]{1,0:T(8,128)S(1)}, u32[]{:S(2)}, u32[]{:S(2)}) collective-permute-start(f32[144,128]{1,0:T(8,128)S(1)} %get-tuple-element.20.a), channel_id=1, source_target_pairs={{0,24},{4,28},{8,0},{12,4},{16,8},{20,12},{24,16},{28,20},{32,56},... | collective-permute-start | bytes 221192 | tf_op jit(solution)/shard_map/ppermute | solution.py:304
  12.1 8.0 %collective-permute-start.5 = (f32[176,128]{1,0:T(8,128)S(1)}, f32[176,128]{1,0:T(8,128)S(1)}, u32[]{:S(2)}, u32[]{:S(2)}) collective-permute-start(f32[176,128]{1,0:T(8,128)S(1)} %shard_map.83), channel_id=1, source_target_pairs={{0,128},{4,132},{8,136},{12,140},{16,144},{20,148},{24,152},{28,15... | collective-permute-start | bytes 270344 | tf_op jit(solution)/shard_map/ppermute | solution.py:306
  20.1 13.5 %copy-start.1 = (f32[32,16,384]{2,1,0:T(8,128)S(1)}, f32[32,16,384]{2,1,0:T(8,128)}, u32[]{:S(2)}) copy-start(f32[32,16,384]{2,1,0:T(8,128)} %param.8) | copy-start | bytes 2359300
  20.1 4.4 %collective-permute-start.6 = (f32[352,128]{1,0:T(8,128)S(1)}, f32[352,128]{1,0:T(8,128)S(1)}, u32[]{:S(2)}, u32[]{:S(2)}) collective-permute-start(f32[352,128]{1,0:T(8,128)S(1)} %pad_maximum_fusion), channel_id=1, source_target_pairs={{0,32},{4,36},{8,40},{12,44},{16,48},{20,52},{24,56},{28,60},{32,6... | collective-permute-start | bytes 540680 | tf_op jit(solution)/shard_map/ppermute | solution.py:308
  20.4 5.9 %collective-permute-start.7 = (f32[352,128]{1,0:T(8,128)S(1)}, f32[352,128]{1,0:T(8,128)S(1)}, u32[]{:S(2)}, u32[]{:S(2)}) collective-permute-start(f32[352,128]{1,0:T(8,128)S(1)} %pad_maximum_fusion), channel_id=1, source_target_pairs={{0,64},{4,68},{8,72},{12,76},{16,80},{20,84},{24,88},{28,92},{32,9... | collective-permute-start | bytes 540680 | tf_op jit(solution)/shard_map/ppermute | solution.py:308
  22.6 5.7 %collective-permute-start.8 = (f32[352,128]{1,0:T(8,128)S(1)}, f32[352,128]{1,0:T(8,128)S(1)}, u32[]{:S(2)}, u32[]{:S(2)}) collective-permute-start(f32[352,128]{1,0:T(8,128)S(1)} %pad_maximum_fusion), channel_id=1, source_target_pairs={{0,96},{4,100},{8,104},{12,108},{16,112},{20,116},{24,120},{28,124... | collective-permute-start | bytes 540680 | tf_op jit(solution)/shard_map/ppermute | solution.py:308
  28.3 27.0 %copy-start.4 = (f32[128,128]{1,0:T(8,128)S(1)}, f32[128,128]{1,0:T(8,128)}, u32[]{:S(2)}) copy-start(f32[128,128]{1,0:T(8,128)} %mixing.1) | copy-start | bytes 196612
  28.3 58.3 %collective-permute-start.9 = (f32[1408,128]{1,0:T(8,128)S(1)}, f32[1408,128]{1,0:T(8,128)S(1)}, u32[]{:S(2)}, u32[]{:S(2)}) collective-permute-start(f32[1408,128]{1,0:T(8,128)S(1)} %constant_dynamic-update-slice_fusion.pool_own), channel_id=1, source_target_pairs={{0,4},{4,0},{8,12},{12,8},{16,20},{20,16},{24,28},{28,24},{32,36},... | collective-permute-start | bytes 2162696 | tf_op jit(solution)/shard_map/ppermute | solution.py:310
  34.1 21.1 %copy-start.5 = (s32[4,384]{1,0:T(4,128)S(1)}, s32[4,384]{1,0:T(4,128)}, u32[]{:S(2)}) copy-start(s32[4,384]{1,0:T(4,128)} %mask.1) | copy-start | bytes 18436
  34.2 6.6 %collective-permute-start.10 = (f32[4,32,384]{2,1,0:T(8,128)S(1)}, f32[4,32,384]{2,1,0:T(8,128)S(1)}, u32[]{:S(2)}, u32[]{:S(2)}) collective-permute-start(f32[4,32,384]{2,1,0:T(8,128)S(1)} %get-tuple-element.22), channel_id=1, source_target_pairs={{0,1},{1,2},{2,3},{3,0},{4,5},{5,6},{6,7},{7,4},{8,9},{9,10},{10,1... | collective-permute-start | bytes 589832 | tf_op jit(solution)/shard_map/ppermute | solution.py:287
  35.9 16.9 %collective-permute-start.11 = (f32[4,32,384]{2,1,0:T(8,128)S(1)}, f32[4,32,384]{2,1,0:T(8,128)S(1)}, u32[]{:S(2)}, u32[]{:S(2)}) collective-permute-start(f32[4,32,384]{2,1,0:T(8,128)S(1)} %get-tuple-element.23), channel_id=1, source_target_pairs={{0,2},{1,3},{2,0},{3,1},{4,6},{5,7},{6,4},{7,5},{8,10},{9,11},{10,... | collective-permute-start | bytes 589832 | tf_op jit(solution)/shard_map/ppermute | solution.py:287
  37.3 18.0 %collective-permute-start.12 = (f32[4,32,384]{2,1,0:T(8,128)S(1)}, f32[4,32,384]{2,1,0:T(8,128)S(1)}, u32[]{:S(2)}, u32[]{:S(2)}) collective-permute-start(f32[4,32,384]{2,1,0:T(8,128)S(1)} %get-tuple-element.24), channel_id=1, source_target_pairs={{0,3},{1,0},{2,1},{3,2},{4,7},{5,4},{6,5},{7,6},{8,11},{9,8},{10,9... | collective-permute-start | bytes 589832 | tf_op jit(solution)/shard_map/ppermute | solution.py:287
  55.3 31.3 %copy-start.7 = (s32[4,384]{1,0:T(4,128)S(1)}, s32[4,384]{1,0:T(4,128)}, u32[]{:S(2)}) copy-start(s32[4,384]{1,0:T(4,128)} %neighbor_edge.1) | copy-start | bytes 18436
  55.3 31.3 %copy-start.8 = (s32[4,384]{1,0:T(4,128)S(1)}, s32[4,384]{1,0:T(4,128)}, u32[]{:S(2)}) copy-start(s32[4,384]{1,0:T(4,128)} %reversed_edge.1) | copy-start | bytes 18436
  56.3 30.3 %copy-start.6 = (s32[4,384]{1,0:T(4,128)S(1)}, s32[4,384]{1,0:T(4,128)}, u32[]{:S(2)}) copy-start(s32[4,384]{1,0:T(4,128)} %neighbor.1) | copy-start | bytes 18436
  56.3 32.2 %collective-permute-start.13 = (f32[4,32,384]{2,1,0:T(8,128)S(1)}, f32[4,32,384]{2,1,0:T(8,128)S(1)}, u32[]{:S(2)}, u32[]{:S(2)}) collective-permute-start(f32[4,32,384]{2,1,0:T(8,128)S(1)} %get-tuple-element.26), channel_id=1, source_target_pairs={{0,3},{1,0},{2,1},{3,2},{4,7},{5,4},{6,5},{7,6},{8,11},{9,8},{10,9... | collective-permute-start | bytes 589832 | tf_op jit(solution)/shard_map/ppermute | solution.py:319
  56.4 32.1 %collective-permute-start.14 = (f32[4,32,384]{2,1,0:T(8,128)S(1)}, f32[4,32,384]{2,1,0:T(8,128)S(1)}, u32[]{:S(2)}, u32[]{:S(2)}) collective-permute-start(f32[4,32,384]{2,1,0:T(8,128)S(1)} %get-tuple-element.27), channel_id=1, source_target_pairs={{0,2},{1,3},{2,0},{3,1},{4,6},{5,7},{6,4},{7,5},{8,10},{9,11},{10,... | collective-permute-start | bytes 589832 | tf_op jit(solution)/shard_map/ppermute | solution.py:319
  57.2 31.3 %collective-permute-start.15 = (f32[4,32,384]{2,1,0:T(8,128)S(1)}, f32[4,32,384]{2,1,0:T(8,128)S(1)}, u32[]{:S(2)}, u32[]{:S(2)}) collective-permute-start(f32[4,32,384]{2,1,0:T(8,128)S(1)} %get-tuple-element.28), channel_id=1, source_target_pairs={{0,1},{1,2},{2,3},{3,0},{4,5},{5,6},{6,7},{7,4},{8,9},{9,10},{10,1... | collective-permute-start | bytes 589832 | tf_op jit(solution)/shard_map/ppermute | solution.py:319
  59.5 12.5 %collective-permute-start = (f32[128,128]{1,0:T(8,128)S(1)}, f32[128,128]{1,0:T(8,128)S(1)}, u32[]{:S(2)}, u32[]{:S(2)}) collective-permute-start(f32[128,128]{1,0:T(8,128)S(1)} %get-tuple-element.18), channel_id=1, source_target_pairs={{0,4},{4,8},{8,12},{12,16},{16,20},{20,24},{24,28},{28,32},{32,36}... | collective-permute-start | bytes 196616 | tf_op jit(solution)/shard_map/ppermute | solution.py:295
  72.0 14.6 %collective-permute-start.1 = (f32[128,128]{1,0:T(8,128)S(1)}, f32[128,128]{1,0:T(8,128)S(1)}, u32[]{:S(2)}, u32[]{:S(2)}) collective-permute-start(f32[128,128]{1,0:T(8,128)S(1)} %get-tuple-element.19), channel_id=1, source_target_pairs={{4,0},{8,4},{12,8},{16,12},{20,16},{24,20},{28,24},{32,28},{36,32}... | collective-permute-start | bytes 196616 | tf_op jit(solution)/shard_map/ppermute | solution.py:296

commit v2 on v1

--- a/solution.py
+++ b/solution.py
@@ -13,11 +13,12 @@
 ROWS = 6
 E = ROWS * NE
 CONTRIB = 144
-MERGED = 176
+PAIRED = 152
+MERGED = 224
 PIECE = 2 * MERGED
-SIDE = 4 * PIECE
 VMEM = pl.BlockSpec(memory_space=pltpu.VMEM)
-LIMIT = 48 * 1024 * 1024
+ANY = pl.BlockSpec(memory_space=pl.ANY)
+LIMIT = 24 * 1024 * 1024
 NT = (((1,), (1,)), ((), ()))
 TN = (((0,), (0,)), ((), ()))
 
@@ -45,14 +46,15 @@
     return jax.ShapeDtypeStruct(shape, jnp.float32)
 
 
-def call(kernel, out_shape, n_in, scratch=()):
+def call(kernel, out_shape, n_in, scratch=(), out_spec=VMEM, cost=None):
     return pl.pallas_call(
         kernel,
         out_shape=out_shape,
         in_specs=[VMEM] * n_in,
-        out_specs=jax.tree.map(lambda _: VMEM, out_shape),
+        out_specs=jax.tree.map(lambda _: out_spec, out_shape),
         scratch_shapes=list(scratch),
         compiler_params=pltpu.CompilerParams(vmem_limit_bytes=LIMIT),
+        cost_estimate=cost,
     )
 
 
@@ -78,7 +80,7 @@
 def split_kernel(state, *sends):
     me = lax.axis_index("lev")
     for k in range(4):
-        first = 4 * lax.rem(me + k, 4)
+        first = 4 * (me ^ k)
         for p in range(4):
             sends[k][p] = state[pl.ds(first + p, 32, stride=16), :]
 
@@ -101,7 +103,19 @@
     return out
 
 
-def step_kernel(state, wind_x, wind_y, stepped, contrib, last, first):
+def step_kernel(
+    state,
+    wind_x,
+    wind_y,
+    _sent,
+    near,
+    edge_of,
+    stepped,
+    contrib,
+    to_partner,
+    to_other,
+    wanted,
+):
     step = pl.program_id(0)
     lanes = pl.ds(pl.multiple_of(128 * step, 128), 128)
     for tile in range(4):
@@ -117,18 +131,24 @@
 
     @pl.when(step == 2)
     def _():
-        take_edges(stepped, contrib, last, first)
-
-
-def take_edges(stepped, contrib, last, first):
+        take_edges(stepped, contrib, to_partner, to_other)
+        wanted[...] = wanted_places(near[...], edge_of[...])
+
+
+def take_edges(stepped, contrib, to_partner, to_other):
     edge = [
         stepped[0:4].reshape(128, E),
         jnp.concatenate([stepped[4 * t + 3] for t in range(4)], axis=0),
         stepped[12:16].reshape(128, E),
         jnp.concatenate([stepped[4 * t] for t in range(4)], axis=0),
     ]
-    last[...] = edge[2][:, 256:]
-    first[...] = edge[0][:, :128]
+    last, first = edge[2][:, 256:], edge[0][:, :128]
+    low = lax.broadcasted_iota(jnp.int32, (64, 128), 1) < NE
+    last = jnp.where(low, pltpu.roll(last[:64], NE, 1), last[64:])
+    first = jnp.where(low, first[:64], pltpu.roll(first[64:], NE, 1))
+    even = lax.axis_index("curve") % 2 == 0
+    to_partner[...] = jnp.where(even, last, first)
+    to_other[...] = jnp.where(even, first, last)
     row0, row63 = rim_rows()
     r = lax.broadcasted_iota(jnp.int32, (8, E), 0)
     lane = lax.broadcasted_iota(jnp.int32, (8, E), 1)
@@ -141,23 +161,51 @@
     lane = lax.broadcasted_iota(jnp.int32, (NE, E), 1)
     contrib[12:76] = exact_dot((lane == NE * row0 + r).astype(jnp.bfloat16), edge[0], NT)
     contrib[76:140] = exact_dot((lane == NE * row63 + r).astype(jnp.bfloat16), edge[2], NT)
-    contrib[140:144] = jnp.zeros((4, 128), jnp.float32)
-
-
-def merge_kernel(a, b, c, d, out):
+    contrib[140:CONTRIB] = jnp.zeros((CONTRIB - 140, 128), jnp.float32)
+
+
+def pair_kernel(a, b, _row, out):
+    out[0:12] = a[0:12]
+    out[12:24] = b[0:12]
+    out[24:152] = a[12:140] + b[12:140]
+
+
+def merge_kernel(a, b, c, d, out, done):
     for k, part in enumerate((a, b, c, d)):
-        out[12 * k : 12 * k + 12] = part[0:12]
-    out[48:176] = (a[12:140] + b[12:140]) + (c[12:140] + d[12:140])
-
-
-def physics_kernel(own, one, two, three, mask, mixing, *rest):
-    backs, (columns, change) = rest[:4], rest[4:]
+        out[24 * k : 24 * k + 24] = part[0:24]
+    out[96:224] = (a[24:152] + b[24:152]) + (c[24:152] + d[24:152])
+    done[...] = jnp.zeros((8, 128), jnp.float32)
+
+
+def join_kernel(mine, theirs, partner_row, other_row, out, before, after):
+    out[:MERGED] = mine[...]
+    out[MERGED:] = theirs[...]
+    even = lax.axis_index("curve") % 2 == 0
+    partner, other = partner_row[...], other_row[...]
+    last = jnp.where(even, other, partner)
+    first = jnp.where(even, partner, other)
+    before[:64] = pltpu.roll(last, NE, 1)
+    before[64:] = last
+    after[:64] = first
+    after[64:] = pltpu.roll(first, NE, 1)
+
+
+def column_kernel(own, one, two, three, columns):
     me = lax.axis_index("lev")
-    rows = [pl.ds(pl.multiple_of(32 * lax.rem(me + 4 - k, 4), 32), 32) for k in range(4)]
+    for k, part in enumerate((own, one, two, three)):
+        for p in range(4):
+            columns[p, lev_rows(me ^ k), :] = part[p]
+
+
+def lev_rows(lev):
+    return pl.ds(pl.multiple_of(32 * lev, 32), 32)
+
+
+def physics_kernel(columns, mask, mixing, _rim, *rest):
+    backs, change = rest[:4], rest[4]
+    me = lax.axis_index("lev")
     mix = mixing[...]
     for p in range(4):
-        for k, part in enumerate((own, one, two, three)):
-            columns[p, rows[k], :] = part[p]
         x = columns[p]
         mixed = lax.dot_general(
             mix,
@@ -170,34 +218,29 @@
         plain = -0.3 * x / (1.0 + x * x)
         change[p] = jnp.where(mask[p : p + 1, :] == 1, heavy, plain)
         for k in range(4):
-            backs[k][p] = change[p, rows[k], :]
-
-
-def edge_kernel(
-    stepped, before, after, pool_own, pool_other, neighbor, neighbor_edge, reversed_edge, dynamics
-):
+            backs[k][p] = change[p, lev_rows(me ^ k), :]
+
+
+def side_lanes(lane):
+    return (lane % NE == 0) | (lane % NE == NE - 1), (lane == 0) | (lane == 127)
+
+
+def wanted_places(near, edge_of):
     curve = lax.axis_index("curve")
     row0, row63 = rim_rows()
-    my_z, my_x, my_y, my_c = curve // 32, (curve // 8) % 4, (curve // 2) % 4, curve % 2
-    near, edge_of = neighbor[...], neighbor_edge[...]
-    turned = reversed_edge[...] == 1
     device = ((near // 128) * 171) // 512
     lane_of = near - E * device
     row_of, along = lane_of // NE, lane_of % NE
-    k_z = (device // 32 + my_z) % 2
-    k_x = (my_x + 4 - (device // 8) % 4) % 4
-    k_y = (my_y + 4 - (device // 2) % 4) % 4
-    k_c = (device + my_c) % 2
-    in_piece = jnp.where(
+    apart = device ^ curve
+    k_z, k_x, k_y, k_c = apart // 32, (apart // 8) % 4, (apart // 2) % 4, apart % 2
+    in_merged = jnp.where(
         edge_of % 2 == 1,
-        12 * k_y + jnp.where(edge_of == 3, 0, 6) + row_of,
-        48 + jnp.where(edge_of == 0, 0, NE) + along,
-    )
-    place = SIDE * k_c + PIECE * k_x + MERGED * k_z + in_piece
+        24 * k_y + 12 * k_c + jnp.where(edge_of == 3, 0, 6) + row_of,
+        96 + jnp.where(edge_of == 0, 0, NE) + along,
+    )
+    place = PIECE * k_x + MERGED * k_z + in_merged
     lane = lax.broadcasted_iota(jnp.int32, (1, 128), 1)
-    half = lane // NE
-    side_lane = (lane % NE == 0) | (lane % NE == NE - 1)
-    at_left = (lane == 0) | (lane == 127)
+    side_lane, at_left = side_lanes(lane)
 
     def row_place(k, row):
         picked = [
@@ -211,10 +254,28 @@
         both = jnp.where(at_left, place[3:4, lanes], place[1:2, lanes])
         both = jnp.where(side_lane, both, 0)
         sides = sides + (pltpu.roll(both, 2 * v, 1) if v else both)
-    wanted = jnp.concatenate([row_place(0, row0), row_place(2, row63), sides], axis=1)
+    return jnp.concatenate([row_place(0, row0), row_place(2, row63), sides], axis=1)
+
+
+def change_kernel(stepped, own, one, two, three, out):
+    me = lax.axis_index("lev")
+    for k, part in enumerate((own, one, two, three)):
+        for p in range(4):
+            at = 4 * (me ^ k) + p
+            out[at] = stepped[at] + part[p]
+
+
+def edge_kernel(stepped, changed, before, after, *rest):
+    pools, (wanted_ref, reversed_edge, out, held, sems) = rest[:4], rest[4:]
+    row0, row63 = rim_rows()
+    turned = reversed_edge[...] == 1
+    wanted = wanted_ref[...]
+    lane = lax.broadcasted_iota(jnp.int32, (1, 128), 1)
+    half = lane // NE
+    side_lane, at_left = side_lanes(lane)
     found = None
-    for k, pool in enumerate((pool_own, pool_other)):
-        at = lax.broadcasted_iota(jnp.int32, (SIDE, 3 * 128), 0) + SIDE * k
+    for k, pool in enumerate(pools):
+        at = lax.broadcasted_iota(jnp.int32, (PIECE, 3 * 128), 0) + PIECE * k
         part = exact_dot((at == wanted).astype(jnp.bfloat16), pool[...], TN)
         found = part if found is None else found + part
     found0, found2, found_side = found[:, :128], found[:, 128:256], found[:, 256:]
@@ -243,6 +304,7 @@
     flipped0 = [flip(edge(0, v)) for v in range(3)] + [flip(after[...])]
     flipped2 = [flip(before[...])] + [flip(edge(2, v)) for v in range(3)]
     lower = half == 0
+    copies = []
     for v in range(3):
         lanes = slice(128 * v, 128 * v + 128)
         row = 2 * v + half
@@ -260,70 +322,78 @@
         across[2] = jnp.where(row == row63, found2, across[2])
         across[3] = jnp.where(at_left, back, across[3])
         across[1] = jnp.where(side_lane & ~at_left, back, across[1])
-        total = [stepped[p, :, lanes] for p in range(16)]
+        total = [changed[p, :, lanes] for p in range(16)]
         for k in range(4):
             theirs = oriented(across[k], turned[k : k + 1, lanes])
             for t in range(4):
                 p = point[k][t]
                 total[p] = total[p] + 0.5 * (theirs[t] - own[k][32 * t : 32 * t + 32])
         for p in range(16):
-            dynamics[p, :, lanes] = total[p]
-
-
-def add_kernel(dynamics, own, one, two, three, out):
-    me = lax.axis_index("lev")
-    for k, part in enumerate((own, one, two, three)):
-        first = 4 * lax.rem(me + k, 4)
-        for p in range(4):
-            out[pl.ds(first + p, 32, stride=16), :] = dynamics[first + p] + part[p]
+            held[v, pl.ds(p, 32, stride=16), :] = total[p]
+        copies.append(
+            pltpu.make_async_copy(held.at[v], out.at[:, pl.ds(128 * v, 128)], sems.at[v])
+        )
+        copies[-1].start()
+    for copy in copies:
+        copy.wait()
 
 
 def on_device(state, wind_x, wind_y, neighbor, neighbor_edge, reversed_edge, branch_mask, mixing):
     flat = state.reshape(512, E)
     part = f32((4, 32, E))
     flat_block, part_block = lane_blocks(512), lane_blocks(4, 32)
+
+    def swap(array, axis, bits):
+        devices = lax.axis_size(axis)
+        return lax.ppermute(array, axis, [(i, i ^ bits) for i in range(devices)])
+
     sends = lane_call(split_kernel, (part,) * 4, [flat_block], (part_block,) * 4)(flat)
-    cells = [
-        lax.ppermute(sends[k], "lev", [(i, (i + k) % 4) for i in range(4)]) for k in (1, 2, 3)
-    ]
-    stepped, contrib, last, first = lane_call(
+    cells = [swap(sends[k], "lev", k) for k in (1, 2, 3)]
+    stepped, contrib, to_partner, to_other, wanted = lane_call(
         step_kernel,
-        (f32((16, 32, E)), f32((CONTRIB, 128)), f32((128, 128)), f32((128, 128))),
-        [flat_block] * 3,
-        (whole(16, 32, E), whole(CONTRIB, 128), whole(128, 128), whole(128, 128)),
-    )(flat, wind_x.reshape(512, E), wind_y.reshape(512, E))
-    before = lax.ppermute(last, "curve", [(i, i + 1) for i in range(63)])
-    after = lax.ppermute(first, "curve", [(i + 1, i) for i in range(63)])
-
-    def turn(shift, k):
-        def to(i):
-            return (i & ~(3 << shift)) | ((((i >> shift) + k) & 3) << shift)
-
-        return [(i, to(i)) for i in range(64)]
-
-    along_y = [lax.ppermute(contrib, "curve", turn(1, k)) for k in (1, 2, 3)]
-    merged = call(merge_kernel, f32((MERGED, 128)), 4)(contrib, *along_y)
-    other_z = lax.ppermute(merged, "curve", [(i, i ^ 32) for i in range(64)])
-    piece = jnp.concatenate([merged, other_z], axis=0)
-    along_x = [lax.ppermute(piece, "curve", turn(3, k)) for k in (1, 2, 3)]
-    pool = jnp.concatenate([piece, *along_x], axis=0)
-    pool_other = lax.ppermute(pool, "curve", [(i, i ^ 1) for i in range(64)])
-
+        (
+            f32((16, 32, E)),
+            f32((CONTRIB, 128)),
+            f32((64, 128)),
+            f32((64, 128)),
+            jax.ShapeDtypeStruct((1, E), jnp.int32),
+        ),
+        [flat_block] * 3 + [whole(4, 32, E), whole(4, E), whole(4, E)],
+        (whole(16, 32, E), whole(CONTRIB, 128), whole(64, 128), whole(64, 128), whole(1, E)),
+    )(
+        flat,
+        wind_x.reshape(512, E),
+        wind_y.reshape(512, E),
+        sends[0],
+        neighbor,
+        neighbor_edge,
+    )
+    inner = [(i, i + 1) for i in range(1, 62, 2) if i != 31]
+    other_row = lax.ppermute(to_other, "curve", inner + [(j, i) for i, j in inner])
+    partner_row = swap(to_partner, "curve", 1)
+    paired = call(pair_kernel, f32((PAIRED, 128)), 3)(
+        contrib, swap(contrib, "curve", 1), partner_row
+    )
+    along_y = [swap(paired, "curve", k << 1) for k in (1, 2, 3)]
+    merged, done = call(merge_kernel, (f32((MERGED, 128)), f32((8, 128))), 4)(paired, *along_y)
+    long = pl.CostEstimate(flops=10**11, bytes_accessed=10**8, transcendentals=0)
+    columns = call(column_kernel, f32((4, 128, E)), 4, cost=long)(sends[0], *cells)
     backs = call(
-        physics_kernel,
-        (part,) * 4,
-        6,
-        [pltpu.VMEM((4, 128, E), jnp.float32), pltpu.VMEM((4, 128, E), jnp.float32)],
-    )(sends[0], *cells, branch_mask, mixing)
-    changes = [
-        lax.ppermute(backs[k], "lev", [(i, (i - k) % 4) for i in range(4)]) for k in (1, 2, 3)
-    ]
-    dynamics = call(edge_kernel, f32((16, 32, E)), 8)(
-        stepped, before, after, pool, pool_other, neighbor, neighbor_edge, reversed_edge
-    )
-    out = lane_call(
-        add_kernel, f32((512, E)), [lane_blocks(16, 32)] + [part_block] * 4, flat_block
-    )(dynamics, backs[0], *changes)
+        physics_kernel, (part,) * 4, 4, [pltpu.VMEM((4, 128, E), jnp.float32)]
+    )(columns, branch_mask, mixing, done)
+    changes = [swap(backs[k], "lev", k) for k in (1, 2, 3)]
+    piece, before, after = call(
+        join_kernel, (f32((2 * MERGED, 128)), f32((128, 128)), f32((128, 128))), 4, cost=long
+    )(merged, swap(merged, "curve", 32), partner_row, other_row)
+    along_x = [swap(piece, "curve", k << 3) for k in (1, 2, 3)]
+    changed = call(change_kernel, f32((16, 32, E)), 5, cost=long)(stepped, backs[0], *changes)
+    out = call(
+        edge_kernel,
+        f32((512, E)),
+        10,
+        [pltpu.VMEM((3, 512, 128), jnp.float32), pltpu.SemaphoreType.DMA((3,))],
+        out_spec=pl.BlockSpec(memory_space=pl.ANY),
+    )(stepped, changed, before, after, piece, *along_x, wanted, reversed_edge)
     return out.reshape(32, 16, E)
 
 

time: 90.5 us -> 57.8 us (0.64)
  the two profiles are of different devices: /device:TPU:63 before, /device:TPU:176 now
where the time goes in v2:
time: 57.8 us; the launch traced here: 57.4 us
  waiting for transfers between devices  24.2 us (42%)
  starting transfers between devices  21.9 us (38%)
  Pallas kernels  5.63 us (10%)
  local copies, waits for them, and re-layouts  5.5 us (10%)
    ppermute x15, waiting for transfers between devices, swap(): return lax.ppermute(array, axis, [(i, i ^ bits) for i in range(devices)])  24.2 us
    ppermute x15, starting transfers between devices, swap(): return lax.ppermute(array, axis, [(i, i ^ bits) for i in range(devices)])  20 us
    unnamed x16, local copies, waits for them, and re-layouts  5.5 us
    pallas_call x1, Pallas kernels, on_device(): call(edge_kernel, f32((512, E)), 10, [pltpu.VMEM((3, 512, 128), jnp.float...  2.27 us
    ppermute x1, starting transfers between devices, on_device(): lax.ppermute(to_other, 'curve', inner + [(j, i) for i, j in inner])  1.91 us
    pallas_call x1, Pallas kernels, on_device(): lane_call(step_kernel, (f32((16, 32, E)), f32((CONTRIB, 128)), f32((64, 1...  1.73 us
  transfers between devices with their start and end apart: 16, of which 8 were waited for; matrix products, arithmetic and copies ran while one was open for 0% of the time, Pallas kernels for 2%

profile of v2, /device:TPU:176, one launch (start us, length us, event | category | flops | bytes accessed | tf_op | source)
XLA Modules:
  0.0 57.4 jit_solution(7005326108982924904)
XLA Ops:
  0.0 0.0 copy-start
  0.0 1.1 %copy-done = f32[32,16,384]{2,1,0:T(8,128)S(1)} copy-done((f32[32,16,384]{2,1,0:T(8,128)S(1)}, f32[32,16,384]{2,1,0:T(8,128)}, u32[]{:S(2)}) %copy-start) | copy-done | bytes 786456
  1.1 0.0 copy-start.1
  1.1 0.4 shard_map.82
  1.6 0.7 %copy-done.1 = f32[32,16,384]{2,1,0:T(8,128)S(1)} copy-done((f32[32,16,384]{2,1,0:T(8,128)S(1)}, f32[32,16,384]{2,1,0:T(8,128)}, u32[]{:S(2)}) %copy-start.1) | copy-done | bytes 786456
  2.3 0.0 copy-start.2
  2.3 1.1 %copy-done.2 = f32[32,16,384]{2,1,0:T(8,128)S(1)} copy-done((f32[32,16,384]{2,1,0:T(8,128)S(1)}, f32[32,16,384]{2,1,0:T(8,128)}, u32[]{:S(2)}) %copy-start.2) | copy-done | bytes 786456
  3.4 0.0 copy-start.4
  3.4 0.7 %copy-done.4 = s32[4,384]{1,0:T(4,128)S(1)} copy-done((s32[4,384]{1,0:T(4,128)S(1)}, s32[4,384]{1,0:T(4,128)}, u32[]{:S(2)}) %copy-start.4) | copy-done | bytes 6168
  4.1 0.0 copy-start.5
  4.1 0.7 %copy-done.5 = s32[4,384]{1,0:T(4,128)S(1)} copy-done((s32[4,384]{1,0:T(4,128)S(1)}, s32[4,384]{1,0:T(4,128)}, u32[]{:S(2)}) %copy-start.5) | copy-done | bytes 6168
  4.8 1.7 %shard_map.83 = (f32[16,32,384]{2,1,0:T(8,128)S(1)}, f32[144,128]{1,0:T(8,128)S(1)}, f32[64,128]{1,0:T(8,128)S(1)}, f32[64,128]{1,0:T(8,128)S(1)}, s32[1,384]{1,0:T(1,128)S(1)}) custom-call(f32[512,384]{1,0:T(8,128)S(1)} %bitcast.5, f32[512,384]{1,0:T(8,128)S(1)} %bitcast.6, f32[512,384]{1,0:T(8,128)S(1)} %bitcast.7, ...), custom_call_target="tpu_custom_call" | custom-call | tf_op jit(solution)/shard_map/pallas_call | solution.py:352
  6.5 0.1 collective-permute-start.3
  6.6 1.1 %collective-permute-start = (f32[4,32,384]{2,1,0:T(8,128)S(1)}, f32[4,32,384]{2,1,0:T(8,128)S(1)}, u32[]{:S(2)}, u32[]{:S(2)}) collective-permute-start(f32[4,32,384]{2,1,0:T(8,128)S(1)} %get-tuple-element.25), channel_id=1, source_target_pairs={{0,1},{1,0},{2,3},{3,2},{4,5},{5,4},{6,7},{7,6},{8,9},{9,8},{10,11... | collective-permute-start | bytes 589832 | tf_op jit(solution)/shard_map/ppermute | solution.py:348
  7.7 1.5 %collective-permute-start.1 = (f32[4,32,384]{2,1,0:T(8,128)S(1)}, f32[4,32,384]{2,1,0:T(8,128)S(1)}, u32[]{:S(2)}, u32[]{:S(2)}) collective-permute-start(f32[4,32,384]{2,1,0:T(8,128)S(1)} %get-tuple-element.26), channel_id=1, source_target_pairs={{0,2},{1,3},{2,0},{3,1},{4,6},{5,7},{6,4},{7,5},{8,10},{9,11},{10,... | collective-permute-start | bytes 589832 | tf_op jit(solution)/shard_map/ppermute | solution.py:348
  9.2 1.0 %collective-permute-start.2 = (f32[4,32,384]{2,1,0:T(8,128)S(1)}, f32[4,32,384]{2,1,0:T(8,128)S(1)}, u32[]{:S(2)}, u32[]{:S(2)}) collective-permute-start(f32[4,32,384]{2,1,0:T(8,128)S(1)} %get-tuple-element.27), channel_id=1, source_target_pairs={{0,3},{1,2},{2,1},{3,0},{4,7},{5,6},{6,5},{7,4},{8,11},{9,10},{10,... | collective-permute-start | bytes 589832 | tf_op jit(solution)/shard_map/ppermute | solution.py:348
  10.2 0.0 collective-permute-start.4
  10.2 1.2 %collective-permute-done.4._row.partner_row = f32[64,128]{1,0:T(8,128)S(1)} collective-permute-done((f32[64,128]{1,0:T(8,128)S(1)}, f32[64,128]{1,0:T(8,128)S(1)}, u32[]{:S(2)}, u32[]{:S(2)}) %collective-permute-start.4) | collective-permute-done | bytes 32800 | tf_op jit(solution)/shard_map/ppermute | solution.py:348
  11.4 0.0 collective-permute-done.3.b
  11.4 0.5 collective-permute-start.7
  12.0 2.9 %collective-permute-start.6 = (f32[152,128]{1,0:T(8,128)S(1)}, f32[152,128]{1,0:T(8,128)S(1)}, u32[]{:S(2)}, u32[]{:S(2)}) collective-permute-start(f32[152,128]{1,0:T(8,128)S(1)} %shard_map.85.a), channel_id=1, source_target_pairs={{0,16},{4,20},{8,24},{12,28},{16,0},{20,4},{24,8},{28,12},{32,48},... | collective-permute-start | bytes 233480 | tf_op jit(solution)/shard_map/ppermute | solution.py:348
  14.9 1.1 %collective-permute-done.7.d = f32[152,128]{1,0:T(8,128)S(1)} collective-permute-done((f32[152,128]{1,0:T(8,128)S(1)}, f32[152,128]{1,0:T(8,128)S(1)}, u32[]{:S(2)}, u32[]{:S(2)}) %collective-permute-start.7) | collective-permute-done | bytes 77856 | tf_op jit(solution)/shard_map/ppermute | solution.py:348
  15.9 4.2 %collective-permute-start.5 = (f32[152,128]{1,0:T(8,128)S(1)}, f32[152,128]{1,0:T(8,128)S(1)}, u32[]{:S(2)}, u32[]{:S(2)}) collective-permute-start(f32[152,128]{1,0:T(8,128)S(1)} %shard_map.85.a), channel_id=1, source_target_pairs={{0,8},{4,12},{8,0},{12,4},{16,24},{20,28},{24,16},{28,20},{32,40},... | collective-permute-start | bytes 233480 | tf_op jit(solution)/shard_map/ppermute | solution.py:348
  20.1 0.0 collective-permute-done.6.c
  20.1 1.9 %collective-permute-start.12 = (f32[64,128]{1,0:T(8,128)S(1)}, f32[64,128]{1,0:T(8,128)S(1)}, u32[]{:S(2)}, u32[]{:S(2)}) collective-permute-start(f32[64,128]{1,0:T(8,128)S(1)} %get-tuple-element.36), channel_id=1, source_target_pairs={{4,8},{12,16},{20,24},{28,32},{36,40},{44,48},{52,56},{60,64},{68,... | collective-permute-start | bytes 98312 | tf_op jit(solution)/shard_map/ppermute | solution.py:372
  22.0 0.5 collective-permute-done.5.b
  22.5 0.0 copy-start.3
  22.5 0.1 collective-permute-start.11
  22.6 0.0 collective-permute-done.one
  22.6 0.3 collective-permute-done.1.two
  22.9 9.8 %collective-permute-done.2.three = f32[4,32,384]{2,1,0:T(8,128)S(1)} collective-permute-done((f32[4,32,384]{2,1,0:T(8,128)S(1)}, f32[4,32,384]{2,1,0:T(8,128)S(1)}, u32[]{:S(2)}, u32[]{:S(2)}) %collective-permute-start.2) | collective-permute-done | bytes 196640 | tf_op jit(solution)/shard_map/ppermute | solution.py:348
  32.7 0.0 copy-start.6
  32.7 0.1 shard_map.84.columns
  32.8 0.0 copy-done.3
  32.8 0.6 %copy-done.6 = s32[4,384]{1,0:T(4,128)S(1)} copy-done((s32[4,384]{1,0:T(4,128)S(1)}, s32[4,384]{1,0:T(4,128)}, u32[]{:S(2)}) %copy-start.6) | copy-done | bytes 6168
  33.4 0.9 %shard_map.87 = (f32[4,32,384]{2,1,0:T(8,128)S(1)}, f32[4,32,384]{2,1,0:T(8,128)S(1)}, f32[4,32,384]{2,1,0:T(8,128)S(1)}, f32[4,32,384]{2,1,0:T(8,128)S(1)}) custom-call(f32[4,128,384]{2,1,0:T(8,128)S(1)} %shard_map.84.columns, s32[4,384]{1,0:T(4,128)S(1)} %copy-done.6, f32[128,128]{1,0:T(8,128)S(1)} %copy-done.3, f32[8,128]{1,0:T(8,128)S(1)} %get-tuple-element.30._rim), custom_call_target="tpu_custom_call" | custom-call | tf_op jit(solution)/shard_map/pallas_call | solution.py:381
  34.3 0.1 collective-permute-start.8
  34.4 1.8 %collective-permute-start.9 = (f32[4,32,384]{2,1,0:T(8,128)S(1)}, f32[4,32,384]{2,1,0:T(8,128)S(1)}, u32[]{:S(2)}, u32[]{:S(2)}) collective-permute-start(f32[4,32,384]{2,1,0:T(8,128)S(1)} %get-tuple-element.33), channel_id=1, source_target_pairs={{0,2},{1,3},{2,0},{3,1},{4,6},{5,7},{6,4},{7,5},{8,10},{9,11},{10,... | collective-permute-start | bytes 589832 | tf_op jit(solution)/shard_map/ppermute | solution.py:348
  36.3 1.6 %collective-permute-start.10 = (f32[4,32,384]{2,1,0:T(8,128)S(1)}, f32[4,32,384]{2,1,0:T(8,128)S(1)}, u32[]{:S(2)}, u32[]{:S(2)}) collective-permute-start(f32[4,32,384]{2,1,0:T(8,128)S(1)} %get-tuple-element.34), channel_id=1, source_target_pairs={{0,3},{1,2},{2,1},{3,0},{4,7},{5,6},{6,5},{7,4},{8,11},{9,10},{10,... | collective-permute-start | bytes 589832 | tf_op jit(solution)/shard_map/ppermute | solution.py:348
  37.9 0.0 collective-permute-done.12.other_row
  37.9 0.0 collective-permute-done.11.theirs
  37.9 0.1 shard_map.89
  38.0 2.8 %collective-permute-start.15 = (f32[448,128]{1,0:T(8,128)S(1)}, f32[448,128]{1,0:T(8,128)S(1)}, u32[]{:S(2)}, u32[]{:S(2)}) collective-permute-start(f32[448,128]{1,0:T(8,128)S(1)} %get-tuple-element.39.rest_0_), channel_id=1, source_target_pairs={{0,96},{4,100},{8,104},{12,108},{16,112},{20,116},{24,120},{28,124... | collective-permute-start | bytes 688136 | tf_op jit(solution)/shard_map/ppermute | solution.py:348
  40.8 0.8 %collective-permute-start.14 = (f32[448,128]{1,0:T(8,128)S(1)}, f32[448,128]{1,0:T(8,128)S(1)}, u32[]{:S(2)}, u32[]{:S(2)}) collective-permute-start(f32[448,128]{1,0:T(8,128)S(1)} %get-tuple-element.39.rest_0_), channel_id=1, source_target_pairs={{0,64},{4,68},{8,72},{12,76},{16,80},{20,84},{24,88},{28,92},{32,9... | collective-permute-start | bytes 688136 | tf_op jit(solution)/shard_map/ppermute | solution.py:348
  41.6 0.6 %collective-permute-done.8.one = f32[4,32,384]{2,1,0:T(8,128)S(1)} collective-permute-done((f32[4,32,384]{2,1,0:T(8,128)S(1)}, f32[4,32,384]{2,1,0:T(8,128)S(1)}, u32[]{:S(2)}, u32[]{:S(2)}) %collective-permute-start.8) | collective-permute-done | bytes 196640 | tf_op jit(solution)/shard_map/ppermute | solution.py:348
  42.2 1.5 %collective-permute-start.13 = (f32[448,128]{1,0:T(8,128)S(1)}, f32[448,128]{1,0:T(8,128)S(1)}, u32[]{:S(2)}, u32[]{:S(2)}) collective-permute-start(f32[448,128]{1,0:T(8,128)S(1)} %get-tuple-element.39.rest_0_), channel_id=1, source_target_pairs={{0,32},{4,36},{8,40},{12,44},{16,48},{20,52},{24,56},{28,60},{32,0... | collective-permute-start | bytes 688136 | tf_op jit(solution)/shard_map/ppermute | solution.py:348
  43.7 6.3 %collective-permute-done.9.two = f32[4,32,384]{2,1,0:T(8,128)S(1)} collective-permute-done((f32[4,32,384]{2,1,0:T(8,128)S(1)}, f32[4,32,384]{2,1,0:T(8,128)S(1)}, u32[]{:S(2)}, u32[]{:S(2)}) %collective-permute-start.9) | collective-permute-done | bytes 196640 | tf_op jit(solution)/shard_map/ppermute | solution.py:348
  50.0 4.4 %collective-permute-done.10.three = f32[4,32,384]{2,1,0:T(8,128)S(1)} collective-permute-done((f32[4,32,384]{2,1,0:T(8,128)S(1)}, f32[4,32,384]{2,1,0:T(8,128)S(1)}, u32[]{:S(2)}, u32[]{:S(2)}) %collective-permute-start.10) | collective-permute-done | bytes 196640 | tf_op jit(solution)/shard_map/ppermute | solution.py:348
  54.4 0.0 copy-start.7
  54.4 0.1 shard_map.88.changed
  54.5 0.0 collective-permute-done.15.rest_3_
  54.5 0.0 collective-permute-done.14.rest_2_
  54.5 0.0 collective-permute-done.13.rest_1_
  54.6 0.5 copy-done.7
  55.1 2.3 %shard_map.90 = f32[512,384]{1,0:T(8,128)} custom-call(f32[16,32,384]{2,1,0:T(8,128)S(1)} %get-tuple-element.24.stepped, f32[16,32,384]{2,1,0:T(8,128)S(1)} %shard_map.88.changed, f32[128,128]{1,0:T(8,128)S(1)} %get-tuple-element.37.before, f32[128,128]{1,0:T(8,128)S(1)} %get-tuple-element.38.after, f32[448,128]{1,0:T(8,128)S(1)} %get-tuple-element.39.rest_0_, ...), custom_call_target="tpu_custom_call" | custom-call | tf_op jit(solution)/shard_map/pallas_call | solution.py:390
  (2 shorter events, 0.0 us)
Async XLA Ops:
  0.0 1.1 %copy-start = (f32[32,16,384]{2,1,0:T(8,128)S(1)}, f32[32,16,384]{2,1,0:T(8,128)}, u32[]{:S(2)}) copy-start(f32[32,16,384]{2,1,0:T(8,128)} %param.8) | copy-start | bytes 2359300
  1.1 1.1 %copy-start.1 = (f32[32,16,384]{2,1,0:T(8,128)S(1)}, f32[32,16,384]{2,1,0:T(8,128)}, u32[]{:S(2)}) copy-start(f32[32,16,384]{2,1,0:T(8,128)} %param.9) | copy-start | bytes 2359300
  2.3 1.1 %copy-start.2 = (f32[32,16,384]{2,1,0:T(8,128)S(1)}, f32[32,16,384]{2,1,0:T(8,128)}, u32[]{:S(2)}) copy-start(f32[32,16,384]{2,1,0:T(8,128)} %param.10) | copy-start | bytes 2359300
  3.4 0.7 %copy-start.4 = (s32[4,384]{1,0:T(4,128)S(1)}, s32[4,384]{1,0:T(4,128)}, u32[]{:S(2)}) copy-start(s32[4,384]{1,0:T(4,128)} %near.1) | copy-start | bytes 18436
  4.1 0.7 %copy-start.5 = (s32[4,384]{1,0:T(4,128)S(1)}, s32[4,384]{1,0:T(4,128)}, u32[]{:S(2)}) copy-start(s32[4,384]{1,0:T(4,128)} %edge_of.1) | copy-start | bytes 18436
  6.5 4.9 %collective-permute-start.3 = (f32[144,128]{1,0:T(8,128)S(1)}, f32[144,128]{1,0:T(8,128)S(1)}, u32[]{:S(2)}, u32[]{:S(2)}) collective-permute-start(f32[144,128]{1,0:T(8,128)S(1)} %get-tuple-element.28.a), channel_id=1, source_target_pairs={{0,4},{4,0},{8,12},{12,8},{16,20},{20,16},{24,28},{28,24},{32,36},... | collective-permute-start | bytes 221192 | tf_op jit(solution)/shard_map/ppermute | solution.py:348
  6.6 16.0 %collective-permute-start = (f32[4,32,384]{2,1,0:T(8,128)S(1)}, f32[4,32,384]{2,1,0:T(8,128)S(1)}, u32[]{:S(2)}, u32[]{:S(2)}) collective-permute-start(f32[4,32,384]{2,1,0:T(8,128)S(1)} %get-tuple-element.25), channel_id=1, source_target_pairs={{0,1},{1,0},{2,3},{3,2},{4,5},{5,4},{6,7},{7,6},{8,9},{9,8},{10,11... | collective-permute-start | bytes 589832 | tf_op jit(solution)/shard_map/ppermute | solution.py:348
  7.7 15.2 %collective-permute-start.1 = (f32[4,32,384]{2,1,0:T(8,128)S(1)}, f32[4,32,384]{2,1,0:T(8,128)S(1)}, u32[]{:S(2)}, u32[]{:S(2)}) collective-permute-start(f32[4,32,384]{2,1,0:T(8,128)S(1)} %get-tuple-element.26), channel_id=1, source_target_pairs={{0,2},{1,3},{2,0},{3,1},{4,6},{5,7},{6,4},{7,5},{8,10},{9,11},{10,... | collective-permute-start | bytes 589832 | tf_op jit(solution)/shard_map/ppermute | solution.py:348
  9.2 23.5 %collective-permute-start.2 = (f32[4,32,384]{2,1,0:T(8,128)S(1)}, f32[4,32,384]{2,1,0:T(8,128)S(1)}, u32[]{:S(2)}, u32[]{:S(2)}) collective-permute-start(f32[4,32,384]{2,1,0:T(8,128)S(1)} %get-tuple-element.27), channel_id=1, source_target_pairs={{0,3},{1,2},{2,1},{3,0},{4,7},{5,6},{6,5},{7,4},{8,11},{9,10},{10,... | collective-permute-start | bytes 589832 | tf_op jit(solution)/shard_map/ppermute | solution.py:348
  10.2 1.2 %collective-permute-start.4 = (f32[64,128]{1,0:T(8,128)S(1)}, f32[64,128]{1,0:T(8,128)S(1)}, u32[]{:S(2)}, u32[]{:S(2)}) collective-permute-start(f32[64,128]{1,0:T(8,128)S(1)} %get-tuple-element.29), channel_id=1, source_target_pairs={{0,4},{4,0},{8,12},{12,8},{16,20},{20,16},{24,28},{28,24},{32,36},... | collective-permute-start | bytes 98312 | tf_op jit(solution)/shard_map/ppermute | solution.py:348
  11.4 4.5 %collective-permute-start.7 = (f32[152,128]{1,0:T(8,128)S(1)}, f32[152,128]{1,0:T(8,128)S(1)}, u32[]{:S(2)}, u32[]{:S(2)}) collective-permute-start(f32[152,128]{1,0:T(8,128)S(1)} %shard_map.85.a), channel_id=1, source_target_pairs={{0,24},{4,28},{8,16},{12,20},{16,8},{20,12},{24,0},{28,4},{32,56},... | collective-permute-start | bytes 233480 | tf_op jit(solution)/shard_map/ppermute | solution.py:348
  12.0 8.1 %collective-permute-start.6 = (f32[152,128]{1,0:T(8,128)S(1)}, f32[152,128]{1,0:T(8,128)S(1)}, u32[]{:S(2)}, u32[]{:S(2)}) collective-permute-start(f32[152,128]{1,0:T(8,128)S(1)} %shard_map.85.a), channel_id=1, source_target_pairs={{0,16},{4,20},{8,24},{12,28},{16,0},{20,4},{24,8},{28,12},{32,48},... | collective-permute-start | bytes 233480 | tf_op jit(solution)/shard_map/ppermute | solution.py:348
  15.9 6.5 %collective-permute-start.5 = (f32[152,128]{1,0:T(8,128)S(1)}, f32[152,128]{1,0:T(8,128)S(1)}, u32[]{:S(2)}, u32[]{:S(2)}) collective-permute-start(f32[152,128]{1,0:T(8,128)S(1)} %shard_map.85.a), channel_id=1, source_target_pairs={{0,8},{4,12},{8,0},{12,4},{16,24},{20,28},{24,16},{28,20},{32,40},... | collective-permute-start | bytes 233480 | tf_op jit(solution)/shard_map/ppermute | solution.py:348
  20.1 17.8 %collective-permute-start.12 = (f32[64,128]{1,0:T(8,128)S(1)}, f32[64,128]{1,0:T(8,128)S(1)}, u32[]{:S(2)}, u32[]{:S(2)}) collective-permute-start(f32[64,128]{1,0:T(8,128)S(1)} %get-tuple-element.36), channel_id=1, source_target_pairs={{4,8},{12,16},{20,24},{28,32},{36,40},{44,48},{52,56},{60,64},{68,... | collective-permute-start | bytes 98312 | tf_op jit(solution)/shard_map/ppermute | solution.py:372
  22.5 10.3 %copy-start.3 = (f32[128,128]{1,0:T(8,128)S(1)}, f32[128,128]{1,0:T(8,128)}, u32[]{:S(2)}) copy-start(f32[128,128]{1,0:T(8,128)} %mixing.1) | copy-start | bytes 196612
  22.5 15.4 %collective-permute-start.11 = (f32[224,128]{1,0:T(8,128)S(1)}, f32[224,128]{1,0:T(8,128)S(1)}, u32[]{:S(2)}, u32[]{:S(2)}) collective-permute-start(f32[224,128]{1,0:T(8,128)S(1)} %get-tuple-element.35.mine), channel_id=1, source_target_pairs={{0,128},{4,132},{8,136},{12,140},{16,144},{20,148},{24,152},{28,15... | collective-permute-start | bytes 344072 | tf_op jit(solution)/shard_map/ppermute | solution.py:348
  32.7 0.7 %copy-start.6 = (s32[4,384]{1,0:T(4,128)S(1)}, s32[4,384]{1,0:T(4,128)}, u32[]{:S(2)}) copy-start(s32[4,384]{1,0:T(4,128)} %mask.1) | copy-start | bytes 18436
  34.3 7.9 %collective-permute-start.8 = (f32[4,32,384]{2,1,0:T(8,128)S(1)}, f32[4,32,384]{2,1,0:T(8,128)S(1)}, u32[]{:S(2)}, u32[]{:S(2)}) collective-permute-start(f32[4,32,384]{2,1,0:T(8,128)S(1)} %get-tuple-element.32), channel_id=1, source_target_pairs={{0,1},{1,0},{2,3},{3,2},{4,5},{5,4},{6,7},{7,6},{8,9},{9,8},{10,11... | collective-permute-start | bytes 589832 | tf_op jit(solution)/shard_map/ppermute | solution.py:348
  34.4 15.6 %collective-permute-start.9 = (f32[4,32,384]{2,1,0:T(8,128)S(1)}, f32[4,32,384]{2,1,0:T(8,128)S(1)}, u32[]{:S(2)}, u32[]{:S(2)}) collective-permute-start(f32[4,32,384]{2,1,0:T(8,128)S(1)} %get-tuple-element.33), channel_id=1, source_target_pairs={{0,2},{1,3},{2,0},{3,1},{4,6},{5,7},{6,4},{7,5},{8,10},{9,11},{10,... | collective-permute-start | bytes 589832 | tf_op jit(solution)/shard_map/ppermute | solution.py:348
  36.3 18.2 %collective-permute-start.10 = (f32[4,32,384]{2,1,0:T(8,128)S(1)}, f32[4,32,384]{2,1,0:T(8,128)S(1)}, u32[]{:S(2)}, u32[]{:S(2)}) collective-permute-start(f32[4,32,384]{2,1,0:T(8,128)S(1)} %get-tuple-element.34), channel_id=1, source_target_pairs={{0,3},{1,2},{2,1},{3,0},{4,7},{5,6},{6,5},{7,4},{8,11},{9,10},{10,... | collective-permute-start | bytes 589832 | tf_op jit(solution)/shard_map/ppermute | solution.py:348
  38.0 16.5 %collective-permute-start.15 = (f32[448,128]{1,0:T(8,128)S(1)}, f32[448,128]{1,0:T(8,128)S(1)}, u32[]{:S(2)}, u32[]{:S(2)}) collective-permute-start(f32[448,128]{1,0:T(8,128)S(1)} %get-tuple-element.39.rest_0_), channel_id=1, source_target_pairs={{0,96},{4,100},{8,104},{12,108},{16,112},{20,116},{24,120},{28,124... | collective-permute-start | bytes 688136 | tf_op jit(solution)/shard_map/ppermute | solution.py:348
  40.8 13.7 %collective-permute-start.14 = (f32[448,128]{1,0:T(8,128)S(1)}, f32[448,128]{1,0:T(8,128)S(1)}, u32[]{:S(2)}, u32[]{:S(2)}) collective-permute-start(f32[448,128]{1,0:T(8,128)S(1)} %get-tuple-element.39.rest_0_), channel_id=1, source_target_pairs={{0,64},{4,68},{8,72},{12,76},{16,80},{20,84},{24,88},{28,92},{32,9... | collective-permute-start | bytes 688136 | tf_op jit(solution)/shard_map/ppermute | solution.py:348
  42.2 12.3 %collective-permute-start.13 = (f32[448,128]{1,0:T(8,128)S(1)}, f32[448,128]{1,0:T(8,128)S(1)}, u32[]{:S(2)}, u32[]{:S(2)}) collective-permute-start(f32[448,128]{1,0:T(8,128)S(1)} %get-tuple-element.39.rest_0_), channel_id=1, source_target_pairs={{0,32},{4,36},{8,40},{12,44},{16,48},{20,52},{24,56},{28,60},{32,0... | collective-permute-start | bytes 688136 | tf_op jit(solution)/shard_map/ppermute | solution.py:348
  54.4 0.7 %copy-start.7 = (s32[4,384]{1,0:T(4,128)S(1)}, s32[4,384]{1,0:T(4,128)}, u32[]{:S(2)}) copy-start(s32[4,384]{1,0:T(4,128)} %rest_5_.1) | copy-start | bytes 18436

commit v3 on v2

--- a/solution.py
+++ b/solution.py
@@ -108,13 +108,10 @@
     wind_x,
     wind_y,
     _sent,
-    near,
-    edge_of,
     stepped,
     contrib,
     to_partner,
     to_other,
-    wanted,
 ):
     step = pl.program_id(0)
     lanes = pl.ds(pl.multiple_of(128 * step, 128), 128)
@@ -132,7 +129,6 @@
     @pl.when(step == 2)
     def _():
         take_edges(stepped, contrib, to_partner, to_other)
-        wanted[...] = wanted_places(near[...], edge_of[...])
 
 
 def take_edges(stepped, contrib, to_partner, to_other):
@@ -164,22 +160,29 @@
     contrib[140:CONTRIB] = jnp.zeros((CONTRIB - 140, 128), jnp.float32)
 
 
-def pair_kernel(a, b, _row, out):
+def pair_kernel(a, b, _row, _one, out):
     out[0:12] = a[0:12]
     out[12:24] = b[0:12]
     out[24:152] = a[12:140] + b[12:140]
 
 
-def merge_kernel(a, b, c, d, out, done):
+def merge_kernel(a, b, c, d, near, edge_of, turns, mask, mixing, *outs):
+    out, wanted, turns_out, mask_out, mixing_out = outs
+    wanted[...] = wanted_places(near[...], edge_of[...])
+    turns_out[...] = turns[...]
+    mask_out[...] = mask[...]
+    mixing_out[...] = mixing[...]
     for k, part in enumerate((a, b, c, d)):
         out[24 * k : 24 * k + 24] = part[0:24]
     out[96:224] = (a[24:152] + b[24:152]) + (c[24:152] + d[24:152])
-    done[...] = jnp.zeros((8, 128), jnp.float32)
-
-
-def join_kernel(mine, theirs, partner_row, other_row, out, before, after):
+
+
+def join_kernel(mine, theirs, partner_row, other_row, out, both, before, after):
     out[:MERGED] = mine[...]
     out[MERGED:] = theirs[...]
+    for k in range(2):
+        both[k, :MERGED] = mine[...]
+        both[k, MERGED:] = theirs[...]
     even = lax.axis_index("curve") % 2 == 0
     partner, other = partner_row[...], other_row[...]
     last = jnp.where(even, other, partner)
@@ -201,7 +204,7 @@
     return pl.ds(pl.multiple_of(32 * lev, 32), 32)
 
 
-def physics_kernel(columns, mask, mixing, _rim, *rest):
+def physics_kernel(columns, mask, mixing, *rest):
     backs, change = rest[:4], rest[4]
     me = lax.axis_index("lev")
     mix = mixing[...]
@@ -257,59 +260,47 @@
     return jnp.concatenate([row_place(0, row0), row_place(2, row63), sides], axis=1)
 
 
-def change_kernel(stepped, own, one, two, three, out):
+def change_kernel(base, own, one, two, three, out):
     me = lax.axis_index("lev")
     for k, part in enumerate((own, one, two, three)):
         for p in range(4):
             at = 4 * (me ^ k) + p
-            out[at] = stepped[at] + part[p]
-
-
-def edge_kernel(stepped, changed, before, after, *rest):
-    pools, (wanted_ref, reversed_edge, out, held, sems) = rest[:4], rest[4:]
+            out[at] = base[at] + part[p]
+
+
+POINT = [[0, 1, 2, 3], [3, 7, 11, 15], [12, 13, 14, 15], [0, 4, 8, 12]]
+
+
+def edge_of_tile(stepped, k, v):
+    return jnp.concatenate([stepped[p, :, 128 * v : 128 * v + 128] for p in POINT[k]], axis=0)
+
+
+def oriented(values, turn):
+    four = [values[32 * t : 32 * t + 32] for t in range(4)]
+    return [jnp.where(turn, four[3 - t], four[t]) for t in range(4)]
+
+
+def rim_masks(v):
     row0, row63 = rim_rows()
-    turned = reversed_edge[...] == 1
-    wanted = wanted_ref[...]
     lane = lax.broadcasted_iota(jnp.int32, (1, 128), 1)
-    half = lane // NE
+    row = 2 * v + lane // NE
     side_lane, at_left = side_lanes(lane)
-    found = None
-    for k, pool in enumerate(pools):
-        at = lax.broadcasted_iota(jnp.int32, (PIECE, 3 * 128), 0) + PIECE * k
-        part = exact_dot((at == wanted).astype(jnp.bfloat16), pool[...], TN)
-        found = part if found is None else found + part
-    found0, found2, found_side = found[:, :128], found[:, 128:256], found[:, 256:]
-
+    return [row == row0, side_lane & ~at_left, row == row63, at_left]
+
+
+def near_kernel(stepped, before, after, turns, base):
+    turned = turns[...] == 1
     backwards = 127 - lax.broadcasted_iota(jnp.int32, (128, 128), 1)
 
     def flip(values):
         return jnp.take_along_axis(values, backwards, axis=1)
 
-    def oriented(values, turn):
-        four = [values[32 * t : 32 * t + 32] for t in range(4)]
-        return [jnp.where(turn, four[3 - t], four[t]) for t in range(4)]
-
-    point = [
-        [0, 1, 2, 3],
-        [3, 7, 11, 15],
-        [12, 13, 14, 15],
-        [0, 4, 8, 12],
-    ]
-
-    def edge(k, v):
-        return jnp.concatenate(
-            [stepped[p, :, 128 * v : 128 * v + 128] for p in point[k]], axis=0
-        )
-
-    flipped0 = [flip(edge(0, v)) for v in range(3)] + [flip(after[...])]
-    flipped2 = [flip(before[...])] + [flip(edge(2, v)) for v in range(3)]
-    lower = half == 0
-    copies = []
+    lower = lax.broadcasted_iota(jnp.int32, (1, 128), 1) < NE
+    flipped0 = [flip(edge_of_tile(stepped, 0, v)) for v in range(3)] + [flip(after[...])]
+    flipped2 = [flip(before[...])] + [flip(edge_of_tile(stepped, 2, v)) for v in range(3)]
     for v in range(3):
         lanes = slice(128 * v, 128 * v + 128)
-        row = 2 * v + half
-        own = [edge(k, v) for k in range(4)]
-        back = pltpu.roll(found_side, (128 - 2 * v) % 128, 1) if v else found_side
+        own = [edge_of_tile(stepped, k, v) for k in range(4)]
         to_next = [pltpu.roll(own[k], 127, 1) for k in (1, 3)]
         to_last = [pltpu.roll(own[k], 1, 1) for k in (1, 3)]
         across = [
@@ -318,16 +309,41 @@
             jnp.where(lower, flipped0[v], flipped0[v + 1]),
             jnp.where(lower, to_last[0], to_next[0]),
         ]
-        across[0] = jnp.where(row == row0, found0, across[0])
-        across[2] = jnp.where(row == row63, found2, across[2])
-        across[3] = jnp.where(at_left, back, across[3])
-        across[1] = jnp.where(side_lane & ~at_left, back, across[1])
-        total = [changed[p, :, lanes] for p in range(16)]
+        total = [stepped[p, :, lanes] for p in range(16)]
+        far = rim_masks(v)
         for k in range(4):
             theirs = oriented(across[k], turned[k : k + 1, lanes])
             for t in range(4):
-                p = point[k][t]
-                total[p] = total[p] + 0.5 * (theirs[t] - own[k][32 * t : 32 * t + 32])
+                p = POINT[k][t]
+                term = 0.5 * (theirs[t] - own[k][32 * t : 32 * t + 32])
+                total[p] = total[p] + jnp.where(far[k], 0.0, term)
+        for p in range(16):
+            base[p, :, lanes] = total[p]
+
+
+def edge_kernel(stepped, changed, own, one, both, three, wanted, turns, out, held, sems):
+    other = 1 - (lax.axis_index("curve") // 16) % 2
+    pools = own, one, both.at[other], three
+    turned = turns[...] == 1
+    found = None
+    for k, pool in enumerate(pools):
+        at = lax.broadcasted_iota(jnp.int32, (PIECE, 3 * 128), 0) + PIECE * k
+        part = exact_dot((at == wanted[...]).astype(jnp.bfloat16), pool[...], TN)
+        found = part if found is None else found + part
+    found0, found2, found_side = found[:, :128], found[:, 128:256], found[:, 256:]
+    copies = []
+    for v in range(3):
+        lanes = slice(128 * v, 128 * v + 128)
+        back = pltpu.roll(found_side, (128 - 2 * v) % 128, 1) if v else found_side
+        total = [changed[p, :, lanes] for p in range(16)]
+        far = rim_masks(v)
+        for k, across in enumerate((found0, back, found2, back)):
+            own = edge_of_tile(stepped, k, v)
+            theirs = oriented(across, turned[k : k + 1, lanes])
+            for t in range(4):
+                p = POINT[k][t]
+                term = 0.5 * (theirs[t] - own[32 * t : 32 * t + 32])
+                total[p] = total[p] + jnp.where(far[k], term, 0.0)
         for p in range(16):
             held[v, pl.ds(p, 32, stride=16), :] = total[p]
         copies.append(
@@ -349,51 +365,65 @@
 
     sends = lane_call(split_kernel, (part,) * 4, [flat_block], (part_block,) * 4)(flat)
     cells = [swap(sends[k], "lev", k) for k in (1, 2, 3)]
-    stepped, contrib, to_partner, to_other, wanted = lane_call(
+    stepped, contrib, to_partner, to_other = lane_call(
         step_kernel,
         (
             f32((16, 32, E)),
             f32((CONTRIB, 128)),
             f32((64, 128)),
             f32((64, 128)),
-            jax.ShapeDtypeStruct((1, E), jnp.int32),
         ),
-        [flat_block] * 3 + [whole(4, 32, E), whole(4, E), whole(4, E)],
-        (whole(16, 32, E), whole(CONTRIB, 128), whole(64, 128), whole(64, 128), whole(1, E)),
+        [flat_block] * 3 + [whole(4, 32, E)],
+        (whole(16, 32, E), whole(CONTRIB, 128), whole(64, 128), whole(64, 128)),
     )(
         flat,
         wind_x.reshape(512, E),
         wind_y.reshape(512, E),
         sends[0],
-        neighbor,
-        neighbor_edge,
     )
     inner = [(i, i + 1) for i in range(1, 62, 2) if i != 31]
     other_row = lax.ppermute(to_other, "curve", inner + [(j, i) for i, j in inner])
     partner_row = swap(to_partner, "curve", 1)
-    paired = call(pair_kernel, f32((PAIRED, 128)), 3)(
-        contrib, swap(contrib, "curve", 1), partner_row
+    paired = call(pair_kernel, f32((PAIRED, 128)), 4)(
+        contrib, swap(contrib, "curve", 1), partner_row, cells[0]
     )
     along_y = [swap(paired, "curve", k << 1) for k in (1, 2, 3)]
-    merged, done = call(merge_kernel, (f32((MERGED, 128)), f32((8, 128))), 4)(paired, *along_y)
+    table = jax.ShapeDtypeStruct((4, E), jnp.int32)
+    merged, wanted, turns, mask, mix = call(
+        merge_kernel,
+        (
+            f32((MERGED, 128)),
+            jax.ShapeDtypeStruct((1, E), jnp.int32),
+            table,
+            table,
+            f32((128, 128)),
+        ),
+        9,
+    )(paired, *along_y, neighbor, neighbor_edge, reversed_edge, branch_mask, mixing)
     long = pl.CostEstimate(flops=10**11, bytes_accessed=10**8, transcendentals=0)
     columns = call(column_kernel, f32((4, 128, E)), 4, cost=long)(sends[0], *cells)
     backs = call(
-        physics_kernel, (part,) * 4, 4, [pltpu.VMEM((4, 128, E), jnp.float32)]
-    )(columns, branch_mask, mixing, done)
+        physics_kernel, (part,) * 4, 3, [pltpu.VMEM((4, 128, E), jnp.float32)]
+    )(columns, mask, mix)
     changes = [swap(backs[k], "lev", k) for k in (1, 2, 3)]
-    piece, before, after = call(
-        join_kernel, (f32((2 * MERGED, 128)), f32((128, 128)), f32((128, 128))), 4, cost=long
+    piece, twice, before, after = call(
+        join_kernel,
+        (f32((PIECE, 128)), f32((2, PIECE, 128)), f32((128, 128)), f32((128, 128))),
+        4,
+        cost=long,
     )(merged, swap(merged, "curve", 32), partner_row, other_row)
-    along_x = [swap(piece, "curve", k << 3) for k in (1, 2, 3)]
-    changed = call(change_kernel, f32((16, 32, E)), 5, cost=long)(stepped, backs[0], *changes)
+    along_x = [swap(piece, "curve", k << 3) for k in (1, 3)]
+    groups = [[i, i ^ 16] for i in range(64) if not i & 16]
+    across_x = lax.all_to_all(twice, "curve", 0, 0, axis_index_groups=groups, tiled=True)
+    base = call(near_kernel, f32((16, 32, E)), 4)(stepped, before, after, turns)
+    changed = call(change_kernel, f32((16, 32, E)), 5, cost=long)(base, backs[0], *changes)
     out = call(
         edge_kernel,
         f32((512, E)),
-        10,
+        8,
         [pltpu.VMEM((3, 512, 128), jnp.float32), pltpu.SemaphoreType.DMA((3,))],
         out_spec=pl.BlockSpec(memory_space=pl.ANY),
-    )(stepped, changed, before, after, piece, *along_x, wanted, reversed_edge)
+    )(stepped, changed, piece, along_x[0], across_x, along_x[1], wanted, turns)
     return out.reshape(32, 16, E)
 
 

time: 57.8 us -> 53.5 us (0.926)
  the two profiles are of different devices: /device:TPU:176 before, /device:TPU:192 now
where the time goes in v3:
time: 53.5 us; the launch traced here: 53.2 us
  waiting for transfers between devices  23.1 us (43%)
  starting transfers between devices  21 us (39%)
  Pallas kernels  6.69 us (13%)
  local copies, waits for them, and re-layouts  2.29 us (4%)
    ppermute x14, waiting for transfers between devices, swap(): return lax.ppermute(array, axis, [(i, i ^ bits) for i in range(devices)])  17.9 us
    ppermute x14, starting transfers between devices, swap(): return lax.ppermute(array, axis, [(i, i ^ bits) for i in range(devices)])  16.9 us
    all_to_all x1, waiting for transfers between devices, on_device(): lax.all_to_all(twice, 'curve', 0, 0, axis_index_groups=groups, tiled=True)  5.19 us
    all_to_all x1, starting transfers between devices, on_device(): lax.all_to_all(twice, 'curve', 0, 0, axis_index_groups=groups, tiled=True)  3.48 us
    unnamed x16, local copies, waits for them, and re-layouts  2.29 us
    pallas_call x1, Pallas kernels, on_device(): call(edge_kernel, f32((512, E)), 8, [pltpu.VMEM((3, 512, 128), jnp.float3...  2.11 us
    pallas_call x1, Pallas kernels, on_device(): lane_call(step_kernel, (f32((16, 32, E)), f32((CONTRIB, 128)), f32((64, 1...  1.73 us
  transfers between devices with their start and end apart: 16, of which 8 were waited for; matrix products, arithmetic and copies ran while one was open for 0% of the time, Pallas kernels for 8%

profile of v3, /device:TPU:192, one launch (start us, length us, event | category | flops | bytes accessed | tf_op | source)
XLA Modules:
  0.0 53.2 jit_solution(13797692187649235035)
XLA Ops:
  0.0 0.0 copy-start
  0.0 1.1 %copy-done = f32[32,16,384]{2,1,0:T(8,128)S(1)} copy-done((f32[32,16,384]{2,1,0:T(8,128)S(1)}, f32[32,16,384]{2,1,0:T(8,128)}, u32[]{:S(2)}) %copy-start) | copy-done | bytes 786456
  1.1 0.0 copy-start.1
  1.1 0.4 shard_map.82
  1.6 1.1 %collective-permute-start.2 = (f32[4,32,384]{2,1,0:T(8,128)S(1)}, f32[4,32,384]{2,1,0:T(8,128)S(1)}, u32[]{:S(2)}, u32[]{:S(2)}) collective-permute-start(f32[4,32,384]{2,1,0:T(8,128)S(1)} %get-tuple-element.30), channel_id=1, source_target_pairs={{0,1},{1,0},{2,3},{3,2},{4,5},{5,4},{6,7},{7,6},{8,9},{9,8},{10,11... | collective-permute-start | bytes 589832 | tf_op jit(solution)/shard_map/ppermute | solution.py:364
  2.7 1.5 %collective-permute-start.8 = (f32[4,32,384]{2,1,0:T(8,128)S(1)}, f32[4,32,384]{2,1,0:T(8,128)S(1)}, u32[]{:S(2)}, u32[]{:S(2)}) collective-permute-start(f32[4,32,384]{2,1,0:T(8,128)S(1)} %get-tuple-element.36), channel_id=1, source_target_pairs={{0,2},{1,3},{2,0},{3,1},{4,6},{5,7},{6,4},{7,5},{8,10},{9,11},{10,... | collective-permute-start | bytes 589832 | tf_op jit(solution)/shard_map/ppermute | solution.py:364
  4.1 1.0 %collective-permute-start.9 = (f32[4,32,384]{2,1,0:T(8,128)S(1)}, f32[4,32,384]{2,1,0:T(8,128)S(1)}, u32[]{:S(2)}, u32[]{:S(2)}) collective-permute-start(f32[4,32,384]{2,1,0:T(8,128)S(1)} %get-tuple-element.37), channel_id=1, source_target_pairs={{0,3},{1,2},{2,1},{3,0},{4,7},{5,6},{6,5},{7,4},{8,11},{9,10},{10,... | collective-permute-start | bytes 589832 | tf_op jit(solution)/shard_map/ppermute | solution.py:364
  5.2 0.0 copy-done.1
  5.2 0.0 copy-start.2
  5.2 1.1 %copy-done.2 = f32[32,16,384]{2,1,0:T(8,128)S(1)} copy-done((f32[32,16,384]{2,1,0:T(8,128)S(1)}, f32[32,16,384]{2,1,0:T(8,128)}, u32[]{:S(2)}) %copy-start.2) | copy-done | bytes 786456
  6.3 1.7 %shard_map.83 = (f32[16,32,384]{2,1,0:T(8,128)S(1)}, f32[144,128]{1,0:T(8,128)S(1)}, f32[64,128]{1,0:T(8,128)S(1)}, f32[64,128]{1,0:T(8,128)S(1)}) custom-call(f32[512,384]{1,0:T(8,128)S(1)} %bitcast.5, f32[512,384]{1,0:T(8,128)S(1)} %bitcast.6, f32[512,384]{1,0:T(8,128)S(1)} %bitcast.7, f32[4,32,384]{2,1,0:T(8,128)S(1)} %get-tuple-element.26._sent.own), custom_call_target="tpu_custom_call" | custom-call | tf_op jit(solution)/shard_map/pallas_call | solution.py:368
  8.0 0.1 collective-permute-start
  8.1 0.0 copy-start.3
  8.2 0.5 collective-permute-start.1
  8.6 0.9 %collective-permute-done.1._row.partner_row = f32[64,128]{1,0:T(8,128)S(1)} collective-permute-done((f32[64,128]{1,0:T(8,128)S(1)}, f32[64,128]{1,0:T(8,128)S(1)}, u32[]{:S(2)}, u32[]{:S(2)}) %collective-permute-start.1) | collective-permute-done | bytes 32800 | tf_op jit(solution)/shard_map/ppermute | solution.py:364
  9.5 0.0 collective-permute-done.b
  9.5 0.5 collective-permute-done.2._one.one
  10.0 0.0 copy-start.4
  10.0 0.0 copy-start.5
  10.0 0.0 copy-start.6
  10.0 0.0 copy-start.7
  10.0 1.7 %collective-permute-start.3 = (f32[152,128]{1,0:T(8,128)S(1)}, f32[152,128]{1,0:T(8,128)S(1)}, u32[]{:S(2)}, u32[]{:S(2)}) collective-permute-start(f32[152,128]{1,0:T(8,128)S(1)} %shard_map.84.a), channel_id=1, source_target_pairs={{0,8},{4,12},{8,0},{12,4},{16,24},{20,28},{24,16},{28,20},{32,40},... | collective-permute-start | bytes 233480 | tf_op jit(solution)/shard_map/ppermute | solution.py:364
  11.7 2.9 %collective-permute-start.4 = (f32[152,128]{1,0:T(8,128)S(1)}, f32[152,128]{1,0:T(8,128)S(1)}, u32[]{:S(2)}, u32[]{:S(2)}) collective-permute-start(f32[152,128]{1,0:T(8,128)S(1)} %shard_map.84.a), channel_id=1, source_target_pairs={{0,16},{4,20},{8,24},{12,28},{16,0},{20,4},{24,8},{28,12},{32,48},... | collective-permute-start | bytes 233480 | tf_op jit(solution)/shard_map/ppermute | solution.py:364
  14.6 0.2 collective-permute-start.5
  14.8 0.0 collective-permute-done.3.b
  14.8 0.7 %collective-permute-start.7 = (f32[64,128]{1,0:T(8,128)S(1)}, f32[64,128]{1,0:T(8,128)S(1)}, u32[]{:S(2)}, u32[]{:S(2)}) collective-permute-start(f32[64,128]{1,0:T(8,128)S(1)} %get-tuple-element.32), channel_id=1, source_target_pairs={{4,8},{12,16},{20,24},{28,32},{36,40},{44,48},{52,56},{60,64},{68,... | collective-permute-start | bytes 98312 | tf_op jit(solution)/shard_map/ppermute | solution.py:385
  15.5 3.0 %collective-permute-done.4.c = f32[152,128]{1,0:T(8,128)S(1)} collective-permute-done((f32[152,128]{1,0:T(8,128)S(1)}, f32[152,128]{1,0:T(8,128)S(1)}, u32[]{:S(2)}, u32[]{:S(2)}) %collective-permute-start.4) | collective-permute-done | bytes 77856 | tf_op jit(solution)/shard_map/ppermute | solution.py:364
  18.5 1.8 %collective-permute-done.5.d = f32[152,128]{1,0:T(8,128)S(1)} collective-permute-done((f32[152,128]{1,0:T(8,128)S(1)}, f32[152,128]{1,0:T(8,128)S(1)}, u32[]{:S(2)}, u32[]{:S(2)}) %collective-permute-start.5) | collective-permute-done | bytes 77856 | tf_op jit(solution)/shard_map/ppermute | solution.py:364
  20.2 0.0 copy-done.3
  20.2 0.0 copy-done.4
  20.2 0.0 copy-done.5
  20.2 0.0 copy-done.6
  20.2 0.0 copy-done.7
  20.2 0.1 shard_map.85
  20.4 0.8 %collective-permute-start.6 = (f32[224,128]{1,0:T(8,128)S(1)}, f32[224,128]{1,0:T(8,128)S(1)}, u32[]{:S(2)}, u32[]{:S(2)}) collective-permute-start(f32[224,128]{1,0:T(8,128)S(1)} %get-tuple-element.31.mine), channel_id=1, source_target_pairs={{0,128},{4,132},{8,136},{12,140},{16,144},{20,148},{24,152},{28,15... | collective-permute-start | bytes 344072 | tf_op jit(solution)/shard_map/ppermute | solution.py:364
  21.2 0.0 collective-permute-done.8.two
  21.2 1.0 %collective-permute-done.9.three = f32[4,32,384]{2,1,0:T(8,128)S(1)} collective-permute-done((f32[4,32,384]{2,1,0:T(8,128)S(1)}, f32[4,32,384]{2,1,0:T(8,128)S(1)}, u32[]{:S(2)}, u32[]{:S(2)}) %collective-permute-start.9) | collective-permute-done | bytes 196640 | tf_op jit(solution)/shard_map/ppermute | solution.py:364
  22.2 0.1 shard_map.88.columns
  22.2 0.9 %shard_map.89 = (f32[4,32,384]{2,1,0:T(8,128)S(1)}, f32[4,32,384]{2,1,0:T(8,128)S(1)}, f32[4,32,384]{2,1,0:T(8,128)S(1)}, f32[4,32,384]{2,1,0:T(8,128)S(1)}) custom-call(f32[4,128,384]{2,1,0:T(8,128)S(1)} %shard_map.88.columns, s32[4,384]{1,0:T(4,128)S(1)} %get-tuple-element.38.mask, f32[128,128]{1,0:T(8,128)S(1)} %get-tuple-element.39.mixing), custom_call_target="tpu_custom_call" | custom-call | tf_op jit(solution)/shard_map/pallas_call | solution.py:405
  23.1 1.6 %collective-permute-start.10 = (f32[4,32,384]{2,1,0:T(8,128)S(1)}, f32[4,32,384]{2,1,0:T(8,128)S(1)}, u32[]{:S(2)}, u32[]{:S(2)}) collective-permute-start(f32[4,32,384]{2,1,0:T(8,128)S(1)} %get-tuple-element.41), channel_id=1, source_target_pairs={{0,1},{1,0},{2,3},{3,2},{4,5},{5,4},{6,7},{7,6},{8,9},{9,8},{10,11... | collective-permute-start | bytes 589832 | tf_op jit(solution)/shard_map/ppermute | solution.py:364
  24.7 1.0 %collective-permute-start.11 = (f32[4,32,384]{2,1,0:T(8,128)S(1)}, f32[4,32,384]{2,1,0:T(8,128)S(1)}, u32[]{:S(2)}, u32[]{:S(2)}) collective-permute-start(f32[4,32,384]{2,1,0:T(8,128)S(1)} %get-tuple-element.42), channel_id=1, source_target_pairs={{0,2},{1,3},{2,0},{3,1},{4,6},{5,7},{6,4},{7,5},{8,10},{9,11},{10,... | collective-permute-start | bytes 589832 | tf_op jit(solution)/shard_map/ppermute | solution.py:364
  25.7 1.0 %collective-permute-start.12 = (f32[4,32,384]{2,1,0:T(8,128)S(1)}, f32[4,32,384]{2,1,0:T(8,128)S(1)}, u32[]{:S(2)}, u32[]{:S(2)}) collective-permute-start(f32[4,32,384]{2,1,0:T(8,128)S(1)} %get-tuple-element.43), channel_id=1, source_target_pairs={{0,3},{1,2},{2,1},{3,0},{4,7},{5,6},{6,5},{7,4},{8,11},{9,10},{10,... | collective-permute-start | bytes 589832 | tf_op jit(solution)/shard_map/ppermute | solution.py:364
  26.7 0.0 collective-permute-done.7.other_row
  26.7 8.8 %collective-permute-done.6.theirs = f32[224,128]{1,0:T(8,128)S(1)} collective-permute-done((f32[224,128]{1,0:T(8,128)S(1)}, f32[224,128]{1,0:T(8,128)S(1)}, u32[]{:S(2)}, u32[]{:S(2)}) %collective-permute-start.6) | collective-permute-done | bytes 114720 | tf_op jit(solution)/shard_map/ppermute | solution.py:364
  35.5 0.8 %shard_map.86 = (f32[448,128]{1,0:T(8,128)S(1)}, f32[2,448,128]{2,1,0:T(8,128)}, f32[128,128]{1,0:T(8,128)S(1)}, f32[128,128]{1,0:T(8,128)S(1)}) custom-call(f32[224,128]{1,0:T(8,128)S(1)} %get-tuple-element.31.mine, f32[224,128]{1,0:T(8,128)S(1)} %collective-permute-done.6.theirs, f32[64,128]{1,0:T(8,128)S(1)} %collective-permute-done.1._row.partner_row, ...), custom_call_target="tpu_custom_call" | custom-call | flops 99999997952 | bytes 100000000 | tf_op jit(solution)/shard_map/pallas_call | solution.py:409
  36.3 1.5 %collective-permute-start.13 = (f32[448,128]{1,0:T(8,128)S(1)}, f32[448,128]{1,0:T(8,128)S(1)}, u32[]{:S(2)}, u32[]{:S(2)}) collective-permute-start(f32[448,128]{1,0:T(8,128)S(1)} %get-tuple-element.44.own), channel_id=1, source_target_pairs={{0,32},{4,36},{8,40},{12,44},{16,48},{20,52},{24,56},{28,60},{32,0... | collective-permute-start | bytes 688136 | tf_op jit(solution)/shard_map/ppermute | solution.py:364
  37.8 2.1 %collective-permute-start.14 = (f32[448,128]{1,0:T(8,128)S(1)}, f32[448,128]{1,0:T(8,128)S(1)}, u32[]{:S(2)}, u32[]{:S(2)}) collective-permute-start(f32[448,128]{1,0:T(8,128)S(1)} %get-tuple-element.44.own), channel_id=1, source_target_pairs={{0,96},{4,100},{8,104},{12,108},{16,112},{20,116},{24,120},{28,124... | collective-permute-start | bytes 688136 | tf_op jit(solution)/shard_map/ppermute | solution.py:364
  39.9 3.5 %all-to-all-start = ((f32[2,448,128]{2,1,0:T(8,128)}), f32[2,448,128]{2,1,0:T(8,128)S(1)}, u32[]{:S(2)}, u32[]{:S(2)}) async-start(f32[2,448,128]{2,1,0:T(8,128)} %get-tuple-element.45), calls=%async_computation | async-start | bytes 917504 | tf_op jit(solution)/shard_map/all_to_all | solution.py:417
  43.4 0.4 shard_map.87.base
  43.8 0.0 collective-permute-done.10.one
  43.8 0.0 collective-permute-done.11.two
  43.8 2.0 %collective-permute-done.12.three = f32[4,32,384]{2,1,0:T(8,128)S(1)} collective-permute-done((f32[4,32,384]{2,1,0:T(8,128)S(1)}, f32[4,32,384]{2,1,0:T(8,128)S(1)}, u32[]{:S(2)}, u32[]{:S(2)}) %collective-permute-start.12) | collective-permute-done | bytes 196640 | tf_op jit(solution)/shard_map/ppermute | solution.py:364
  45.8 0.1 shard_map.90.changed
  45.9 0.0 collective-permute-done.13.one
  45.9 0.0 collective-permute-done.14.three
  45.9 5.2 %all-to-all-done.both = f32[2,448,128]{2,1,0:T(8,128)S(1)} async-done(((f32[2,448,128]{2,1,0:T(8,128)}), f32[2,448,128]{2,1,0:T(8,128)S(1)}, u32[]{:S(2)}, u32[]{:S(2)}) %all-to-all-start) | async-done | bytes 458784 | tf_op jit(solution)/shard_map/all_to_all | solution.py:417
  51.1 2.1 %shard_map.91 = f32[512,384]{1,0:T(8,128)} custom-call(f32[16,32,384]{2,1,0:T(8,128)S(1)} %get-tuple-element.27.stepped, f32[16,32,384]{2,1,0:T(8,128)S(1)} %shard_map.90.changed, f32[448,128]{1,0:T(8,128)S(1)} %get-tuple-element.44.own, f32[448,128]{1,0:T(8,128)S(1)} %collective-permute-done.13.one, f32[2,448,128]{2,1,0:T(8,128)S(1)} %all-to-all-done.both, ...), custom_call_target="tpu_custom_call" | custom-call | tf_op jit(solution)/shard_map/pallas_call | solution.py:420
  (1 shorter events, 0.0 us)
Async XLA Ops:
  0.0 1.1 %copy-start = (f32[32,16,384]{2,1,0:T(8,128)S(1)}, f32[32,16,384]{2,1,0:T(8,128)}, u32[]{:S(2)}) copy-start(f32[32,16,384]{2,1,0:T(8,128)} %param.8) | copy-start | bytes 2359300
  1.1 4.0 %copy-start.1 = (f32[32,16,384]{2,1,0:T(8,128)S(1)}, f32[32,16,384]{2,1,0:T(8,128)}, u32[]{:S(2)}) copy-start(f32[32,16,384]{2,1,0:T(8,128)} %param.9) | copy-start | bytes 2359300
  1.6 8.4 %collective-permute-start.2 = (f32[4,32,384]{2,1,0:T(8,128)S(1)}, f32[4,32,384]{2,1,0:T(8,128)S(1)}, u32[]{:S(2)}, u32[]{:S(2)}) collective-permute-start(f32[4,32,384]{2,1,0:T(8,128)S(1)} %get-tuple-element.30), channel_id=1, source_target_pairs={{0,1},{1,0},{2,3},{3,2},{4,5},{5,4},{6,7},{7,6},{8,9},{9,8},{10,11... | collective-permute-start | bytes 589832 | tf_op jit(solution)/shard_map/ppermute | solution.py:364
  2.7 18.5 %collective-permute-start.8 = (f32[4,32,384]{2,1,0:T(8,128)S(1)}, f32[4,32,384]{2,1,0:T(8,128)S(1)}, u32[]{:S(2)}, u32[]{:S(2)}) collective-permute-start(f32[4,32,384]{2,1,0:T(8,128)S(1)} %get-tuple-element.36), channel_id=1, source_target_pairs={{0,2},{1,3},{2,0},{3,1},{4,6},{5,7},{6,4},{7,5},{8,10},{9,11},{10,... | collective-permute-start | bytes 589832 | tf_op jit(solution)/shard_map/ppermute | solution.py:364
  4.1 18.0 %collective-permute-start.9 = (f32[4,32,384]{2,1,0:T(8,128)S(1)}, f32[4,32,384]{2,1,0:T(8,128)S(1)}, u32[]{:S(2)}, u32[]{:S(2)}) collective-permute-start(f32[4,32,384]{2,1,0:T(8,128)S(1)} %get-tuple-element.37), channel_id=1, source_target_pairs={{0,3},{1,2},{2,1},{3,0},{4,7},{5,6},{6,5},{7,4},{8,11},{9,10},{10,... | collective-permute-start | bytes 589832 | tf_op jit(solution)/shard_map/ppermute | solution.py:364
  5.2 1.1 %copy-start.2 = (f32[32,16,384]{2,1,0:T(8,128)S(1)}, f32[32,16,384]{2,1,0:T(8,128)}, u32[]{:S(2)}) copy-start(f32[32,16,384]{2,1,0:T(8,128)} %param.10) | copy-start | bytes 2359300
  8.0 1.5 %collective-permute-start = (f32[144,128]{1,0:T(8,128)S(1)}, f32[144,128]{1,0:T(8,128)S(1)}, u32[]{:S(2)}, u32[]{:S(2)}) collective-permute-start(f32[144,128]{1,0:T(8,128)S(1)} %get-tuple-element.28.a), channel_id=1, source_target_pairs={{0,4},{4,0},{8,12},{12,8},{16,20},{20,16},{24,28},{28,24},{32,36},... | collective-permute-start | bytes 221192 | tf_op jit(solution)/shard_map/ppermute | solution.py:364
  8.1 12.1 %copy-start.3 = (f32[128,128]{1,0:T(8,128)S(1)}, f32[128,128]{1,0:T(8,128)}, u32[]{:S(2)}) copy-start(f32[128,128]{1,0:T(8,128)} %mixing.1) | copy-start | bytes 196612
  8.2 1.3 %collective-permute-start.1 = (f32[64,128]{1,0:T(8,128)S(1)}, f32[64,128]{1,0:T(8,128)S(1)}, u32[]{:S(2)}, u32[]{:S(2)}) collective-permute-start(f32[64,128]{1,0:T(8,128)S(1)} %get-tuple-element.29), channel_id=1, source_target_pairs={{0,4},{4,0},{8,12},{12,8},{16,20},{20,16},{24,28},{28,24},{32,36},... | collective-permute-start | bytes 98312 | tf_op jit(solution)/shard_map/ppermute | solution.py:364
  10.0 10.2 %copy-start.4 = (s32[4,384]{1,0:T(4,128)S(1)}, s32[4,384]{1,0:T(4,128)}, u32[]{:S(2)}) copy-start(s32[4,384]{1,0:T(4,128)} %near.1) | copy-start | bytes 18436
  10.0 10.2 %copy-start.5 = (s32[4,384]{1,0:T(4,128)S(1)}, s32[4,384]{1,0:T(4,128)}, u32[]{:S(2)}) copy-start(s32[4,384]{1,0:T(4,128)} %edge_of.1) | copy-start | bytes 18436
  10.0 10.2 %copy-start.6 = (s32[4,384]{1,0:T(4,128)S(1)}, s32[4,384]{1,0:T(4,128)}, u32[]{:S(2)}) copy-start(s32[4,384]{1,0:T(4,128)} %turns.1) | copy-start | bytes 18436
  10.0 10.2 %copy-start.7 = (s32[4,384]{1,0:T(4,128)S(1)}, s32[4,384]{1,0:T(4,128)}, u32[]{:S(2)}) copy-start(s32[4,384]{1,0:T(4,128)} %mask.1) | copy-start | bytes 18436
  10.0 4.8 %collective-permute-start.3 = (f32[152,128]{1,0:T(8,128)S(1)}, f32[152,128]{1,0:T(8,128)S(1)}, u32[]{:S(2)}, u32[]{:S(2)}) collective-permute-start(f32[152,128]{1,0:T(8,128)S(1)} %shard_map.84.a), channel_id=1, source_target_pairs={{0,8},{4,12},{8,0},{12,4},{16,24},{20,28},{24,16},{28,20},{32,40},... | collective-permute-start | bytes 233480 | tf_op jit(solution)/shard_map/ppermute | solution.py:364
  11.7 6.8 %collective-permute-start.4 = (f32[152,128]{1,0:T(8,128)S(1)}, f32[152,128]{1,0:T(8,128)S(1)}, u32[]{:S(2)}, u32[]{:S(2)}) collective-permute-start(f32[152,128]{1,0:T(8,128)S(1)} %shard_map.84.a), channel_id=1, source_target_pairs={{0,16},{4,20},{8,24},{12,28},{16,0},{20,4},{24,8},{28,12},{32,48},... | collective-permute-start | bytes 233480 | tf_op jit(solution)/shard_map/ppermute | solution.py:364
  14.6 5.6 %collective-permute-start.5 = (f32[152,128]{1,0:T(8,128)S(1)}, f32[152,128]{1,0:T(8,128)S(1)}, u32[]{:S(2)}, u32[]{:S(2)}) collective-permute-start(f32[152,128]{1,0:T(8,128)S(1)} %shard_map.84.a), channel_id=1, source_target_pairs={{0,24},{4,28},{8,16},{12,20},{16,8},{20,12},{24,0},{28,4},{32,56},... | collective-permute-start | bytes 233480 | tf_op jit(solution)/shard_map/ppermute | solution.py:364
  14.8 11.9 %collective-permute-start.7 = (f32[64,128]{1,0:T(8,128)S(1)}, f32[64,128]{1,0:T(8,128)S(1)}, u32[]{:S(2)}, u32[]{:S(2)}) collective-permute-start(f32[64,128]{1,0:T(8,128)S(1)} %get-tuple-element.32), channel_id=1, source_target_pairs={{4,8},{12,16},{20,24},{28,32},{36,40},{44,48},{52,56},{60,64},{68,... | collective-permute-start | bytes 98312 | tf_op jit(solution)/shard_map/ppermute | solution.py:385
  20.4 15.1 %collective-permute-start.6 = (f32[224,128]{1,0:T(8,128)S(1)}, f32[224,128]{1,0:T(8,128)S(1)}, u32[]{:S(2)}, u32[]{:S(2)}) collective-permute-start(f32[224,128]{1,0:T(8,128)S(1)} %get-tuple-element.31.mine), channel_id=1, source_target_pairs={{0,128},{4,132},{8,136},{12,140},{16,144},{20,148},{24,152},{28,15... | collective-permute-start | bytes 344072 | tf_op jit(solution)/shard_map/ppermute | solution.py:364
  23.1 20.7 %collective-permute-start.10 = (f32[4,32,384]{2,1,0:T(8,128)S(1)}, f32[4,32,384]{2,1,0:T(8,128)S(1)}, u32[]{:S(2)}, u32[]{:S(2)}) collective-permute-start(f32[4,32,384]{2,1,0:T(8,128)S(1)} %get-tuple-element.41), channel_id=1, source_target_pairs={{0,1},{1,0},{2,3},{3,2},{4,5},{5,4},{6,7},{7,6},{8,9},{9,8},{10,11... | collective-permute-start | bytes 589832 | tf_op jit(solution)/shard_map/ppermute | solution.py:364
  24.7 19.1 %collective-permute-start.11 = (f32[4,32,384]{2,1,0:T(8,128)S(1)}, f32[4,32,384]{2,1,0:T(8,128)S(1)}, u32[]{:S(2)}, u32[]{:S(2)}) collective-permute-start(f32[4,32,384]{2,1,0:T(8,128)S(1)} %get-tuple-element.42), channel_id=1, source_target_pairs={{0,2},{1,3},{2,0},{3,1},{4,6},{5,7},{6,4},{7,5},{8,10},{9,11},{10,... | collective-permute-start | bytes 589832 | tf_op jit(solution)/shard_map/ppermute | solution.py:364
  25.7 20.1 %collective-permute-start.12 = (f32[4,32,384]{2,1,0:T(8,128)S(1)}, f32[4,32,384]{2,1,0:T(8,128)S(1)}, u32[]{:S(2)}, u32[]{:S(2)}) collective-permute-start(f32[4,32,384]{2,1,0:T(8,128)S(1)} %get-tuple-element.43), channel_id=1, source_target_pairs={{0,3},{1,2},{2,1},{3,0},{4,7},{5,6},{6,5},{7,4},{8,11},{9,10},{10,... | collective-permute-start | bytes 589832 | tf_op jit(solution)/shard_map/ppermute | solution.py:364
  36.3 9.6 %collective-permute-start.13 = (f32[448,128]{1,0:T(8,128)S(1)}, f32[448,128]{1,0:T(8,128)S(1)}, u32[]{:S(2)}, u32[]{:S(2)}) collective-permute-start(f32[448,128]{1,0:T(8,128)S(1)} %get-tuple-element.44.own), channel_id=1, source_target_pairs={{0,32},{4,36},{8,40},{12,44},{16,48},{20,52},{24,56},{28,60},{32,0... | collective-permute-start | bytes 688136 | tf_op jit(solution)/shard_map/ppermute | solution.py:364
  37.8 8.1 %collective-permute-start.14 = (f32[448,128]{1,0:T(8,128)S(1)}, f32[448,128]{1,0:T(8,128)S(1)}, u32[]{:S(2)}, u32[]{:S(2)}) collective-permute-start(f32[448,128]{1,0:T(8,128)S(1)} %get-tuple-element.44.own), channel_id=1, source_target_pairs={{0,96},{4,100},{8,104},{12,108},{16,112},{20,116},{24,120},{28,124... | collective-permute-start | bytes 688136 | tf_op jit(solution)/shard_map/ppermute | solution.py:364
  39.9 11.2 %all-to-all-start = ((f32[2,448,128]{2,1,0:T(8,128)}), f32[2,448,128]{2,1,0:T(8,128)S(1)}, u32[]{:S(2)}, u32[]{:S(2)}) async-start(f32[2,448,128]{2,1,0:T(8,128)} %get-tuple-element.45), calls=%async_computation | async-start | bytes 917504 | tf_op jit(solution)/shard_map/all_to_all | solution.py:417

commit v4 on v3

--- a/solution.py
+++ b/solution.py
@@ -15,7 +15,7 @@
 CONTRIB = 144
 PAIRED = 152
 MERGED = 224
-PIECE = 2 * MERGED
+HALF = 4 * MERGED
 VMEM = pl.BlockSpec(memory_space=pltpu.VMEM)
 ANY = pl.BlockSpec(memory_space=pl.ANY)
 LIMIT = 24 * 1024 * 1024
@@ -161,8 +161,9 @@
 
 
 def pair_kernel(a, b, _row, _one, out):
-    out[0:12] = a[0:12]
-    out[12:24] = b[0:12]
+    even = lax.axis_index("curve") % 2 == 0
+    out[0:12] = jnp.where(even, a[0:12], b[0:12])
+    out[12:24] = jnp.where(even, b[0:12], a[0:12])
     out[24:152] = a[12:140] + b[12:140]
 
 
@@ -178,11 +179,10 @@
 
 
 def join_kernel(mine, theirs, partner_row, other_row, out, both, before, after):
-    out[:MERGED] = mine[...]
-    out[MERGED:] = theirs[...]
+    half = jnp.where(lax.axis_index("curve") % 2 == 0, mine[...], theirs[...])
+    out[...] = half
     for k in range(2):
-        both[k, :MERGED] = mine[...]
-        both[k, MERGED:] = theirs[...]
+        both[k] = half
     even = lax.axis_index("curve") % 2 == 0
     partner, other = partner_row[...], other_row[...]
     last = jnp.where(even, other, partner)
@@ -204,7 +204,7 @@
     return pl.ds(pl.multiple_of(32 * lev, 32), 32)
 
 
-def physics_kernel(columns, mask, mixing, *rest):
+def physics_kernel(columns, mask, mixing, _wanted, *rest):
     backs, change = rest[:4], rest[4]
     me = lax.axis_index("lev")
     mix = mixing[...]
@@ -235,13 +235,13 @@
     lane_of = near - E * device
     row_of, along = lane_of // NE, lane_of % NE
     apart = device ^ curve
-    k_z, k_x, k_y, k_c = apart // 32, (apart // 8) % 4, (apart // 2) % 4, apart % 2
+    k_x, k_y = (apart // 8) % 4, (apart // 2) % 4
     in_merged = jnp.where(
         edge_of % 2 == 1,
-        24 * k_y + 12 * k_c + jnp.where(edge_of == 3, 0, 6) + row_of,
+        24 * k_y + 12 * (device % 2) + jnp.where(edge_of == 3, 0, 6) + row_of,
         96 + jnp.where(edge_of == 0, 0, NE) + along,
     )
-    place = PIECE * k_x + MERGED * k_z + in_merged
+    place = HALF * (apart // 32) + MERGED * k_x + in_merged
     lane = lax.broadcasted_iota(jnp.int32, (1, 128), 1)
     side_lane, at_left = side_lanes(lane)
 
@@ -321,15 +321,22 @@
             base[p, :, lanes] = total[p]
 
 
-def edge_kernel(stepped, changed, own, one, both, three, wanted, turns, out, held, sems):
-    other = 1 - (lax.axis_index("curve") // 16) % 2
-    pools = own, one, both.at[other], three
-    turned = turns[...] == 1
+def pick_kernel(own, one, both, three, wanted, partner_wanted, mine, theirs):
+    curve = lax.axis_index("curve")
+    pools = own, one, both.at[1 - (curve // 16) % 2], three
+    want = jnp.concatenate([wanted[...], partner_wanted[...]], axis=1)
     found = None
     for k, pool in enumerate(pools):
-        at = lax.broadcasted_iota(jnp.int32, (PIECE, 3 * 128), 0) + PIECE * k
-        part = exact_dot((at == wanted[...]).astype(jnp.bfloat16), pool[...], TN)
+        at = lax.broadcasted_iota(jnp.int32, (MERGED, 2 * E), 0) + (MERGED * k + HALF * (curve % 2))
+        part = exact_dot((at == want).astype(jnp.bfloat16), pool[...], TN)
         found = part if found is None else found + part
+    mine[...] = found[:, :E]
+    theirs[...] = found[:, E:]
+
+
+def edge_kernel(stepped, changed, mine, theirs, turns, out, held, sems):
+    turned = turns[...] == 1
+    found = mine[...] + theirs[...]
     found0, found2, found_side = found[:, :128], found[:, 128:256], found[:, 256:]
     copies = []
     for v in range(3):
@@ -400,30 +407,39 @@
         ),
         9,
     )(paired, *along_y, neighbor, neighbor_edge, reversed_edge, branch_mask, mixing)
+    partner_wanted = swap(wanted, "curve", 1)
+    other_half = lax.ppermute(
+        merged,
+        "curve",
+        [(i, i ^ 32) for i in range(1, 64, 2)],
+    )
     long = pl.CostEstimate(flops=10**11, bytes_accessed=10**8, transcendentals=0)
     columns = call(column_kernel, f32((4, 128, E)), 4, cost=long)(sends[0], *cells)
     backs = call(
-        physics_kernel, (part,) * 4, 3, [pltpu.VMEM((4, 128, E), jnp.float32)]
-    )(columns, mask, mix)
+        physics_kernel, (part,) * 4, 4, [pltpu.VMEM((4, 128, E), jnp.float32)]
+    )(columns, mask, mix, partner_wanted)
     changes = [swap(backs[k], "lev", k) for k in (1, 2, 3)]
     piece, twice, before, after = call(
         join_kernel,
-        (f32((PIECE, 128)), f32((2, PIECE, 128)), f32((128, 128)), f32((128, 128))),
+        (f32((MERGED, 128)), f32((2, MERGED, 128)), f32((128, 128)), f32((128, 128))),
         4,
         cost=long,
-    )(merged, swap(merged, "curve", 32), partner_row, other_row)
+    )(merged, other_half, partner_row, other_row)
     along_x = [swap(piece, "curve", k << 3) for k in (1, 3)]
     groups = [[i, i ^ 16] for i in range(64) if not i & 16]
     across_x = lax.all_to_all(twice, "curve", 0, 0, axis_index_groups=groups, tiled=True)
     base = call(near_kernel, f32((16, 32, E)), 4)(stepped, before, after, turns)
     changed = call(change_kernel, f32((16, 32, E)), 5, cost=long)(base, backs[0], *changes)
+    mine, theirs = call(pick_kernel, (f32((128, E)), f32((128, E))), 6)(
+        piece, along_x[0], across_x, along_x[1], wanted, partner_wanted
+    )
     out = call(
         edge_kernel,
         f32((512, E)),
-        8,
+        5,
         [pltpu.VMEM((3, 512, 128), jnp.float32), pltpu.SemaphoreType.DMA((3,))],
         out_spec=pl.BlockSpec(memory_space=pl.ANY),
-    )(stepped, changed, piece, along_x[0], across_x, along_x[1], wanted, turns)
+    )(stepped, changed, mine, swap(theirs, "curve", 1), turns)
     return out.reshape(32, 16, E)
 
 

time: 53.5 us -> 51.8 us (0.968)
  the two profiles are of different devices: /device:TPU:192 before, /device:TPU:1 now
where the time goes in v4:
time: 51.8 us; the launch traced here: 51.1 us
  starting transfers between devices  34.9 us (67%)
  Pallas kernels  7.37 us (14%)
  waiting for transfers between devices  6.23 us (12%)
  local copies, waits for them, and re-layouts  2.3 us (4%)
    ppermute x15, starting transfers between devices, swap(): return lax.ppermute(array, axis, [(i, i ^ bits) for i in range(devices)])  19.5 us
    ppermute x1, starting transfers between devices, on_device(): lax.ppermute(merged, 'curve', [(i, i ^ 32) for i in range(1, 64, 2)])  8.28 us
    all_to_all x1, starting transfers between devices, on_device(): lax.all_to_all(twice, 'curve', 0, 0, axis_index_groups=groups, tiled=True)  4.51 us
    ppermute x15, waiting for transfers between devices, swap(): return lax.ppermute(array, axis, [(i, i ^ bits) for i in range(devices)])  4.2 us
    ppermute x1, starting transfers between devices, on_device(): lax.ppermute(to_other, 'curve', inner + [(j, i) for i, j in inner])  2.65 us
    unnamed x16, local copies, waits for them, and re-layouts  2.3 us
    all_to_all x1, waiting for transfers between devices, on_device(): lax.all_to_all(twice, 'curve', 0, 0, axis_index_groups=groups, tiled=True)  2.02 us
    pallas_call x1, Pallas kernels, on_device(): lane_call(step_kernel, (f32((16, 32, E)), f32((CONTRIB, 128)), f32((64, 1...  1.73 us
  transfers between devices with their start and end apart: 18, of which 6 were waited for; matrix products, arithmetic and copies ran while one was open for 0% of the time, Pallas kernels for 11%

profile of v4, /device:TPU:1, one launch (start us, length us, event | category | flops | bytes accessed | tf_op | source)
XLA Modules:
  0.0 51.1 jit_solution(11116383092902210936)
XLA Ops:
  0.0 0.0 copy-start
  0.0 1.1 %copy-done = f32[32,16,384]{2,1,0:T(8,128)S(1)} copy-done((f32[32,16,384]{2,1,0:T(8,128)S(1)}, f32[32,16,384]{2,1,0:T(8,128)}, u32[]{:S(2)}) %copy-start) | copy-done | bytes 786456
  1.1 0.0 copy-start.1
  1.1 0.4 shard_map.82
  1.6 2.6 %collective-permute-start.2 = (f32[4,32,384]{2,1,0:T(8,128)S(1)}, f32[4,32,384]{2,1,0:T(8,128)S(1)}, u32[]{:S(2)}, u32[]{:S(2)}) collective-permute-start(f32[4,32,384]{2,1,0:T(8,128)S(1)} %get-tuple-element.32), channel_id=1, source_target_pairs={{0,1},{1,0},{2,3},{3,2},{4,5},{5,4},{6,7},{7,6},{8,9},{9,8},{10,11... | collective-permute-start | bytes 589832 | tf_op jit(solution)/shard_map/ppermute | solution.py:371
  4.1 3.0 %collective-permute-start.8 = (f32[4,32,384]{2,1,0:T(8,128)S(1)}, f32[4,32,384]{2,1,0:T(8,128)S(1)}, u32[]{:S(2)}, u32[]{:S(2)}) collective-permute-start(f32[4,32,384]{2,1,0:T(8,128)S(1)} %get-tuple-element.38), channel_id=1, source_target_pairs={{0,2},{1,3},{2,0},{3,1},{4,6},{5,7},{6,4},{7,5},{8,10},{9,11},{10,... | collective-permute-start | bytes 589832 | tf_op jit(solution)/shard_map/ppermute | solution.py:371
  7.1 0.0 collective-permute-start.9
  7.1 0.0 copy-done.1
  7.1 0.0 copy-start.2
  7.1 1.1 %copy-done.2 = f32[32,16,384]{2,1,0:T(8,128)S(1)} copy-done((f32[32,16,384]{2,1,0:T(8,128)S(1)}, f32[32,16,384]{2,1,0:T(8,128)}, u32[]{:S(2)}) %copy-start.2) | copy-done | bytes 786456
  8.3 1.7 %shard_map.83 = (f32[16,32,384]{2,1,0:T(8,128)S(1)}, f32[144,128]{1,0:T(8,128)S(1)}, f32[64,128]{1,0:T(8,128)S(1)}, f32[64,128]{1,0:T(8,128)S(1)}) custom-call(f32[512,384]{1,0:T(8,128)S(1)} %bitcast.5, f32[512,384]{1,0:T(8,128)S(1)} %bitcast.6, f32[512,384]{1,0:T(8,128)S(1)} %bitcast.7, f32[4,32,384]{2,1,0:T(8,128)S(1)} %get-tuple-element.28._sent.own), custom_call_target="tpu_custom_call" | custom-call | tf_op jit(solution)/shard_map/pallas_call | solution.py:375
  10.0 2.3 %collective-permute-start = (f32[144,128]{1,0:T(8,128)S(1)}, f32[144,128]{1,0:T(8,128)S(1)}, u32[]{:S(2)}, u32[]{:S(2)}) collective-permute-start(f32[144,128]{1,0:T(8,128)S(1)} %get-tuple-element.30.a), channel_id=1, source_target_pairs={{0,4},{4,0},{8,12},{12,8},{16,20},{20,16},{24,28},{28,24},{32,36},... | collective-permute-start | bytes 221192 | tf_op jit(solution)/shard_map/ppermute | solution.py:371
  12.3 0.0 copy-start.3
  12.3 0.1 collective-permute-start.1
  12.4 1.1 %collective-permute-done.1._row.partner_row = f32[64,128]{1,0:T(8,128)S(1)} collective-permute-done((f32[64,128]{1,0:T(8,128)S(1)}, f32[64,128]{1,0:T(8,128)S(1)}, u32[]{:S(2)}, u32[]{:S(2)}) %collective-permute-start.1) | collective-permute-done | bytes 32800 | tf_op jit(solution)/shard_map/ppermute | solution.py:371
  13.5 0.0 collective-permute-done.b
  13.5 0.0 collective-permute-done.2._one.one
  13.5 0.0 copy-start.4
  13.5 0.0 copy-start.5
  13.5 0.0 copy-start.6
  13.5 0.0 copy-start.7
  13.6 1.9 %collective-permute-start.5 = (f32[152,128]{1,0:T(8,128)S(1)}, f32[152,128]{1,0:T(8,128)S(1)}, u32[]{:S(2)}, u32[]{:S(2)}) collective-permute-start(f32[152,128]{1,0:T(8,128)S(1)} %shard_map.84.a), channel_id=1, source_target_pairs={{0,24},{4,28},{8,16},{12,20},{16,8},{20,12},{24,0},{28,4},{32,56},... | collective-permute-start | bytes 233480 | tf_op jit(solution)/shard_map/ppermute | solution.py:371
  15.4 0.3 collective-permute-start.4
  15.8 1.1 %collective-permute-start.3 = (f32[152,128]{1,0:T(8,128)S(1)}, f32[152,128]{1,0:T(8,128)S(1)}, u32[]{:S(2)}, u32[]{:S(2)}) collective-permute-start(f32[152,128]{1,0:T(8,128)S(1)} %shard_map.84.a), channel_id=1, source_target_pairs={{0,8},{4,12},{8,0},{12,4},{16,24},{20,28},{24,16},{28,20},{32,40},... | collective-permute-start | bytes 233480 | tf_op jit(solution)/shard_map/ppermute | solution.py:371
  16.9 1.5 %collective-permute-done.5.d = f32[152,128]{1,0:T(8,128)S(1)} collective-permute-done((f32[152,128]{1,0:T(8,128)S(1)}, f32[152,128]{1,0:T(8,128)S(1)}, u32[]{:S(2)}, u32[]{:S(2)}) %collective-permute-start.5) | collective-permute-done | bytes 77856 | tf_op jit(solution)/shard_map/ppermute | solution.py:371
  18.4 2.6 %collective-permute-start.7 = (f32[64,128]{1,0:T(8,128)S(1)}, f32[64,128]{1,0:T(8,128)S(1)}, u32[]{:S(2)}, u32[]{:S(2)}) collective-permute-start(f32[64,128]{1,0:T(8,128)S(1)} %get-tuple-element.34), channel_id=1, source_target_pairs={{4,8},{12,16},{20,24},{28,32},{36,40},{44,48},{52,56},{60,64},{68,... | collective-permute-start | bytes 98312 | tf_op jit(solution)/shard_map/ppermute | solution.py:392
  21.1 0.0 collective-permute-done.4.c
  21.1 0.0 collective-permute-done.3.b
  21.1 0.0 copy-done.3
  21.1 0.0 copy-done.4
  21.1 0.0 copy-done.5
  21.1 0.0 copy-done.6
  21.1 0.0 copy-done.7
  21.1 0.1 shard_map.85
  21.3 1.5 %collective-permute-start.10 = (s32[1,384]{1,0:T(1,128)S(1)}, s32[1,384]{1,0:T(1,128)S(1)}, u32[]{:S(2)}, u32[]{:S(2)}) collective-permute-start(s32[1,384]{1,0:T(1,128)S(1)} %get-tuple-element.42.wanted), channel_id=1, source_target_pairs={{0,4},{4,0},{8,12},{12,8},{16,20},{20,16},{24,28},{28,24},{32,36},... | collective-permute-start | bytes 4616 | tf_op jit(solution)/shard_map/ppermute | solution.py:371
  22.8 8.3 %collective-permute-start.6 = (f32[224,128]{1,0:T(8,128)S(1)}, f32[224,128]{1,0:T(8,128)S(1)}, u32[]{:S(2)}, u32[]{:S(2)}) collective-permute-start(f32[224,128]{1,0:T(8,128)S(1)} %get-tuple-element.33.mine), channel_id=1, source_target_pairs={{4,132},{12,140},{20,148},{28,156},{36,164},{44,172},{52,180},{60,... | collective-permute-start | bytes 344072 | tf_op jit(solution)/shard_map/ppermute | solution.py:411
  31.1 0.0 collective-permute-done.8.two
  31.1 0.0 collective-permute-done.9.three
  31.1 0.1 shard_map.88.columns
  31.2 0.0 collective-permute-done.10._wanted.partner_wanted
  31.2 0.9 %shard_map.89 = (f32[4,32,384]{2,1,0:T(8,128)S(1)}, f32[4,32,384]{2,1,0:T(8,128)S(1)}, f32[4,32,384]{2,1,0:T(8,128)S(1)}, f32[4,32,384]{2,1,0:T(8,128)S(1)}) custom-call(f32[4,128,384]{2,1,0:T(8,128)S(1)} %shard_map.88.columns, s32[4,384]{1,0:T(4,128)S(1)} %get-tuple-element.40.mask, f32[128,128]{1,0:T(8,128)S(1)} %get-tuple-element.41.mixing, ...), custom_call_target="tpu_custom_call" | custom-call | tf_op jit(solution)/shard_map/pallas_call | solution.py:418
  32.1 0.1 collective-permute-start.11
  32.2 1.9 %collective-permute-start.12 = (f32[4,32,384]{2,1,0:T(8,128)S(1)}, f32[4,32,384]{2,1,0:T(8,128)S(1)}, u32[]{:S(2)}, u32[]{:S(2)}) collective-permute-start(f32[4,32,384]{2,1,0:T(8,128)S(1)} %get-tuple-element.45), channel_id=1, source_target_pairs={{0,2},{1,3},{2,0},{3,1},{4,6},{5,7},{6,4},{7,5},{8,10},{9,11},{10,... | collective-permute-start | bytes 589832 | tf_op jit(solution)/shard_map/ppermute | solution.py:371
  34.1 1.6 %collective-permute-start.13 = (f32[4,32,384]{2,1,0:T(8,128)S(1)}, f32[4,32,384]{2,1,0:T(8,128)}, u32[]{:S(2)}, u32[]{:S(2)}) collective-permute-start(f32[4,32,384]{2,1,0:T(8,128)S(1)} %get-tuple-element.46), channel_id=1, source_target_pairs={{0,3},{1,2},{2,1},{3,0},{4,7},{5,6},{6,5},{7,4},{8,11},{9,10},{10,... | collective-permute-start | bytes 589832 | tf_op jit(solution)/shard_map/ppermute | solution.py:371
  35.7 0.0 collective-permute-done.7.other_row
  35.7 0.0 collective-permute-done.6.theirs
  35.7 0.7 %shard_map.86 = (f32[224,128]{1,0:T(8,128)S(1)}, f32[2,224,128]{2,1,0:T(8,128)}, f32[128,128]{1,0:T(8,128)S(1)}, f32[128,128]{1,0:T(8,128)S(1)}) custom-call(f32[224,128]{1,0:T(8,128)S(1)} %get-tuple-element.33.mine, f32[224,128]{1,0:T(8,128)S(1)} %collective-permute-done.6.theirs, f32[64,128]{1,0:T(8,128)S(1)} %collective-permute-done.1._row.partner_row, ...), custom_call_target="tpu_custom_call" | custom-call | flops 99999997952 | bytes 100000000 | tf_op jit(solution)/shard_map/pallas_call | solution.py:422
  36.4 4.5 %all-to-all-start = ((f32[2,224,128]{2,1,0:T(8,128)}), f32[2,224,128]{2,1,0:T(8,128)S(1)}, u32[]{:S(2)}, u32[]{:S(2)}) async-start(f32[2,224,128]{2,1,0:T(8,128)} %get-tuple-element.48), calls=%async_computation | async-start | bytes 458752 | tf_op jit(solution)/shard_map/all_to_all | solution.py:430
  40.9 3.0 %collective-permute-start.15 = (f32[224,128]{1,0:T(8,128)S(1)}, f32[224,128]{1,0:T(8,128)S(1)}, u32[]{:S(2)}, u32[]{:S(2)}) collective-permute-start(f32[224,128]{1,0:T(8,128)S(1)} %get-tuple-element.47.own), channel_id=1, source_target_pairs={{0,96},{4,100},{8,104},{12,108},{16,112},{20,116},{24,120},{28,124... | collective-permute-start | bytes 344072 | tf_op jit(solution)/shard_map/ppermute | solution.py:371
  44.0 0.0 collective-permute-start.14
  44.0 0.4 shard_map.87.base
  44.4 2.0 %all-to-all-done.both = f32[2,224,128]{2,1,0:T(8,128)S(1)} async-done(((f32[2,224,128]{2,1,0:T(8,128)}), f32[2,224,128]{2,1,0:T(8,128)S(1)}, u32[]{:S(2)}, u32[]{:S(2)}) %all-to-all-start) | async-done | bytes 229408 | tf_op jit(solution)/shard_map/all_to_all | solution.py:430
  46.4 1.0 %collective-permute-done.15.three = f32[224,128]{1,0:T(8,128)S(1)} collective-permute-done((f32[224,128]{1,0:T(8,128)S(1)}, f32[224,128]{1,0:T(8,128)S(1)}, u32[]{:S(2)}, u32[]{:S(2)}) %collective-permute-start.15) | collective-permute-done | bytes 114720 | tf_op jit(solution)/shard_map/ppermute | solution.py:371
  47.4 0.2 collective-permute-done.14.one
  47.6 0.8 %shard_map.91 = (f32[128,384]{1,0:T(8,128)S(1)}, f32[128,384]{1,0:T(8,128)S(1)}) custom-call(f32[224,128]{1,0:T(8,128)S(1)} %get-tuple-element.47.own, f32[224,128]{1,0:T(8,128)S(1)} %collective-permute-done.14.one, f32[2,224,128]{2,1,0:T(8,128)S(1)} %all-to-all-done.both, f32[224,128]{1,0:T(8,128)S(1)} %collective-permute-done.15.three, ...), custom_call_target="tpu_custom_call" | custom-call | tf_op jit(solution)/shard_map/pallas_call | solution.py:433
  48.4 0.1 collective-permute-start.16
  48.5 0.0 collective-permute-done.11.one
  48.6 0.0 collective-permute-done.12.two
  48.6 0.0 collective-permute-done.13.three
  48.6 1.0 %shard_map.90.changed = f32[16,32,384]{2,1,0:T(8,128)S(1)} custom-call(f32[16,32,384]{2,1,0:T(8,128)S(1)} %shard_map.87.base, f32[4,32,384]{2,1,0:T(8,128)S(1)} %get-tuple-element.43.own, f32[4,32,384]{2,1,0:T(8,128)S(1)} %collective-permute-done.11.one, f32[4,32,384]{2,1,0:T(8,128)S(1)} %collective-permute-done.12.two, ...), custom_call_target="tpu_custom_call" | custom-call | flops 99999997952 | bytes 100000000 | tf_op jit(solution)/shard_map/pallas_call | solution.py:432
  49.6 0.4 collective-permute-done.16.theirs
  50.0 1.1 %shard_map.92 = f32[512,384]{1,0:T(8,128)} custom-call(f32[16,32,384]{2,1,0:T(8,128)S(1)} %get-tuple-element.29.stepped, f32[16,32,384]{2,1,0:T(8,128)S(1)} %shard_map.90.changed, f32[128,384]{1,0:T(8,128)S(1)} %get-tuple-element.49.mine, f32[128,384]{1,0:T(8,128)S(1)} %collective-permute-done.16.theirs, s32[4,384]{1,0:T(4,128)S(1)} %get-tuple-element.37.turns), custom_call_target="tpu_custom_call" | custom-call | tf_op jit(solution)/shard_map/pallas_call | solution.py:436
  (1 shorter events, 0.0 us)
Async XLA Ops:
  0.0 1.1 %copy-start = (f32[32,16,384]{2,1,0:T(8,128)S(1)}, f32[32,16,384]{2,1,0:T(8,128)}, u32[]{:S(2)}) copy-start(f32[32,16,384]{2,1,0:T(8,128)} %param.8) | copy-start | bytes 2359300
  1.1 6.0 %copy-start.1 = (f32[32,16,384]{2,1,0:T(8,128)S(1)}, f32[32,16,384]{2,1,0:T(8,128)}, u32[]{:S(2)}) copy-start(f32[32,16,384]{2,1,0:T(8,128)} %param.9) | copy-start | bytes 2359300
  1.6 11.9 %collective-permute-start.2 = (f32[4,32,384]{2,1,0:T(8,128)S(1)}, f32[4,32,384]{2,1,0:T(8,128)S(1)}, u32[]{:S(2)}, u32[]{:S(2)}) collective-permute-start(f32[4,32,384]{2,1,0:T(8,128)S(1)} %get-tuple-element.32), channel_id=1, source_target_pairs={{0,1},{1,0},{2,3},{3,2},{4,5},{5,4},{6,7},{7,6},{8,9},{9,8},{10,11... | collective-permute-start | bytes 589832 | tf_op jit(solution)/shard_map/ppermute | solution.py:371
  4.1 26.9 %collective-permute-start.8 = (f32[4,32,384]{2,1,0:T(8,128)S(1)}, f32[4,32,384]{2,1,0:T(8,128)S(1)}, u32[]{:S(2)}, u32[]{:S(2)}) collective-permute-start(f32[4,32,384]{2,1,0:T(8,128)S(1)} %get-tuple-element.38), channel_id=1, source_target_pairs={{0,2},{1,3},{2,0},{3,1},{4,6},{5,7},{6,4},{7,5},{8,10},{9,11},{10,... | collective-permute-start | bytes 589832 | tf_op jit(solution)/shard_map/ppermute | solution.py:371
  7.1 23.9 %collective-permute-start.9 = (f32[4,32,384]{2,1,0:T(8,128)S(1)}, f32[4,32,384]{2,1,0:T(8,128)S(1)}, u32[]{:S(2)}, u32[]{:S(2)}) collective-permute-start(f32[4,32,384]{2,1,0:T(8,128)S(1)} %get-tuple-element.39), channel_id=1, source_target_pairs={{0,3},{1,2},{2,1},{3,0},{4,7},{5,6},{6,5},{7,4},{8,11},{9,10},{10,... | collective-permute-start | bytes 589832 | tf_op jit(solution)/shard_map/ppermute | solution.py:371
  7.1 1.1 %copy-start.2 = (f32[32,16,384]{2,1,0:T(8,128)S(1)}, f32[32,16,384]{2,1,0:T(8,128)}, u32[]{:S(2)}) copy-start(f32[32,16,384]{2,1,0:T(8,128)} %param.10) | copy-start | bytes 2359300
  10.0 3.5 %collective-permute-start = (f32[144,128]{1,0:T(8,128)S(1)}, f32[144,128]{1,0:T(8,128)S(1)}, u32[]{:S(2)}, u32[]{:S(2)}) collective-permute-start(f32[144,128]{1,0:T(8,128)S(1)} %get-tuple-element.30.a), channel_id=1, source_target_pairs={{0,4},{4,0},{8,12},{12,8},{16,20},{20,16},{24,28},{28,24},{32,36},... | collective-permute-start | bytes 221192 | tf_op jit(solution)/shard_map/ppermute | solution.py:371
  12.3 8.8 %copy-start.3 = (f32[128,128]{1,0:T(8,128)S(1)}, f32[128,128]{1,0:T(8,128)}, u32[]{:S(2)}) copy-start(f32[128,128]{1,0:T(8,128)} %mixing.1) | copy-start | bytes 196612
  12.3 1.2 %collective-permute-start.1 = (f32[64,128]{1,0:T(8,128)S(1)}, f32[64,128]{1,0:T(8,128)S(1)}, u32[]{:S(2)}, u32[]{:S(2)}) collective-permute-start(f32[64,128]{1,0:T(8,128)S(1)} %get-tuple-element.31), channel_id=1, source_target_pairs={{0,4},{4,0},{8,12},{12,8},{16,20},{20,16},{24,28},{28,24},{32,36},... | collective-permute-start | bytes 98312 | tf_op jit(solution)/shard_map/ppermute | solution.py:371
  13.5 7.6 %copy-start.4 = (s32[4,384]{1,0:T(4,128)S(1)}, s32[4,384]{1,0:T(4,128)}, u32[]{:S(2)}) copy-start(s32[4,384]{1,0:T(4,128)} %near.1) | copy-start | bytes 18436
  13.5 7.6 %copy-start.5 = (s32[4,384]{1,0:T(4,128)S(1)}, s32[4,384]{1,0:T(4,128)}, u32[]{:S(2)}) copy-start(s32[4,384]{1,0:T(4,128)} %edge_of.1) | copy-start | bytes 18436
  13.5 7.6 %copy-start.6 = (s32[4,384]{1,0:T(4,128)S(1)}, s32[4,384]{1,0:T(4,128)}, u32[]{:S(2)}) copy-start(s32[4,384]{1,0:T(4,128)} %turns.1) | copy-start | bytes 18436
  13.5 7.6 %copy-start.7 = (s32[4,384]{1,0:T(4,128)S(1)}, s32[4,384]{1,0:T(4,128)}, u32[]{:S(2)}) copy-start(s32[4,384]{1,0:T(4,128)} %mask.1) | copy-start | bytes 18436
  13.6 4.8 %collective-permute-start.5 = (f32[152,128]{1,0:T(8,128)S(1)}, f32[152,128]{1,0:T(8,128)S(1)}, u32[]{:S(2)}, u32[]{:S(2)}) collective-permute-start(f32[152,128]{1,0:T(8,128)S(1)} %shard_map.84.a), channel_id=1, source_target_pairs={{0,24},{4,28},{8,16},{12,20},{16,8},{20,12},{24,0},{28,4},{32,56},... | collective-permute-start | bytes 233480 | tf_op jit(solution)/shard_map/ppermute | solution.py:371
  15.4 5.6 %collective-permute-start.4 = (f32[152,128]{1,0:T(8,128)S(1)}, f32[152,128]{1,0:T(8,128)S(1)}, u32[]{:S(2)}, u32[]{:S(2)}) collective-permute-start(f32[152,128]{1,0:T(8,128)S(1)} %shard_map.84.a), channel_id=1, source_target_pairs={{0,16},{4,20},{8,24},{12,28},{16,0},{20,4},{24,8},{28,12},{32,48},... | collective-permute-start | bytes 233480 | tf_op jit(solution)/shard_map/ppermute | solution.py:371
  15.8 5.3 %collective-permute-start.3 = (f32[152,128]{1,0:T(8,128)S(1)}, f32[152,128]{1,0:T(8,128)S(1)}, u32[]{:S(2)}, u32[]{:S(2)}) collective-permute-start(f32[152,128]{1,0:T(8,128)S(1)} %shard_map.84.a), channel_id=1, source_target_pairs={{0,8},{4,12},{8,0},{12,4},{16,24},{20,28},{24,16},{28,20},{32,40},... | collective-permute-start | bytes 233480 | tf_op jit(solution)/shard_map/ppermute | solution.py:371
  18.4 17.3 %collective-permute-start.7 = (f32[64,128]{1,0:T(8,128)S(1)}, f32[64,128]{1,0:T(8,128)S(1)}, u32[]{:S(2)}, u32[]{:S(2)}) collective-permute-start(f32[64,128]{1,0:T(8,128)S(1)} %get-tuple-element.34), channel_id=1, source_target_pairs={{4,8},{12,16},{20,24},{28,32},{36,40},{44,48},{52,56},{60,64},{68,... | collective-permute-start | bytes 98312 | tf_op jit(solution)/shard_map/ppermute | solution.py:392
  21.3 9.9 %collective-permute-start.10 = (s32[1,384]{1,0:T(1,128)S(1)}, s32[1,384]{1,0:T(1,128)S(1)}, u32[]{:S(2)}, u32[]{:S(2)}) collective-permute-start(s32[1,384]{1,0:T(1,128)S(1)} %get-tuple-element.42.wanted), channel_id=1, source_target_pairs={{0,4},{4,0},{8,12},{12,8},{16,20},{20,16},{24,28},{28,24},{32,36},... | collective-permute-start | bytes 4616 | tf_op jit(solution)/shard_map/ppermute | solution.py:371
  22.8 12.9 %collective-permute-start.6 = (f32[224,128]{1,0:T(8,128)S(1)}, f32[224,128]{1,0:T(8,128)S(1)}, u32[]{:S(2)}, u32[]{:S(2)}) collective-permute-start(f32[224,128]{1,0:T(8,128)S(1)} %get-tuple-element.33.mine), channel_id=1, source_target_pairs={{4,132},{12,140},{20,148},{28,156},{36,164},{44,172},{52,180},{60,... | collective-permute-start | bytes 344072 | tf_op jit(solution)/shard_map/ppermute | solution.py:411
  32.1 16.5 %collective-permute-start.11 = (f32[4,32,384]{2,1,0:T(8,128)S(1)}, f32[4,32,384]{2,1,0:T(8,128)S(1)}, u32[]{:S(2)}, u32[]{:S(2)}) collective-permute-start(f32[4,32,384]{2,1,0:T(8,128)S(1)} %get-tuple-element.44), channel_id=1, source_target_pairs={{0,1},{1,0},{2,3},{3,2},{4,5},{5,4},{6,7},{7,6},{8,9},{9,8},{10,11... | collective-permute-start | bytes 589832 | tf_op jit(solution)/shard_map/ppermute | solution.py:371
  32.2 16.4 %collective-permute-start.12 = (f32[4,32,384]{2,1,0:T(8,128)S(1)}, f32[4,32,384]{2,1,0:T(8,128)S(1)}, u32[]{:S(2)}, u32[]{:S(2)}) collective-permute-start(f32[4,32,384]{2,1,0:T(8,128)S(1)} %get-tuple-element.45), channel_id=1, source_target_pairs={{0,2},{1,3},{2,0},{3,1},{4,6},{5,7},{6,4},{7,5},{8,10},{9,11},{10,... | collective-permute-start | bytes 589832 | tf_op jit(solution)/shard_map/ppermute | solution.py:371
  34.1 14.5 %collective-permute-start.13 = (f32[4,32,384]{2,1,0:T(8,128)S(1)}, f32[4,32,384]{2,1,0:T(8,128)}, u32[]{:S(2)}, u32[]{:S(2)}) collective-permute-start(f32[4,32,384]{2,1,0:T(8,128)S(1)} %get-tuple-element.46), channel_id=1, source_target_pairs={{0,3},{1,2},{2,1},{3,0},{4,7},{5,6},{6,5},{7,4},{8,11},{9,10},{10,... | collective-permute-start | bytes 589832 | tf_op jit(solution)/shard_map/ppermute | solution.py:371
  36.4 10.0 %all-to-all-start = ((f32[2,224,128]{2,1,0:T(8,128)}), f32[2,224,128]{2,1,0:T(8,128)S(1)}, u32[]{:S(2)}, u32[]{:S(2)}) async-start(f32[2,224,128]{2,1,0:T(8,128)} %get-tuple-element.48), calls=%async_computation | async-start | bytes 458752 | tf_op jit(solution)/shard_map/all_to_all | solution.py:430
  40.9 6.4 %collective-permute-start.15 = (f32[224,128]{1,0:T(8,128)S(1)}, f32[224,128]{1,0:T(8,128)S(1)}, u32[]{:S(2)}, u32[]{:S(2)}) collective-permute-start(f32[224,128]{1,0:T(8,128)S(1)} %get-tuple-element.47.own), channel_id=1, source_target_pairs={{0,96},{4,100},{8,104},{12,108},{16,112},{20,116},{24,120},{28,124... | collective-permute-start | bytes 344072 | tf_op jit(solution)/shard_map/ppermute | solution.py:371
  44.0 3.6 %collective-permute-start.14 = (f32[224,128]{1,0:T(8,128)S(1)}, f32[224,128]{1,0:T(8,128)S(1)}, u32[]{:S(2)}, u32[]{:S(2)}) collective-permute-start(f32[224,128]{1,0:T(8,128)S(1)} %get-tuple-element.47.own), channel_id=1, source_target_pairs={{0,32},{4,36},{8,40},{12,44},{16,48},{20,52},{24,56},{28,60},{32,0... | collective-permute-start | bytes 344072 | tf_op jit(solution)/shard_map/ppermute | solution.py:371
  48.4 1.5 %collective-permute-start.16 = (f32[128,384]{1,0:T(8,128)S(1)}, f32[128,384]{1,0:T(8,128)S(1)}, u32[]{:S(2)}, u32[]{:S(2)}) collective-permute-start(f32[128,384]{1,0:T(8,128)S(1)} %get-tuple-element.50), channel_id=1, source_target_pairs={{0,4},{4,0},{8,12},{12,8},{16,20},{20,16},{24,28},{28,24},{32,36},... | collective-permute-start | bytes 589832 | tf_op jit(solution)/shard_map/ppermute | solution.py:371

commit v5 on v4

--- a/solution.py
+++ b/solution.py
@@ -260,7 +260,7 @@
     return jnp.concatenate([row_place(0, row0), row_place(2, row63), sides], axis=1)
 
 
-def change_kernel(base, own, one, two, three, out):
+def change_kernel(base, own, two, three, one, out):
     me = lax.axis_index("lev")
     for k, part in enumerate((own, one, two, three)):
         for p in range(4):
@@ -418,7 +418,7 @@
     backs = call(
         physics_kernel, (part,) * 4, 4, [pltpu.VMEM((4, 128, E), jnp.float32)]
     )(columns, mask, mix, partner_wanted)
-    changes = [swap(backs[k], "lev", k) for k in (1, 2, 3)]
+    changes = [swap(backs[k], "lev", k) for k in (2, 3, 1)]
     piece, twice, before, after = call(
         join_kernel,
         (f32((MERGED, 128)), f32((2, MERGED, 128)), f32((128, 128)), f32((128, 128))),

time: 51.8 us -> 51.3 us (level)
  the two profiles are of different devices: /device:TPU:1 before, /device:TPU:193 now
where the time goes in v5:
time: 51.3 us; the launch traced here: 51 us
  starting transfers between devices  32 us (62%)
  waiting for transfers between devices  9.11 us (18%)
  Pallas kernels  7.38 us (14%)
  local copies, waits for them, and re-layouts  2.3 us (4%)
    ppermute x15, starting transfers between devices, swap(): return lax.ppermute(array, axis, [(i, i ^ bits) for i in range(devices)])  17.1 us
    all_to_all x1, starting transfers between devices, on_device(): lax.all_to_all(twice, 'curve', 0, 0, axis_index_groups=groups, tiled=True)  9.77 us
    ppermute x15, waiting for transfers between devices, swap(): return lax.ppermute(array, axis, [(i, i ^ bits) for i in range(devices)])  4.94 us
    ppermute x1, starting transfers between devices, on_device(): lax.ppermute(to_other, 'curve', inner + [(j, i) for i, j in inner])  2.98 us
    ppermute x1, waiting for transfers between devices, on_device(): lax.ppermute(merged, 'curve', [(i, i ^ 32) for i in range(1, 64, 2)])  2.67 us
    unnamed x16, local copies, waits for them, and re-layouts  2.3 us
    ppermute x1, starting transfers between devices, on_device(): lax.ppermute(merged, 'curve', [(i, i ^ 32) for i in range(1, 64, 2)])  2.16 us
    pallas_call x1, Pallas kernels, on_device(): lane_call(step_kernel, (f32((16, 32, E)), f32((CONTRIB, 128)), f32((64, 1...  1.73 us
  transfers between devices with their start and end apart: 18, of which 7 were waited for; matrix products, arithmetic and copies ran while one was open for 0% of the time, Pallas kernels for 11%

profile of v5, /device:TPU:193, one launch (start us, length us, event | category | flops | bytes accessed | tf_op | source)
XLA Modules:
  0.0 51.0 jit_solution(17026732185439189090)
XLA Ops:
  0.0 0.0 copy-start
  0.0 1.1 %copy-done = f32[32,16,384]{2,1,0:T(8,128)S(1)} copy-done((f32[32,16,384]{2,1,0:T(8,128)S(1)}, f32[32,16,384]{2,1,0:T(8,128)}, u32[]{:S(2)}) %copy-start) | copy-done | bytes 786456
  1.1 0.0 copy-start.1
  1.1 0.4 shard_map.82
  1.6 0.8 %collective-permute-start.2 = (f32[4,32,384]{2,1,0:T(8,128)S(1)}, f32[4,32,384]{2,1,0:T(8,128)S(1)}, u32[]{:S(2)}, u32[]{:S(2)}) collective-permute-start(f32[4,32,384]{2,1,0:T(8,128)S(1)} %get-tuple-element.32), channel_id=1, source_target_pairs={{0,1},{1,0},{2,3},{3,2},{4,5},{5,4},{6,7},{7,6},{8,9},{9,8},{10,11... | collective-permute-start | bytes 589832 | tf_op jit(solution)/shard_map/ppermute | solution.py:371
  2.4 1.2 %collective-permute-start.8 = (f32[4,32,384]{2,1,0:T(8,128)S(1)}, f32[4,32,384]{2,1,0:T(8,128)S(1)}, u32[]{:S(2)}, u32[]{:S(2)}) collective-permute-start(f32[4,32,384]{2,1,0:T(8,128)S(1)} %get-tuple-element.38), channel_id=1, source_target_pairs={{0,2},{1,3},{2,0},{3,1},{4,6},{5,7},{6,4},{7,5},{8,10},{9,11},{10,... | collective-permute-start | bytes 589832 | tf_op jit(solution)/shard_map/ppermute | solution.py:371
  3.6 0.7 %collective-permute-start.9 = (f32[4,32,384]{2,1,0:T(8,128)S(1)}, f32[4,32,384]{2,1,0:T(8,128)S(1)}, u32[]{:S(2)}, u32[]{:S(2)}) collective-permute-start(f32[4,32,384]{2,1,0:T(8,128)S(1)} %get-tuple-element.39), channel_id=1, source_target_pairs={{0,3},{1,2},{2,1},{3,0},{4,7},{5,6},{6,5},{7,4},{8,11},{9,10},{10,... | collective-permute-start | bytes 589832 | tf_op jit(solution)/shard_map/ppermute | solution.py:371
  4.3 0.0 copy-done.1
  4.3 0.0 copy-start.2
  4.3 1.1 %copy-done.2 = f32[32,16,384]{2,1,0:T(8,128)S(1)} copy-done((f32[32,16,384]{2,1,0:T(8,128)S(1)}, f32[32,16,384]{2,1,0:T(8,128)}, u32[]{:S(2)}) %copy-start.2) | copy-done | bytes 786456
  5.5 1.7 %shard_map.83 = (f32[16,32,384]{2,1,0:T(8,128)S(1)}, f32[144,128]{1,0:T(8,128)S(1)}, f32[64,128]{1,0:T(8,128)S(1)}, f32[64,128]{1,0:T(8,128)S(1)}) custom-call(f32[512,384]{1,0:T(8,128)S(1)} %bitcast.5, f32[512,384]{1,0:T(8,128)S(1)} %bitcast.6, f32[512,384]{1,0:T(8,128)S(1)} %bitcast.7, f32[4,32,384]{2,1,0:T(8,128)S(1)} %get-tuple-element.28._sent.own), custom_call_target="tpu_custom_call" | custom-call | tf_op jit(solution)/shard_map/pallas_call | solution.py:375
  7.2 1.6 %collective-permute-start = (f32[144,128]{1,0:T(8,128)S(1)}, f32[144,128]{1,0:T(8,128)S(1)}, u32[]{:S(2)}, u32[]{:S(2)}) collective-permute-start(f32[144,128]{1,0:T(8,128)S(1)} %get-tuple-element.30.a), channel_id=1, source_target_pairs={{0,4},{4,0},{8,12},{12,8},{16,20},{20,16},{24,28},{28,24},{32,36},... | collective-permute-start | bytes 221192 | tf_op jit(solution)/shard_map/ppermute | solution.py:371
  8.8 0.0 copy-start.3
  8.8 0.1 collective-permute-start.1
  8.9 1.1 %collective-permute-done.1._row.partner_row = f32[64,128]{1,0:T(8,128)S(1)} collective-permute-done((f32[64,128]{1,0:T(8,128)S(1)}, f32[64,128]{1,0:T(8,128)S(1)}, u32[]{:S(2)}, u32[]{:S(2)}) %collective-permute-start.1) | collective-permute-done | bytes 32800 | tf_op jit(solution)/shard_map/ppermute | solution.py:371
  10.0 0.0 collective-permute-done.b
  10.0 0.0 collective-permute-done.2._one.one
  10.0 0.0 copy-start.4
  10.0 0.0 copy-start.5
  10.0 0.0 copy-start.6
  10.0 0.0 copy-start.7
  10.1 2.8 %collective-permute-start.5 = (f32[152,128]{1,0:T(8,128)S(1)}, f32[152,128]{1,0:T(8,128)S(1)}, u32[]{:S(2)}, u32[]{:S(2)}) collective-permute-start(f32[152,128]{1,0:T(8,128)S(1)} %shard_map.84.a), channel_id=1, source_target_pairs={{0,24},{4,28},{8,16},{12,20},{16,8},{20,12},{24,0},{28,4},{32,56},... | collective-permute-start | bytes 233480 | tf_op jit(solution)/shard_map/ppermute | solution.py:371
  12.9 0.3 collective-permute-start.4
  13.3 0.3 collective-permute-start.3
  13.6 1.7 %collective-permute-done.5.d = f32[152,128]{1,0:T(8,128)S(1)} collective-permute-done((f32[152,128]{1,0:T(8,128)S(1)}, f32[152,128]{1,0:T(8,128)S(1)}, u32[]{:S(2)}, u32[]{:S(2)}) %collective-permute-start.5) | collective-permute-done | bytes 77856 | tf_op jit(solution)/shard_map/ppermute | solution.py:371
  15.3 3.0 %collective-permute-start.7 = (f32[64,128]{1,0:T(8,128)S(1)}, f32[64,128]{1,0:T(8,128)S(1)}, u32[]{:S(2)}, u32[]{:S(2)}) collective-permute-start(f32[64,128]{1,0:T(8,128)S(1)} %get-tuple-element.34), channel_id=1, source_target_pairs={{4,8},{12,16},{20,24},{28,32},{36,40},{44,48},{52,56},{60,64},{68,... | collective-permute-start | bytes 98312 | tf_op jit(solution)/shard_map/ppermute | solution.py:392
  18.3 0.0 collective-permute-done.4.c
  18.3 0.0 collective-permute-done.3.b
  18.3 0.0 copy-done.3
  18.3 0.0 copy-done.4
  18.3 0.0 copy-done.5
  18.3 0.0 copy-done.6
  18.4 0.0 copy-done.7
  18.4 0.1 shard_map.85
  18.5 1.7 %collective-permute-start.10 = (s32[1,384]{1,0:T(1,128)S(1)}, s32[1,384]{1,0:T(1,128)S(1)}, u32[]{:S(2)}, u32[]{:S(2)}) collective-permute-start(s32[1,384]{1,0:T(1,128)S(1)} %get-tuple-element.42.wanted), channel_id=1, source_target_pairs={{0,4},{4,0},{8,12},{12,8},{16,20},{20,16},{24,28},{28,24},{32,36},... | collective-permute-start | bytes 4616 | tf_op jit(solution)/shard_map/ppermute | solution.py:371
  20.2 2.2 %collective-permute-start.6 = (f32[224,128]{1,0:T(8,128)S(1)}, f32[224,128]{1,0:T(8,128)S(1)}, u32[]{:S(2)}, u32[]{:S(2)}) collective-permute-start(f32[224,128]{1,0:T(8,128)S(1)} %get-tuple-element.33.mine), channel_id=1, source_target_pairs={{4,132},{12,140},{20,148},{28,156},{36,164},{44,172},{52,180},{60,... | collective-permute-start | bytes 344072 | tf_op jit(solution)/shard_map/ppermute | solution.py:411
  22.4 0.0 collective-permute-done.8.two
  22.4 0.0 collective-permute-done.9.three
  22.4 0.1 shard_map.88.columns
  22.5 0.0 collective-permute-done.10._wanted.partner_wanted
  22.5 0.9 %shard_map.89 = (f32[4,32,384]{2,1,0:T(8,128)S(1)}, f32[4,32,384]{2,1,0:T(8,128)S(1)}, f32[4,32,384]{2,1,0:T(8,128)S(1)}, f32[4,32,384]{2,1,0:T(8,128)S(1)}) custom-call(f32[4,128,384]{2,1,0:T(8,128)S(1)} %shard_map.88.columns, s32[4,384]{1,0:T(4,128)S(1)} %get-tuple-element.40.mask, f32[128,128]{1,0:T(8,128)S(1)} %get-tuple-element.41.mixing, ...), custom_call_target="tpu_custom_call" | custom-call | tf_op jit(solution)/shard_map/pallas_call | solution.py:418
  23.4 2.2 %collective-permute-start.11 = (f32[4,32,384]{2,1,0:T(8,128)S(1)}, f32[4,32,384]{2,1,0:T(8,128)S(1)}, u32[]{:S(2)}, u32[]{:S(2)}) collective-permute-start(f32[4,32,384]{2,1,0:T(8,128)S(1)} %get-tuple-element.44), channel_id=1, source_target_pairs={{0,2},{1,3},{2,0},{3,1},{4,6},{5,7},{6,4},{7,5},{8,10},{9,11},{10,... | collective-permute-start | bytes 589832 | tf_op jit(solution)/shard_map/ppermute | solution.py:371
  25.6 1.6 %collective-permute-start.12 = (f32[4,32,384]{2,1,0:T(8,128)S(1)}, f32[4,32,384]{2,1,0:T(8,128)S(1)}, u32[]{:S(2)}, u32[]{:S(2)}) collective-permute-start(f32[4,32,384]{2,1,0:T(8,128)S(1)} %get-tuple-element.45), channel_id=1, source_target_pairs={{0,3},{1,2},{2,1},{3,0},{4,7},{5,6},{6,5},{7,4},{8,11},{9,10},{10,... | collective-permute-start | bytes 589832 | tf_op jit(solution)/shard_map/ppermute | solution.py:371
  27.2 0.0 collective-permute-start.13
  27.2 0.0 collective-permute-done.7.other_row
  27.2 2.7 %collective-permute-done.6.theirs = f32[224,128]{1,0:T(8,128)S(1)} collective-permute-done((f32[224,128]{1,0:T(8,128)S(1)}, f32[224,128]{1,0:T(8,128)S(1)}, u32[]{:S(2)}, u32[]{:S(2)}) %collective-permute-start.6) | collective-permute-done | bytes 114720 | tf_op jit(solution)/shard_map/ppermute | solution.py:411
  29.9 0.7 %shard_map.86 = (f32[224,128]{1,0:T(8,128)S(1)}, f32[2,224,128]{2,1,0:T(8,128)}, f32[128,128]{1,0:T(8,128)S(1)}, f32[128,128]{1,0:T(8,128)S(1)}) custom-call(f32[224,128]{1,0:T(8,128)S(1)} %get-tuple-element.33.mine, f32[224,128]{1,0:T(8,128)S(1)} %collective-permute-done.6.theirs, f32[64,128]{1,0:T(8,128)S(1)} %collective-permute-done.1._row.partner_row, ...), custom_call_target="tpu_custom_call" | custom-call | flops 99999997952 | bytes 100000000 | tf_op jit(solution)/shard_map/pallas_call | solution.py:422
  30.6 9.8 %all-to-all-start = ((f32[2,224,128]{2,1,0:T(8,128)}), f32[2,224,128]{2,1,0:T(8,128)S(1)}, u32[]{:S(2)}, u32[]{:S(2)}) async-start(f32[2,224,128]{2,1,0:T(8,128)} %get-tuple-element.48), calls=%async_computation | async-start | bytes 458752 | tf_op jit(solution)/shard_map/all_to_all | solution.py:430
  40.4 3.5 %collective-permute-start.15 = (f32[224,128]{1,0:T(8,128)S(1)}, f32[224,128]{1,0:T(8,128)S(1)}, u32[]{:S(2)}, u32[]{:S(2)}) collective-permute-start(f32[224,128]{1,0:T(8,128)S(1)} %get-tuple-element.47.own), channel_id=1, source_target_pairs={{0,96},{4,100},{8,104},{12,108},{16,112},{20,116},{24,120},{28,124... | collective-permute-start | bytes 344072 | tf_op jit(solution)/shard_map/ppermute | solution.py:371
  43.9 0.0 collective-permute-start.14
  43.9 0.4 shard_map.87.base
  44.3 1.5 %all-to-all-done.both = f32[2,224,128]{2,1,0:T(8,128)S(1)} async-done(((f32[2,224,128]{2,1,0:T(8,128)}), f32[2,224,128]{2,1,0:T(8,128)S(1)}, u32[]{:S(2)}, u32[]{:S(2)}) %all-to-all-start) | async-done | bytes 229408 | tf_op jit(solution)/shard_map/all_to_all | solution.py:430
  45.9 1.1 %collective-permute-done.15.three = f32[224,128]{1,0:T(8,128)S(1)} collective-permute-done((f32[224,128]{1,0:T(8,128)S(1)}, f32[224,128]{1,0:T(8,128)S(1)}, u32[]{:S(2)}, u32[]{:S(2)}) %collective-permute-start.15) | collective-permute-done | bytes 114720 | tf_op jit(solution)/shard_map/ppermute | solution.py:371
  47.0 0.6 %collective-permute-done.14.one = f32[224,128]{1,0:T(8,128)S(1)} collective-permute-done((f32[224,128]{1,0:T(8,128)S(1)}, f32[224,128]{1,0:T(8,128)S(1)}, u32[]{:S(2)}, u32[]{:S(2)}) %collective-permute-start.14) | collective-permute-done | bytes 114720 | tf_op jit(solution)/shard_map/ppermute | solution.py:371
  47.6 0.8 %shard_map.91 = (f32[128,384]{1,0:T(8,128)S(1)}, f32[128,384]{1,0:T(8,128)S(1)}) custom-call(f32[224,128]{1,0:T(8,128)S(1)} %get-tuple-element.47.own, f32[224,128]{1,0:T(8,128)S(1)} %collective-permute-done.14.one, f32[2,224,128]{2,1,0:T(8,128)S(1)} %all-to-all-done.both, f32[224,128]{1,0:T(8,128)S(1)} %collective-permute-done.15.three, ...), custom_call_target="tpu_custom_call" | custom-call | tf_op jit(solution)/shard_map/pallas_call | solution.py:433
  48.4 0.1 collective-permute-start.16
  48.5 0.0 collective-permute-done.11.two
  48.5 0.0 collective-permute-done.12.three
  48.5 0.0 collective-permute-done.13.one
  48.5 1.0 %shard_map.90.changed = f32[16,32,384]{2,1,0:T(8,128)S(1)} custom-call(f32[16,32,384]{2,1,0:T(8,128)S(1)} %shard_map.87.base, f32[4,32,384]{2,1,0:T(8,128)S(1)} %get-tuple-element.43.own, f32[4,32,384]{2,1,0:T(8,128)S(1)} %collective-permute-done.11.two, f32[4,32,384]{2,1,0:T(8,128)S(1)} %collective-permute-done.12.three, ...), custom_call_target="tpu_custom_call" | custom-call | flops 99999997952 | bytes 100000000 | tf_op jit(solution)/shard_map/pallas_call | solution.py:432
  49.6 0.4 collective-permute-done.16.theirs
  49.9 1.1 %shard_map.92 = f32[512,384]{1,0:T(8,128)} custom-call(f32[16,32,384]{2,1,0:T(8,128)S(1)} %get-tuple-element.29.stepped, f32[16,32,384]{2,1,0:T(8,128)S(1)} %shard_map.90.changed, f32[128,384]{1,0:T(8,128)S(1)} %get-tuple-element.49.mine, f32[128,384]{1,0:T(8,128)S(1)} %collective-permute-done.16.theirs, s32[4,384]{1,0:T(4,128)S(1)} %get-tuple-element.37.turns), custom_call_target="tpu_custom_call" | custom-call | tf_op jit(solution)/shard_map/pallas_call | solution.py:436
  (1 shorter events, 0.0 us)
Async XLA Ops:
  0.0 1.1 %copy-start = (f32[32,16,384]{2,1,0:T(8,128)S(1)}, f32[32,16,384]{2,1,0:T(8,128)}, u32[]{:S(2)}) copy-start(f32[32,16,384]{2,1,0:T(8,128)} %param.8) | copy-start | bytes 2359300
  1.1 3.2 %copy-start.1 = (f32[32,16,384]{2,1,0:T(8,128)S(1)}, f32[32,16,384]{2,1,0:T(8,128)}, u32[]{:S(2)}) copy-start(f32[32,16,384]{2,1,0:T(8,128)} %param.9) | copy-start | bytes 2359300
  1.6 8.4 %collective-permute-start.2 = (f32[4,32,384]{2,1,0:T(8,128)S(1)}, f32[4,32,384]{2,1,0:T(8,128)S(1)}, u32[]{:S(2)}, u32[]{:S(2)}) collective-permute-start(f32[4,32,384]{2,1,0:T(8,128)S(1)} %get-tuple-element.32), channel_id=1, source_target_pairs={{0,1},{1,0},{2,3},{3,2},{4,5},{5,4},{6,7},{7,6},{8,9},{9,8},{10,11... | collective-permute-start | bytes 589832 | tf_op jit(solution)/shard_map/ppermute | solution.py:371
  2.4 20.0 %collective-permute-start.8 = (f32[4,32,384]{2,1,0:T(8,128)S(1)}, f32[4,32,384]{2,1,0:T(8,128)S(1)}, u32[]{:S(2)}, u32[]{:S(2)}) collective-permute-start(f32[4,32,384]{2,1,0:T(8,128)S(1)} %get-tuple-element.38), channel_id=1, source_target_pairs={{0,2},{1,3},{2,0},{3,1},{4,6},{5,7},{6,4},{7,5},{8,10},{9,11},{10,... | collective-permute-start | bytes 589832 | tf_op jit(solution)/shard_map/ppermute | solution.py:371
  3.6 18.8 %collective-permute-start.9 = (f32[4,32,384]{2,1,0:T(8,128)S(1)}, f32[4,32,384]{2,1,0:T(8,128)S(1)}, u32[]{:S(2)}, u32[]{:S(2)}) collective-permute-start(f32[4,32,384]{2,1,0:T(8,128)S(1)} %get-tuple-element.39), channel_id=1, source_target_pairs={{0,3},{1,2},{2,1},{3,0},{4,7},{5,6},{6,5},{7,4},{8,11},{9,10},{10,... | collective-permute-start | bytes 589832 | tf_op jit(solution)/shard_map/ppermute | solution.py:371
  4.3 1.1 %copy-start.2 = (f32[32,16,384]{2,1,0:T(8,128)S(1)}, f32[32,16,384]{2,1,0:T(8,128)}, u32[]{:S(2)}) copy-start(f32[32,16,384]{2,1,0:T(8,128)} %param.10) | copy-start | bytes 2359300
  7.2 2.8 %collective-permute-start = (f32[144,128]{1,0:T(8,128)S(1)}, f32[144,128]{1,0:T(8,128)S(1)}, u32[]{:S(2)}, u32[]{:S(2)}) collective-permute-start(f32[144,128]{1,0:T(8,128)S(1)} %get-tuple-element.30.a), channel_id=1, source_target_pairs={{0,4},{4,0},{8,12},{12,8},{16,20},{20,16},{24,28},{28,24},{32,36},... | collective-permute-start | bytes 221192 | tf_op jit(solution)/shard_map/ppermute | solution.py:371
  8.8 9.5 %copy-start.3 = (f32[128,128]{1,0:T(8,128)S(1)}, f32[128,128]{1,0:T(8,128)}, u32[]{:S(2)}) copy-start(f32[128,128]{1,0:T(8,128)} %mixing.1) | copy-start | bytes 196612
  8.8 1.2 %collective-permute-start.1 = (f32[64,128]{1,0:T(8,128)S(1)}, f32[64,128]{1,0:T(8,128)S(1)}, u32[]{:S(2)}, u32[]{:S(2)}) collective-permute-start(f32[64,128]{1,0:T(8,128)S(1)} %get-tuple-element.31), channel_id=1, source_target_pairs={{0,4},{4,0},{8,12},{12,8},{16,20},{20,16},{24,28},{28,24},{32,36},... | collective-permute-start | bytes 98312 | tf_op jit(solution)/shard_map/ppermute | solution.py:371
  10.0 8.3 %copy-start.4 = (s32[4,384]{1,0:T(4,128)S(1)}, s32[4,384]{1,0:T(4,128)}, u32[]{:S(2)}) copy-start(s32[4,384]{1,0:T(4,128)} %near.1) | copy-start | bytes 18436
  10.0 8.3 %copy-start.5 = (s32[4,384]{1,0:T(4,128)S(1)}, s32[4,384]{1,0:T(4,128)}, u32[]{:S(2)}) copy-start(s32[4,384]{1,0:T(4,128)} %edge_of.1) | copy-start | bytes 18436
  10.0 8.3 %copy-start.6 = (s32[4,384]{1,0:T(4,128)S(1)}, s32[4,384]{1,0:T(4,128)}, u32[]{:S(2)}) copy-start(s32[4,384]{1,0:T(4,128)} %turns.1) | copy-start | bytes 18436
  10.0 8.3 %copy-start.7 = (s32[4,384]{1,0:T(4,128)S(1)}, s32[4,384]{1,0:T(4,128)}, u32[]{:S(2)}) copy-start(s32[4,384]{1,0:T(4,128)} %mask.1) | copy-start | bytes 18436
  10.1 5.2 %collective-permute-start.5 = (f32[152,128]{1,0:T(8,128)S(1)}, f32[152,128]{1,0:T(8,128)S(1)}, u32[]{:S(2)}, u32[]{:S(2)}) collective-permute-start(f32[152,128]{1,0:T(8,128)S(1)} %shard_map.84.a), channel_id=1, source_target_pairs={{0,24},{4,28},{8,16},{12,20},{16,8},{20,12},{24,0},{28,4},{32,56},... | collective-permute-start | bytes 233480 | tf_op jit(solution)/shard_map/ppermute | solution.py:371
  12.9 5.4 %collective-permute-start.4 = (f32[152,128]{1,0:T(8,128)S(1)}, f32[152,128]{1,0:T(8,128)S(1)}, u32[]{:S(2)}, u32[]{:S(2)}) collective-permute-start(f32[152,128]{1,0:T(8,128)S(1)} %shard_map.84.a), channel_id=1, source_target_pairs={{0,16},{4,20},{8,24},{12,28},{16,0},{20,4},{24,8},{28,12},{32,48},... | collective-permute-start | bytes 233480 | tf_op jit(solution)/shard_map/ppermute | solution.py:371
  13.3 5.0 %collective-permute-start.3 = (f32[152,128]{1,0:T(8,128)S(1)}, f32[152,128]{1,0:T(8,128)S(1)}, u32[]{:S(2)}, u32[]{:S(2)}) collective-permute-start(f32[152,128]{1,0:T(8,128)S(1)} %shard_map.84.a), channel_id=1, source_target_pairs={{0,8},{4,12},{8,0},{12,4},{16,24},{20,28},{24,16},{28,20},{32,40},... | collective-permute-start | bytes 233480 | tf_op jit(solution)/shard_map/ppermute | solution.py:371
  15.3 11.9 %collective-permute-start.7 = (f32[64,128]{1,0:T(8,128)S(1)}, f32[64,128]{1,0:T(8,128)S(1)}, u32[]{:S(2)}, u32[]{:S(2)}) collective-permute-start(f32[64,128]{1,0:T(8,128)S(1)} %get-tuple-element.34), channel_id=1, source_target_pairs={{4,8},{12,16},{20,24},{28,32},{36,40},{44,48},{52,56},{60,64},{68,... | collective-permute-start | bytes 98312 | tf_op jit(solution)/shard_map/ppermute | solution.py:392
  18.5 4.0 %collective-permute-start.10 = (s32[1,384]{1,0:T(1,128)S(1)}, s32[1,384]{1,0:T(1,128)S(1)}, u32[]{:S(2)}, u32[]{:S(2)}) collective-permute-start(s32[1,384]{1,0:T(1,128)S(1)} %get-tuple-element.42.wanted), channel_id=1, source_target_pairs={{0,4},{4,0},{8,12},{12,8},{16,20},{20,16},{24,28},{28,24},{32,36},... | collective-permute-start | bytes 4616 | tf_op jit(solution)/shard_map/ppermute | solution.py:371
  20.2 9.7 %collective-permute-start.6 = (f32[224,128]{1,0:T(8,128)S(1)}, f32[224,128]{1,0:T(8,128)S(1)}, u32[]{:S(2)}, u32[]{:S(2)}) collective-permute-start(f32[224,128]{1,0:T(8,128)S(1)} %get-tuple-element.33.mine), channel_id=1, source_target_pairs={{4,132},{12,140},{20,148},{28,156},{36,164},{44,172},{52,180},{60,... | collective-permute-start | bytes 344072 | tf_op jit(solution)/shard_map/ppermute | solution.py:411
  23.4 25.1 %collective-permute-start.11 = (f32[4,32,384]{2,1,0:T(8,128)S(1)}, f32[4,32,384]{2,1,0:T(8,128)S(1)}, u32[]{:S(2)}, u32[]{:S(2)}) collective-permute-start(f32[4,32,384]{2,1,0:T(8,128)S(1)} %get-tuple-element.44), channel_id=1, source_target_pairs={{0,2},{1,3},{2,0},{3,1},{4,6},{5,7},{6,4},{7,5},{8,10},{9,11},{10,... | collective-permute-start | bytes 589832 | tf_op jit(solution)/shard_map/ppermute | solution.py:371
  25.6 22.9 %collective-permute-start.12 = (f32[4,32,384]{2,1,0:T(8,128)S(1)}, f32[4,32,384]{2,1,0:T(8,128)S(1)}, u32[]{:S(2)}, u32[]{:S(2)}) collective-permute-start(f32[4,32,384]{2,1,0:T(8,128)S(1)} %get-tuple-element.45), channel_id=1, source_target_pairs={{0,3},{1,2},{2,1},{3,0},{4,7},{5,6},{6,5},{7,4},{8,11},{9,10},{10,... | collective-permute-start | bytes 589832 | tf_op jit(solution)/shard_map/ppermute | solution.py:371
  27.2 21.3 %collective-permute-start.13 = (f32[4,32,384]{2,1,0:T(8,128)S(1)}, f32[4,32,384]{2,1,0:T(8,128)}, u32[]{:S(2)}, u32[]{:S(2)}) collective-permute-start(f32[4,32,384]{2,1,0:T(8,128)S(1)} %get-tuple-element.46), channel_id=1, source_target_pairs={{0,1},{1,0},{2,3},{3,2},{4,5},{5,4},{6,7},{7,6},{8,9},{9,8},{10,11... | collective-permute-start | bytes 589832 | tf_op jit(solution)/shard_map/ppermute | solution.py:371
  30.6 15.2 %all-to-all-start = ((f32[2,224,128]{2,1,0:T(8,128)}), f32[2,224,128]{2,1,0:T(8,128)S(1)}, u32[]{:S(2)}, u32[]{:S(2)}) async-start(f32[2,224,128]{2,1,0:T(8,128)} %get-tuple-element.48), calls=%async_computation | async-start | bytes 458752 | tf_op jit(solution)/shard_map/all_to_all | solution.py:430
  40.4 6.6 %collective-permute-start.15 = (f32[224,128]{1,0:T(8,128)S(1)}, f32[224,128]{1,0:T(8,128)S(1)}, u32[]{:S(2)}, u32[]{:S(2)}) collective-permute-start(f32[224,128]{1,0:T(8,128)S(1)} %get-tuple-element.47.own), channel_id=1, source_target_pairs={{0,96},{4,100},{8,104},{12,108},{16,112},{20,116},{24,120},{28,124... | collective-permute-start | bytes 344072 | tf_op jit(solution)/shard_map/ppermute | solution.py:371
  43.9 3.6 %collective-permute-start.14 = (f32[224,128]{1,0:T(8,128)S(1)}, f32[224,128]{1,0:T(8,128)S(1)}, u32[]{:S(2)}, u32[]{:S(2)}) collective-permute-start(f32[224,128]{1,0:T(8,128)S(1)} %get-tuple-element.47.own), channel_id=1, source_target_pairs={{0,32},{4,36},{8,40},{12,44},{16,48},{20,52},{24,56},{28,60},{32,0... | collective-permute-start | bytes 344072 | tf_op jit(solution)/shard_map/ppermute | solution.py:371
  48.4 1.5 %collective-permute-start.16 = (f32[128,384]{1,0:T(8,128)S(1)}, f32[128,384]{1,0:T(8,128)S(1)}, u32[]{:S(2)}, u32[]{:S(2)}) collective-permute-start(f32[128,384]{1,0:T(8,128)S(1)} %get-tuple-element.50), channel_id=1, source_target_pairs={{0,4},{4,0},{8,12},{12,8},{16,20},{20,16},{24,28},{28,24},{32,36},... | collective-permute-start | bytes 589832 | tf_op jit(solution)/shard_map/ppermute | solution.py:371

commit v6 on v5

--- a/solution.py
+++ b/solution.py
@@ -110,7 +110,6 @@
     _sent,
     stepped,
     contrib,
-    to_partner,
     to_other,
 ):
     step = pl.program_id(0)
@@ -128,10 +127,10 @@
 
     @pl.when(step == 2)
     def _():
-        take_edges(stepped, contrib, to_partner, to_other)
-
-
-def take_edges(stepped, contrib, to_partner, to_other):
+        take_edges(stepped, contrib, to_other)
+
+
+def take_edges(stepped, contrib, to_other):
     edge = [
         stepped[0:4].reshape(128, E),
         jnp.concatenate([stepped[4 * t + 3] for t in range(4)], axis=0),
@@ -143,7 +142,7 @@
     last = jnp.where(low, pltpu.roll(last[:64], NE, 1), last[64:])
     first = jnp.where(low, first[:64], pltpu.roll(first[64:], NE, 1))
     even = lax.axis_index("curve") % 2 == 0
-    to_partner[...] = jnp.where(even, last, first)
+    contrib[CONTRIB:] = jnp.where(even, last, first)
     to_other[...] = jnp.where(even, first, last)
     row0, row63 = rim_rows()
     r = lax.broadcasted_iota(jnp.int32, (8, E), 0)
@@ -160,7 +159,7 @@
     contrib[140:CONTRIB] = jnp.zeros((CONTRIB - 140, 128), jnp.float32)
 
 
-def pair_kernel(a, b, _row, _one, out):
+def pair_kernel(a, b, _one, out):
     even = lax.axis_index("curve") % 2 == 0
     out[0:12] = jnp.where(even, a[0:12], b[0:12])
     out[12:24] = jnp.where(even, b[0:12], a[0:12])
@@ -184,7 +183,7 @@
     for k in range(2):
         both[k] = half
     even = lax.axis_index("curve") % 2 == 0
-    partner, other = partner_row[...], other_row[...]
+    partner, other = partner_row[CONTRIB:], other_row[...]
     last = jnp.where(even, other, partner)
     first = jnp.where(even, partner, other)
     before[:64] = pltpu.roll(last, NE, 1)
@@ -262,10 +261,9 @@
 
 def change_kernel(base, own, two, three, one, out):
     me = lax.axis_index("lev")
-    for k, part in enumerate((own, one, two, three)):
-        for p in range(4):
-            at = 4 * (me ^ k) + p
-            out[at] = base[at] + part[p]
+    for k, part in ((0, own), (2, two), (3, three), (1, one)):
+        rows = pl.ds(4 * (me ^ k), 4)
+        out[rows] = base[rows] + part[...]
 
 
 POINT = [[0, 1, 2, 3], [3, 7, 11, 15], [12, 13, 14, 15], [0, 4, 8, 12]]
@@ -372,16 +370,15 @@
 
     sends = lane_call(split_kernel, (part,) * 4, [flat_block], (part_block,) * 4)(flat)
     cells = [swap(sends[k], "lev", k) for k in (1, 2, 3)]
-    stepped, contrib, to_partner, to_other = lane_call(
+    stepped, contrib, to_other = lane_call(
         step_kernel,
         (
             f32((16, 32, E)),
-            f32((CONTRIB, 128)),
-            f32((64, 128)),
+            f32((CONTRIB + 64, 128)),
             f32((64, 128)),
         ),
         [flat_block] * 3 + [whole(4, 32, E)],
-        (whole(16, 32, E), whole(CONTRIB, 128), whole(64, 128), whole(64, 128)),
+        (whole(16, 32, E), whole(CONTRIB + 64, 128), whole(64, 128)),
     )(
         flat,
         wind_x.reshape(512, E),
@@ -390,9 +387,9 @@
     )
     inner = [(i, i + 1) for i in range(1, 62, 2) if i != 31]
     other_row = lax.ppermute(to_other, "curve", inner + [(j, i) for i, j in inner])
-    partner_row = swap(to_partner, "curve", 1)
-    paired = call(pair_kernel, f32((PAIRED, 128)), 4)(
-        contrib, swap(contrib, "curve", 1), partner_row, cells[0]
+    partner = swap(contrib, "curve", 1)
+    paired = call(pair_kernel, f32((PAIRED, 128)), 3)(
+        contrib, partner, cells[0]
     )
     along_y = [swap(paired, "curve", k << 1) for k in (1, 2, 3)]
     table = jax.ShapeDtypeStruct((4, E), jnp.int32)
@@ -424,7 +421,7 @@
         (f32((MERGED, 128)), f32((2, MERGED, 128)), f32((128, 128)), f32((128, 128))),
         4,
         cost=long,
-    )(merged, other_half, partner_row, other_row)
+    )(merged, other_half, partner, other_row)
     along_x = [swap(piece, "curve", k << 3) for k in (1, 3)]
     groups = [[i, i ^ 16] for i in range(64) if not i & 16]
     across_x = lax.all_to_all(twice, "curve", 0, 0, axis_index_groups=groups, tiled=True)

time: 51.3 us -> 50.2 us (0.979)
  the two profiles are of different devices: /device:TPU:193 before, /device:TPU:1 now
where the time goes in v6:
time: 50.2 us; the launch traced here: 49.9 us
  starting transfers between devices  33.9 us (68%)
  Pallas kernels  7.38 us (15%)
  waiting for transfers between devices  6.08 us (12%)
  local copies, waits for them, and re-layouts  2.29 us (5%)
    ppermute x14, starting transfers between devices, swap(): return lax.ppermute(array, axis, [(i, i ^ bits) for i in range(devices)])  18.4 us
    ppermute x1, starting transfers between devices, on_device(): lax.ppermute(merged, 'curve', [(i, i ^ 32) for i in range(1, 64, 2)])  8.35 us
    all_to_all x1, starting transfers between devices, on_device(): lax.all_to_all(twice, 'curve', 0, 0, axis_index_groups=groups, tiled=True)  4.24 us
    ppermute x14, waiting for transfers between devices, swap(): return lax.ppermute(array, axis, [(i, i ^ bits) for i in range(devices)])  4.06 us
    ppermute x1, starting transfers between devices, on_device(): lax.ppermute(to_other, 'curve', inner + [(j, i) for i, j in inner])  2.92 us
    unnamed x16, local copies, waits for them, and re-layouts  2.29 us
    all_to_all x1, waiting for transfers between devices, on_device(): lax.all_to_all(twice, 'curve', 0, 0, axis_index_groups=groups, tiled=True)  2.02 us
    pallas_call x1, Pallas kernels, on_device(): lane_call(step_kernel, (f32((16, 32, E)), f32((CONTRIB + 64, 128)), f32((...  1.73 us
  transfers between devices with their start and end apart: 17, of which 6 were waited for; matrix products, arithmetic and copies ran while one was open for 0% of the time, Pallas kernels for 12%

profile of v6, /device:TPU:1, one launch (start us, length us, event | category | flops | bytes accessed | tf_op | source)
XLA Modules:
  0.0 49.9 jit_solution(9597301590508498526)
XLA Ops:
  0.0 0.0 copy-start
  0.0 1.1 %copy-done = f32[32,16,384]{2,1,0:T(8,128)S(1)} copy-done((f32[32,16,384]{2,1,0:T(8,128)S(1)}, f32[32,16,384]{2,1,0:T(8,128)}, u32[]{:S(2)}) %copy-start) | copy-done | bytes 786456
  1.1 0.0 copy-start.1
  1.1 0.4 shard_map.82
  1.6 2.6 %collective-permute-start.1 = (f32[4,32,384]{2,1,0:T(8,128)S(1)}, f32[4,32,384]{2,1,0:T(8,128)S(1)}, u32[]{:S(2)}, u32[]{:S(2)}) collective-permute-start(f32[4,32,384]{2,1,0:T(8,128)S(1)} %get-tuple-element.30), channel_id=1, source_target_pairs={{0,1},{1,0},{2,3},{3,2},{4,5},{5,4},{6,7},{7,6},{8,9},{9,8},{10,11... | collective-permute-start | bytes 589832 | tf_op jit(solution)/shard_map/ppermute | solution.py:369
  4.1 3.0 %collective-permute-start.7 = (f32[4,32,384]{2,1,0:T(8,128)S(1)}, f32[4,32,384]{2,1,0:T(8,128)S(1)}, u32[]{:S(2)}, u32[]{:S(2)}) collective-permute-start(f32[4,32,384]{2,1,0:T(8,128)S(1)} %get-tuple-element.36), channel_id=1, source_target_pairs={{0,2},{1,3},{2,0},{3,1},{4,6},{5,7},{6,4},{7,5},{8,10},{9,11},{10,... | collective-permute-start | bytes 589832 | tf_op jit(solution)/shard_map/ppermute | solution.py:369
  7.1 0.0 collective-permute-start.8
  7.1 0.0 copy-done.1
  7.1 0.0 copy-start.2
  7.1 1.1 %copy-done.2 = f32[32,16,384]{2,1,0:T(8,128)S(1)} copy-done((f32[32,16,384]{2,1,0:T(8,128)S(1)}, f32[32,16,384]{2,1,0:T(8,128)}, u32[]{:S(2)}) %copy-start.2) | copy-done | bytes 786456
  8.3 1.7 %shard_map.83 = (f32[16,32,384]{2,1,0:T(8,128)S(1)}, f32[208,128]{1,0:T(8,128)S(1)}, f32[64,128]{1,0:T(8,128)S(1)}) custom-call(f32[512,384]{1,0:T(8,128)S(1)} %bitcast.5, f32[512,384]{1,0:T(8,128)S(1)} %bitcast.6, f32[512,384]{1,0:T(8,128)S(1)} %bitcast.7, f32[4,32,384]{2,1,0:T(8,128)S(1)} %get-tuple-element.27._sent.own), custom_call_target="tpu_custom_call" | custom-call | tf_op jit(solution)/shard_map/pallas_call | solution.py:373
  10.0 0.0 copy-start.3
  10.0 2.3 %collective-permute-start = (f32[208,128]{1,0:T(8,128)S(1)}, f32[208,128]{1,0:T(8,128)S(1)}, u32[]{:S(2)}, u32[]{:S(2)}) collective-permute-start(f32[208,128]{1,0:T(8,128)S(1)} %get-tuple-element.29.a), channel_id=1, source_target_pairs={{0,4},{4,0},{8,12},{12,8},{16,20},{20,16},{24,28},{28,24},{32,36},... | collective-permute-start | bytes 319496 | tf_op jit(solution)/shard_map/ppermute | solution.py:369
  12.3 1.0 %collective-permute-done.b.partner_row = f32[208,128]{1,0:T(8,128)S(1)} collective-permute-done((f32[208,128]{1,0:T(8,128)S(1)}, f32[208,128]{1,0:T(8,128)S(1)}, u32[]{:S(2)}, u32[]{:S(2)}) %collective-permute-start) | collective-permute-done | bytes 106528 | tf_op jit(solution)/shard_map/ppermute | solution.py:369
  13.2 0.0 collective-permute-done.1._one.one
  13.2 0.0 copy-start.4
  13.2 0.0 copy-start.5
  13.2 0.0 copy-start.6
  13.2 0.0 copy-start.7
  13.3 1.9 %collective-permute-start.4 = (f32[152,128]{1,0:T(8,128)S(1)}, f32[152,128]{1,0:T(8,128)S(1)}, u32[]{:S(2)}, u32[]{:S(2)}) collective-permute-start(f32[152,128]{1,0:T(8,128)S(1)} %shard_map.84.a), channel_id=1, source_target_pairs={{0,24},{4,28},{8,16},{12,20},{16,8},{20,12},{24,0},{28,4},{32,56},... | collective-permute-start | bytes 233480 | tf_op jit(solution)/shard_map/ppermute | solution.py:369
  15.2 0.3 collective-permute-start.3
  15.5 1.1 %collective-permute-start.2 = (f32[152,128]{1,0:T(8,128)S(1)}, f32[152,128]{1,0:T(8,128)S(1)}, u32[]{:S(2)}, u32[]{:S(2)}) collective-permute-start(f32[152,128]{1,0:T(8,128)S(1)} %shard_map.84.a), channel_id=1, source_target_pairs={{0,8},{4,12},{8,0},{12,4},{16,24},{20,28},{24,16},{28,20},{32,40},... | collective-permute-start | bytes 233480 | tf_op jit(solution)/shard_map/ppermute | solution.py:369
  16.6 1.5 %collective-permute-done.4.d = f32[152,128]{1,0:T(8,128)S(1)} collective-permute-done((f32[152,128]{1,0:T(8,128)S(1)}, f32[152,128]{1,0:T(8,128)S(1)}, u32[]{:S(2)}, u32[]{:S(2)}) %collective-permute-start.4) | collective-permute-done | bytes 77856 | tf_op jit(solution)/shard_map/ppermute | solution.py:369
  18.1 2.9 %collective-permute-start.6 = (f32[64,128]{1,0:T(8,128)S(1)}, f32[64,128]{1,0:T(8,128)S(1)}, u32[]{:S(2)}, u32[]{:S(2)}) collective-permute-start(f32[64,128]{1,0:T(8,128)S(1)} %get-tuple-element.32), channel_id=1, source_target_pairs={{4,8},{12,16},{20,24},{28,32},{36,40},{44,48},{52,56},{60,64},{68,... | collective-permute-start | bytes 98312 | tf_op jit(solution)/shard_map/ppermute | solution.py:389
  21.1 0.0 collective-permute-done.3.c
  21.1 0.0 collective-permute-done.2.b
  21.1 0.0 copy-done.3
  21.1 0.0 copy-done.4
  21.1 0.0 copy-done.5
  21.1 0.0 copy-done.6
  21.1 0.0 copy-done.7
  21.1 0.1 shard_map.85
  21.3 1.4 %collective-permute-start.9 = (s32[1,384]{1,0:T(1,128)S(1)}, s32[1,384]{1,0:T(1,128)S(1)}, u32[]{:S(2)}, u32[]{:S(2)}) collective-permute-start(s32[1,384]{1,0:T(1,128)S(1)} %get-tuple-element.40.wanted), channel_id=1, source_target_pairs={{0,4},{4,0},{8,12},{12,8},{16,20},{20,16},{24,28},{28,24},{32,36},... | collective-permute-start | bytes 4616 | tf_op jit(solution)/shard_map/ppermute | solution.py:369
  22.7 8.3 %collective-permute-start.5 = (f32[224,128]{1,0:T(8,128)S(1)}, f32[224,128]{1,0:T(8,128)S(1)}, u32[]{:S(2)}, u32[]{:S(2)}) collective-permute-start(f32[224,128]{1,0:T(8,128)S(1)} %get-tuple-element.31.mine), channel_id=1, source_target_pairs={{4,132},{12,140},{20,148},{28,156},{36,164},{44,172},{52,180},{60,... | collective-permute-start | bytes 344072 | tf_op jit(solution)/shard_map/ppermute | solution.py:408
  31.1 0.0 collective-permute-done.7.two
  31.1 0.0 collective-permute-done.8.three
  31.1 0.1 shard_map.88.columns
  31.2 0.0 collective-permute-done.9._wanted.partner_wanted
  31.2 0.9 %shard_map.89 = (f32[4,32,384]{2,1,0:T(8,128)S(1)}, f32[4,32,384]{2,1,0:T(8,128)S(1)}, f32[4,32,384]{2,1,0:T(8,128)S(1)}, f32[4,32,384]{2,1,0:T(8,128)S(1)}) custom-call(f32[4,128,384]{2,1,0:T(8,128)S(1)} %shard_map.88.columns, s32[4,384]{1,0:T(4,128)S(1)} %get-tuple-element.38.mask, f32[128,128]{1,0:T(8,128)S(1)} %get-tuple-element.39.mixing, ...), custom_call_target="tpu_custom_call" | custom-call | tf_op jit(solution)/shard_map/pallas_call | solution.py:415
  32.1 0.1 collective-permute-start.10
  32.2 1.7 %collective-permute-start.11 = (f32[4,32,384]{2,1,0:T(8,128)S(1)}, f32[4,32,384]{2,1,0:T(8,128)S(1)}, u32[]{:S(2)}, u32[]{:S(2)}) collective-permute-start(f32[4,32,384]{2,1,0:T(8,128)S(1)} %get-tuple-element.43), channel_id=1, source_target_pairs={{0,3},{1,2},{2,1},{3,0},{4,7},{5,6},{6,5},{7,4},{8,11},{9,10},{10,... | collective-permute-start | bytes 589832 | tf_op jit(solution)/shard_map/ppermute | solution.py:369
  33.9 0.9 %collective-permute-start.12 = (f32[4,32,384]{2,1,0:T(8,128)S(1)}, f32[4,32,384]{2,1,0:T(8,128)}, u32[]{:S(2)}, u32[]{:S(2)}) collective-permute-start(f32[4,32,384]{2,1,0:T(8,128)S(1)} %get-tuple-element.44), channel_id=1, source_target_pairs={{0,1},{1,0},{2,3},{3,2},{4,5},{5,4},{6,7},{7,6},{8,9},{9,8},{10,11... | collective-permute-start | bytes 589832 | tf_op jit(solution)/shard_map/ppermute | solution.py:369
  34.8 0.0 collective-permute-done.6.other_row
  34.8 0.0 collective-permute-done.5.theirs
  34.8 0.7 %shard_map.86 = (f32[224,128]{1,0:T(8,128)S(1)}, f32[2,224,128]{2,1,0:T(8,128)}, f32[128,128]{1,0:T(8,128)S(1)}, f32[128,128]{1,0:T(8,128)S(1)}) custom-call(f32[224,128]{1,0:T(8,128)S(1)} %get-tuple-element.31.mine, f32[224,128]{1,0:T(8,128)S(1)} %collective-permute-done.5.theirs, f32[208,128]{1,0:T(8,128)S(1)} %collective-permute-done.b.partner_row, ...), custom_call_target="tpu_custom_call" | custom-call | flops 99999997952 | bytes 100000000 | tf_op jit(solution)/shard_map/pallas_call | solution.py:419
  35.5 4.2 %all-to-all-start = ((f32[2,224,128]{2,1,0:T(8,128)}), f32[2,224,128]{2,1,0:T(8,128)S(1)}, u32[]{:S(2)}, u32[]{:S(2)}) async-start(f32[2,224,128]{2,1,0:T(8,128)} %get-tuple-element.46), calls=%async_computation | async-start | bytes 458752 | tf_op jit(solution)/shard_map/all_to_all | solution.py:427
  39.8 3.0 %collective-permute-start.14 = (f32[224,128]{1,0:T(8,128)S(1)}, f32[224,128]{1,0:T(8,128)S(1)}, u32[]{:S(2)}, u32[]{:S(2)}) collective-permute-start(f32[224,128]{1,0:T(8,128)S(1)} %get-tuple-element.45.own), channel_id=1, source_target_pairs={{0,96},{4,100},{8,104},{12,108},{16,112},{20,116},{24,120},{28,124... | collective-permute-start | bytes 344072 | tf_op jit(solution)/shard_map/ppermute | solution.py:369
  42.8 0.0 collective-permute-start.13
  42.8 0.4 shard_map.87.base
  43.2 2.0 %all-to-all-done.both = f32[2,224,128]{2,1,0:T(8,128)S(1)} async-done(((f32[2,224,128]{2,1,0:T(8,128)}), f32[2,224,128]{2,1,0:T(8,128)S(1)}, u32[]{:S(2)}, u32[]{:S(2)}) %all-to-all-start) | async-done | bytes 229408 | tf_op jit(solution)/shard_map/all_to_all | solution.py:427
  45.2 1.0 %collective-permute-done.14.three = f32[224,128]{1,0:T(8,128)S(1)} collective-permute-done((f32[224,128]{1,0:T(8,128)S(1)}, f32[224,128]{1,0:T(8,128)S(1)}, u32[]{:S(2)}, u32[]{:S(2)}) %collective-permute-start.14) | collective-permute-done | bytes 114720 | tf_op jit(solution)/shard_map/ppermute | solution.py:369
  46.2 0.2 collective-permute-done.13.one
  46.4 0.8 %shard_map.91 = (f32[128,384]{1,0:T(8,128)S(1)}, f32[128,384]{1,0:T(8,128)S(1)}) custom-call(f32[224,128]{1,0:T(8,128)S(1)} %get-tuple-element.45.own, f32[224,128]{1,0:T(8,128)S(1)} %collective-permute-done.13.one, f32[2,224,128]{2,1,0:T(8,128)S(1)} %all-to-all-done.both, f32[224,128]{1,0:T(8,128)S(1)} %collective-permute-done.14.three, ...), custom_call_target="tpu_custom_call" | custom-call | tf_op jit(solution)/shard_map/pallas_call | solution.py:430
  47.3 0.1 collective-permute-start.15
  47.4 0.0 collective-permute-done.10.two
  47.4 0.0 collective-permute-done.11.three
  47.4 0.0 collective-permute-done.12.one
  47.4 1.0 %shard_map.90.changed = f32[16,32,384]{2,1,0:T(8,128)S(1)} custom-call(f32[16,32,384]{2,1,0:T(8,128)S(1)} %shard_map.87.base, f32[4,32,384]{2,1,0:T(8,128)S(1)} %get-tuple-element.41.own, f32[4,32,384]{2,1,0:T(8,128)S(1)} %collective-permute-done.10.two, f32[4,32,384]{2,1,0:T(8,128)S(1)} %collective-permute-done.11.three, ...), custom_call_target="tpu_custom_call" | custom-call | flops 99999997952 | bytes 100000000 | tf_op jit(solution)/shard_map/pallas_call | solution.py:429
  48.4 0.4 collective-permute-done.15.theirs
  48.8 1.1 %shard_map.92 = f32[512,384]{1,0:T(8,128)} custom-call(f32[16,32,384]{2,1,0:T(8,128)S(1)} %get-tuple-element.28.stepped, f32[16,32,384]{2,1,0:T(8,128)S(1)} %shard_map.90.changed, f32[128,384]{1,0:T(8,128)S(1)} %get-tuple-element.47.mine, f32[128,384]{1,0:T(8,128)S(1)} %collective-permute-done.15.theirs, s32[4,384]{1,0:T(4,128)S(1)} %get-tuple-element.35.turns), custom_call_target="tpu_custom_call" | custom-call | tf_op jit(solution)/shard_map/pallas_call | solution.py:433
  (1 shorter events, 0.0 us)
Async XLA Ops:
  0.0 1.1 %copy-start = (f32[32,16,384]{2,1,0:T(8,128)S(1)}, f32[32,16,384]{2,1,0:T(8,128)}, u32[]{:S(2)}) copy-start(f32[32,16,384]{2,1,0:T(8,128)} %param.8) | copy-start | bytes 2359300
  1.1 6.0 %copy-start.1 = (f32[32,16,384]{2,1,0:T(8,128)S(1)}, f32[32,16,384]{2,1,0:T(8,128)}, u32[]{:S(2)}) copy-start(f32[32,16,384]{2,1,0:T(8,128)} %param.9) | copy-start | bytes 2359300
  1.6 11.7 %collective-permute-start.1 = (f32[4,32,384]{2,1,0:T(8,128)S(1)}, f32[4,32,384]{2,1,0:T(8,128)S(1)}, u32[]{:S(2)}, u32[]{:S(2)}) collective-permute-start(f32[4,32,384]{2,1,0:T(8,128)S(1)} %get-tuple-element.30), channel_id=1, source_target_pairs={{0,1},{1,0},{2,3},{3,2},{4,5},{5,4},{6,7},{7,6},{8,9},{9,8},{10,11... | collective-permute-start | bytes 589832 | tf_op jit(solution)/shard_map/ppermute | solution.py:369
  4.1 26.9 %collective-permute-start.7 = (f32[4,32,384]{2,1,0:T(8,128)S(1)}, f32[4,32,384]{2,1,0:T(8,128)S(1)}, u32[]{:S(2)}, u32[]{:S(2)}) collective-permute-start(f32[4,32,384]{2,1,0:T(8,128)S(1)} %get-tuple-element.36), channel_id=1, source_target_pairs={{0,2},{1,3},{2,0},{3,1},{4,6},{5,7},{6,4},{7,5},{8,10},{9,11},{10,... | collective-permute-start | bytes 589832 | tf_op jit(solution)/shard_map/ppermute | solution.py:369
  7.1 23.9 %collective-permute-start.8 = (f32[4,32,384]{2,1,0:T(8,128)S(1)}, f32[4,32,384]{2,1,0:T(8,128)S(1)}, u32[]{:S(2)}, u32[]{:S(2)}) collective-permute-start(f32[4,32,384]{2,1,0:T(8,128)S(1)} %get-tuple-element.37), channel_id=1, source_target_pairs={{0,3},{1,2},{2,1},{3,0},{4,7},{5,6},{6,5},{7,4},{8,11},{9,10},{10,... | collective-permute-start | bytes 589832 | tf_op jit(solution)/shard_map/ppermute | solution.py:369
  7.1 1.1 %copy-start.2 = (f32[32,16,384]{2,1,0:T(8,128)S(1)}, f32[32,16,384]{2,1,0:T(8,128)}, u32[]{:S(2)}) copy-start(f32[32,16,384]{2,1,0:T(8,128)} %param.10) | copy-start | bytes 2359300
  10.0 11.1 %copy-start.3 = (f32[128,128]{1,0:T(8,128)S(1)}, f32[128,128]{1,0:T(8,128)}, u32[]{:S(2)}) copy-start(f32[128,128]{1,0:T(8,128)} %mixing.1) | copy-start | bytes 196612
  10.0 3.2 %collective-permute-start = (f32[208,128]{1,0:T(8,128)S(1)}, f32[208,128]{1,0:T(8,128)S(1)}, u32[]{:S(2)}, u32[]{:S(2)}) collective-permute-start(f32[208,128]{1,0:T(8,128)S(1)} %get-tuple-element.29.a), channel_id=1, source_target_pairs={{0,4},{4,0},{8,12},{12,8},{16,20},{20,16},{24,28},{28,24},{32,36},... | collective-permute-start | bytes 319496 | tf_op jit(solution)/shard_map/ppermute | solution.py:369
  13.2 7.8 %copy-start.4 = (s32[4,384]{1,0:T(4,128)S(1)}, s32[4,384]{1,0:T(4,128)}, u32[]{:S(2)}) copy-start(s32[4,384]{1,0:T(4,128)} %near.1) | copy-start | bytes 18436
  13.2 7.9 %copy-start.5 = (s32[4,384]{1,0:T(4,128)S(1)}, s32[4,384]{1,0:T(4,128)}, u32[]{:S(2)}) copy-start(s32[4,384]{1,0:T(4,128)} %edge_of.1) | copy-start | bytes 18436
  13.2 7.9 %copy-start.6 = (s32[4,384]{1,0:T(4,128)S(1)}, s32[4,384]{1,0:T(4,128)}, u32[]{:S(2)}) copy-start(s32[4,384]{1,0:T(4,128)} %turns.1) | copy-start | bytes 18436
  13.2 7.9 %copy-start.7 = (s32[4,384]{1,0:T(4,128)S(1)}, s32[4,384]{1,0:T(4,128)}, u32[]{:S(2)}) copy-start(s32[4,384]{1,0:T(4,128)} %mask.1) | copy-start | bytes 18436
  13.3 4.8 %collective-permute-start.4 = (f32[152,128]{1,0:T(8,128)S(1)}, f32[152,128]{1,0:T(8,128)S(1)}, u32[]{:S(2)}, u32[]{:S(2)}) collective-permute-start(f32[152,128]{1,0:T(8,128)S(1)} %shard_map.84.a), channel_id=1, source_target_pairs={{0,24},{4,28},{8,16},{12,20},{16,8},{20,12},{24,0},{28,4},{32,56},... | collective-permute-start | bytes 233480 | tf_op jit(solution)/shard_map/ppermute | solution.py:369
  15.2 5.9 %collective-permute-start.3 = (f32[152,128]{1,0:T(8,128)S(1)}, f32[152,128]{1,0:T(8,128)S(1)}, u32[]{:S(2)}, u32[]{:S(2)}) collective-permute-start(f32[152,128]{1,0:T(8,128)S(1)} %shard_map.84.a), channel_id=1, source_target_pairs={{0,16},{4,20},{8,24},{12,28},{16,0},{20,4},{24,8},{28,12},{32,48},... | collective-permute-start | bytes 233480 | tf_op jit(solution)/shard_map/ppermute | solution.py:369
  15.5 5.5 %collective-permute-start.2 = (f32[152,128]{1,0:T(8,128)S(1)}, f32[152,128]{1,0:T(8,128)S(1)}, u32[]{:S(2)}, u32[]{:S(2)}) collective-permute-start(f32[152,128]{1,0:T(8,128)S(1)} %shard_map.84.a), channel_id=1, source_target_pairs={{0,8},{4,12},{8,0},{12,4},{16,24},{20,28},{24,16},{28,20},{32,40},... | collective-permute-start | bytes 233480 | tf_op jit(solution)/shard_map/ppermute | solution.py:369
  18.1 16.7 %collective-permute-start.6 = (f32[64,128]{1,0:T(8,128)S(1)}, f32[64,128]{1,0:T(8,128)S(1)}, u32[]{:S(2)}, u32[]{:S(2)}) collective-permute-start(f32[64,128]{1,0:T(8,128)S(1)} %get-tuple-element.32), channel_id=1, source_target_pairs={{4,8},{12,16},{20,24},{28,32},{36,40},{44,48},{52,56},{60,64},{68,... | collective-permute-start | bytes 98312 | tf_op jit(solution)/shard_map/ppermute | solution.py:389
  21.3 9.9 %collective-permute-start.9 = (s32[1,384]{1,0:T(1,128)S(1)}, s32[1,384]{1,0:T(1,128)S(1)}, u32[]{:S(2)}, u32[]{:S(2)}) collective-permute-start(s32[1,384]{1,0:T(1,128)S(1)} %get-tuple-element.40.wanted), channel_id=1, source_target_pairs={{0,4},{4,0},{8,12},{12,8},{16,20},{20,16},{24,28},{28,24},{32,36},... | collective-permute-start | bytes 4616 | tf_op jit(solution)/shard_map/ppermute | solution.py:369
  22.7 12.1 %collective-permute-start.5 = (f32[224,128]{1,0:T(8,128)S(1)}, f32[224,128]{1,0:T(8,128)S(1)}, u32[]{:S(2)}, u32[]{:S(2)}) collective-permute-start(f32[224,128]{1,0:T(8,128)S(1)} %get-tuple-element.31.mine), channel_id=1, source_target_pairs={{4,132},{12,140},{20,148},{28,156},{36,164},{44,172},{52,180},{60,... | collective-permute-start | bytes 344072 | tf_op jit(solution)/shard_map/ppermute | solution.py:408
  32.1 15.3 %collective-permute-start.10 = (f32[4,32,384]{2,1,0:T(8,128)S(1)}, f32[4,32,384]{2,1,0:T(8,128)S(1)}, u32[]{:S(2)}, u32[]{:S(2)}) collective-permute-start(f32[4,32,384]{2,1,0:T(8,128)S(1)} %get-tuple-element.42), channel_id=1, source_target_pairs={{0,2},{1,3},{2,0},{3,1},{4,6},{5,7},{6,4},{7,5},{8,10},{9,11},{10,... | collective-permute-start | bytes 589832 | tf_op jit(solution)/shard_map/ppermute | solution.py:369
  32.2 15.2 %collective-permute-start.11 = (f32[4,32,384]{2,1,0:T(8,128)S(1)}, f32[4,32,384]{2,1,0:T(8,128)S(1)}, u32[]{:S(2)}, u32[]{:S(2)}) collective-permute-start(f32[4,32,384]{2,1,0:T(8,128)S(1)} %get-tuple-element.43), channel_id=1, source_target_pairs={{0,3},{1,2},{2,1},{3,0},{4,7},{5,6},{6,5},{7,4},{8,11},{9,10},{10,... | collective-permute-start | bytes 589832 | tf_op jit(solution)/shard_map/ppermute | solution.py:369
  33.9 13.5 %collective-permute-start.12 = (f32[4,32,384]{2,1,0:T(8,128)S(1)}, f32[4,32,384]{2,1,0:T(8,128)}, u32[]{:S(2)}, u32[]{:S(2)}) collective-permute-start(f32[4,32,384]{2,1,0:T(8,128)S(1)} %get-tuple-element.44), channel_id=1, source_target_pairs={{0,1},{1,0},{2,3},{3,2},{4,5},{5,4},{6,7},{7,6},{8,9},{9,8},{10,11... | collective-permute-start | bytes 589832 | tf_op jit(solution)/shard_map/ppermute | solution.py:369
  35.5 9.7 %all-to-all-start = ((f32[2,224,128]{2,1,0:T(8,128)}), f32[2,224,128]{2,1,0:T(8,128)S(1)}, u32[]{:S(2)}, u32[]{:S(2)}) async-start(f32[2,224,128]{2,1,0:T(8,128)} %get-tuple-element.46), calls=%async_computation | async-start | bytes 458752 | tf_op jit(solution)/shard_map/all_to_all | solution.py:427
  39.8 6.4 %collective-permute-start.14 = (f32[224,128]{1,0:T(8,128)S(1)}, f32[224,128]{1,0:T(8,128)S(1)}, u32[]{:S(2)}, u32[]{:S(2)}) collective-permute-start(f32[224,128]{1,0:T(8,128)S(1)} %get-tuple-element.45.own), channel_id=1, source_target_pairs={{0,96},{4,100},{8,104},{12,108},{16,112},{20,116},{24,120},{28,124... | collective-permute-start | bytes 344072 | tf_op jit(solution)/shard_map/ppermute | solution.py:369
  42.8 3.6 %collective-permute-start.13 = (f32[224,128]{1,0:T(8,128)S(1)}, f32[224,128]{1,0:T(8,128)S(1)}, u32[]{:S(2)}, u32[]{:S(2)}) collective-permute-start(f32[224,128]{1,0:T(8,128)S(1)} %get-tuple-element.45.own), channel_id=1, source_target_pairs={{0,32},{4,36},{8,40},{12,44},{16,48},{20,52},{24,56},{28,60},{32,0... | collective-permute-start | bytes 344072 | tf_op jit(solution)/shard_map/ppermute | solution.py:369
  47.3 1.5 %collective-permute-start.15 = (f32[128,384]{1,0:T(8,128)S(1)}, f32[128,384]{1,0:T(8,128)S(1)}, u32[]{:S(2)}, u32[]{:S(2)}) collective-permute-start(f32[128,384]{1,0:T(8,128)S(1)} %get-tuple-element.48), channel_id=1, source_target_pairs={{0,4},{4,0},{8,12},{12,8},{16,20},{20,16},{24,28},{28,24},{32,36},... | collective-permute-start | bytes 589832 | tf_op jit(solution)/shard_map/ppermute | solution.py:369
